TPU v7x, 32 devices: a whole 2x2x4 slice. The times are simulated.
32 devices in a mesh: groups: 2 (over y), dp: 8 (over z, x), mp: 2 (over core).
Axes of the slice: x: 2, y: 2, z: 4, core: 2. Of those that a mesh axis runs over, the one named last changes fastest.
Arguments:
- hidden_input: bfloat16 [2048, 8192], P(('groups', 'dp')), parts along dimension 0, may hold values from -6 to 6
- upstream: bfloat16 [2048, 1024], P(('groups', 'dp')), parts along dimension 0, may hold values from -6 to 6
- rollout_row_counts: int32 [2048], P(('groups', 'dp')), parts along dimension 0, may hold values from 0 to 4
- tenant_of_block: int32 [16], P('groups'), parts along dimension 0, may hold values from 0 to 15
- frozen_value_weight: bfloat16 [8192, 1024], P('mp', 'dp'), may hold values from -0.1875 to 0.1875
- common_down_factor: bfloat16 [8192, 64], replicated, may hold values from -0.0625 to 0.0625
- adapter_up_factor: bfloat16 [32, 64, 1024], P(('groups', 'dp')), parts along dimension 0, may hold values from -0.75 to 0.75
Outputs:
- input_gradient: bfloat16 [2048, 8192], P(('groups', 'dp'), 'mp'), parts along dimension 0
- up_factor_gradient: bfloat16 [32, 64, 1024], P(('groups', 'dp')), parts along dimension 0
There are 2 independent parts, one for each index of `groups`. A program takes and returns all parts, laid end to end along the dimension named above; an argument that names none is the same for every part. Nothing has to cross between parts.
All inputs are finite; a program needn't handle non-finite values.
Results may differ from a plain program's by a relative error of at most 0.0054.
Values may be sent and summed in bfloat16 or wider, within the bound.
No kernel may reach another device: no remote copies, remote signals or barrier semaphores. Data moves between devices by JAX's collectives and lax.ppermute only.
A program may use at most 64 MiB of HBM per device.

v0:
```python
import jax
import jax.numpy as jnp
from jax import lax
from jax.sharding import PartitionSpec as P

adapter_scale = 2.0


def local(
    hidden_input,
    upstream,
    rollout_row_counts,
    tenant_of_block,
    frozen_value_weight,
    common_down_factor,
    adapter_up_factor,
):
    dp_count = lax.axis_size("dp")
    mp_count = lax.axis_size("mp")
    model_shard_index = lax.axis_index("mp")
    half_width = frozen_value_weight.shape[0]
    tenant_within_shard = adapter_up_factor.shape[0]
    rank_width = common_down_factor.shape[1]
    shard_rank = rank_width // mp_count
    out_width = upstream.shape[1]
    local_rows = hidden_input.shape[0]
    block_total = tenant_of_block.shape[0]
    rows_per_block = local_rows * dp_count // block_total
    col_width = out_width // dp_count
    weighted = (
        rollout_row_counts[:, None].astype(jnp.float32) * upstream.astype(jnp.float32)
    ).astype(jnp.bfloat16)
    down_part = lax.dynamic_slice_in_dim(
        common_down_factor, model_shard_index * shard_rank, shard_rank, 1
    )
    low_part = jnp.dot(hidden_input, down_part, preferred_element_type=jnp.float32).astype(
        jnp.bfloat16
    )
    up_shard_rank = lax.dynamic_slice_in_dim(
        adapter_up_factor, model_shard_index * shard_rank, shard_rank, 1
    )
    up_flat = up_shard_rank.reshape(tenant_within_shard * shard_rank, out_width)
    grad_cols, up_cols = (
        lax.all_to_all(weighted, "dp", split_axis=1, concat_axis=0, tiled=True),
        lax.all_to_all(up_flat, "dp", split_axis=1, concat_axis=0, tiled=True),
    )
    up_cols = up_cols.reshape(tenant_within_shard * dp_count, shard_rank, col_width)
    grad_blocks = grad_cols.reshape(block_total, rows_per_block, col_width)
    selected = up_cols[tenant_of_block]
    term = jnp.einsum("brc,bkc->brk", grad_blocks, selected, preferred_element_type=jnp.float32)
    back_part = lax.psum_scatter(
        term.reshape(lax.axis_size("dp") * local_rows, shard_rank),
        "dp",
        scatter_dimension=0,
        tiled=True,
    ).astype(jnp.bfloat16)
    all_codes = lax.all_gather(low_part, "dp", axis=0, tiled=True)
    code_blocks = all_codes.reshape(block_total, rows_per_block, shard_rank)
    per_block = jnp.einsum(
        "brk,brc->bkc", code_blocks, grad_blocks, preferred_element_type=jnp.float32
    )
    onehot = (
        tenant_of_block[None, :]
        == jnp.arange(tenant_within_shard * dp_count, dtype=jnp.int32)[:, None]
    ).astype(jnp.float32)
    tenant_part = jnp.einsum("tb,bkc->tkc", onehot, per_block, precision=lax.Precision.HIGHEST)
    per_tenant_sums = lax.all_to_all(
        tenant_part.astype(jnp.bfloat16), "dp", split_axis=0, concat_axis=2, tiled=True
    ).astype(tenant_part.dtype)
    gradient_share = (per_tenant_sums * (adapter_scale / rows_per_block)).astype(jnp.bfloat16)
    backward_rank, up_factor_gradient = (
        lax.all_gather(back_part, "mp", axis=1, tiled=True),
        lax.all_gather(gradient_share, "mp", axis=1, tiled=True),
    )
    whole_weight = lax.all_gather(frozen_value_weight, "dp", axis=1, tiled=True)
    frozen_term = jnp.dot(weighted, whole_weight.T, preferred_element_type=jnp.float32)
    down_factor_half = lax.dynamic_slice_in_dim(
        common_down_factor, model_shard_index * half_width, half_width, 0
    )
    adapter_term = jnp.dot(backward_rank, down_factor_half.T, preferred_element_type=jnp.float32)
    input_gradient = (frozen_term + adapter_scale * adapter_term).astype(jnp.bfloat16)
    return (input_gradient, up_factor_gradient)


def solution(mesh):
    placed = (
        P(("groups", "dp"), None),
        P(("groups", "dp"), None),
        P(("groups", "dp")),
        P("groups"),
        P("mp", "dp"),
        P(),
        P(("groups", "dp"), None, None),
    )
    return jax.shard_map(
        local,
        mesh=mesh,
        in_specs=placed,
        out_specs=(P(("groups", "dp"), "mp"), P(("groups", "dp"), None, None)),
        check_vma=False,
    )
```

profile of v0, /device:TPU:0, one launch (start us, length us, event | category | flops | bytes accessed | tf_op | source)
XLA Modules:
  0.0 238.2 jit_solution(6534930688794445221)
XLA Ops:
  7.2 1.1 constant_dynamic-slice_fusion
  8.3 0.7 copy.23
  9.0 7.3 %all-to-all-start.1 = ((bf16[64,8,128]{2,0,1:T(8,128)(2,1)}), bf16[64,8,128]{2,0,1:T(8,128)(2,1)S(1)}, u32[]{:S(2)}, u32[]{:S(2)}) async-start(bf16[64,8,128]{2,0,1:T(8,128)(2,1)} %copy.23), calls=%async_computation.1 | async-start | bytes 262144 | tf_op jit(solution)/shard_map/all_to_all | solution.py:45
  16.2 1.1 copy.21
  17.3 0.7 convert_element_type.39
  18.0 0.1 multiply_convert_fusion
  18.1 0.8 copy.22
  18.9 4.6 %all-to-all-done.1 = bf16[64,8,128]{2,0,1:T(8,128)(2,1)S(1)} async-done(((bf16[64,8,128]{2,0,1:T(8,128)(2,1)}), bf16[64,8,128]{2,0,1:T(8,128)(2,1)S(1)}, u32[]{:S(2)}, u32[]{:S(2)}) %all-to-all-start.1) | async-done | bytes 131104 | tf_op jit(solution)/shard_map/all_to_all | solution.py:45
  23.6 3.4 %all-to-all-start = ((bf16[128,8,128]{2,0,1:T(8,128)(2,1)}), bf16[128,8,128]{2,0,1:T(8,128)(2,1)S(1)}, u32[]{:S(2)}, u32[]{:S(2)}) async-start(bf16[128,8,128]{2,0,1:T(8,128)(2,1)} %copy.22), calls=%async_computation | async-start | bytes 524288 | tf_op jit(solution)/shard_map/all_to_all | solution.py:44
  27.0 0.0 reduce-scatter.2.cloned.1.call-start
  27.1 0.6 gather_fusion
  27.6 7.5 %all-to-all-done = bf16[128,8,128]{2,0,1:T(8,128)(2,1)S(1)} async-done(((bf16[128,8,128]{2,0,1:T(8,128)(2,1)}), bf16[128,8,128]{2,0,1:T(8,128)(2,1)S(1)}, u32[]{:S(2)}, u32[]{:S(2)}) %all-to-all-start) | async-done | bytes 262176 | tf_op jit(solution)/shard_map/all_to_all | solution.py:44
  35.1 0.3 convolution_bitcast_fusion
  35.4 0.7 copy.42
  36.1 0.0 reduce-scatter.2.cloned.1.call-update
  36.1 0.0 all-gather.2.cloned.1.call-start
  36.1 0.7 all-gather.2.cloned.1.call-update
  36.9 1.8 fusion.2
  38.7 26.0 %all_gather.14 = bf16[1024,32]{0,1:T(8,128)(2,1)S(1)} all-gather(bf16[128,32]{0,1:T(8,128)(2,1)S(1)} %fusion.2), channel_id=1, replica_groups=mesh['groups'=2,'dp'=8,'mp'=2] {'dp'}, dimensions={0}, use_global_device_ids=true | all-gather | bytes 73728 | tf_op jit(solution)/shard_map/all_gather | solution.py:57
  64.7 0.2 fusion.5
  64.9 0.4 convolution_convert_fusion
  65.3 0.7 copy.27
  66.0 3.4 %all-to-all-start.2 = ((bf16[16,32,128]{2,1,0:T(8,128)(2,1)}), bf16[16,32,128]{2,1,0:T(8,128)(2,1)S(1)}, u32[]{:S(2)}, u32[]{:S(2)}) async-start(bf16[16,32,128]{2,1,0:T(8,128)(2,1)} %copy.27), calls=%async_computation.3 | async-start | bytes 262144 | tf_op jit(solution)/shard_map/all_to_all | solution.py:67
  69.4 7.3 %all-to-all-done.2 = bf16[16,32,128]{2,1,0:T(8,128)(2,1)S(1)} async-done(((bf16[16,32,128]{2,1,0:T(8,128)(2,1)}), bf16[16,32,128]{2,1,0:T(8,128)(2,1)S(1)}, u32[]{:S(2)}, u32[]{:S(2)}) %all-to-all-start.2) | async-done | bytes 131104 | tf_op jit(solution)/shard_map/all_to_all | solution.py:67
  76.7 2.0 all_gather.15
  78.7 17.6 %reduce-scatter.2.cloned.1.call-done = f32[128,32]{0,1:T(8,128)} async-done(((f32[1024,32]{0,1:T(8,128)}), f32[128,32]{0,1:T(8,128)}) %reduce-scatter.2.cloned.1.call-update) | async-done | bytes 16400 | tf_op jit(solution)/shard_map/reduce_scatter | solution.py:51
  96.3 0.7 convert_element_type.42
  97.0 1.8 all_gather.13
  98.8 124.0 %all-gather.2.cloned.1.call-done = bf16[4096,1024]{1,0:T(8,128)(2,1)} async-done(((bf16[4096,128]{1,0:T(8,128)(2,1)}), bf16[4096,1024]{1,0:T(8,128)(2,1)}) %all-gather.2.cloned.1.call-update) | async-done | bytes 8388624 | tf_op jit(solution)/shard_map/all_gather | solution.py:75
  222.8 6.4 %fusion.16 = f32[128,4096]{1,0:T(8,128)S(1)} fusion(bf16[128,1024]{0,1:T(8,128)(2,1)S(1)} %multiply_convert_fusion, bf16[4096,1024]{1,0:T(8,128)(2,1)} %all-gather.2.cloned.1.call-done), kind=kOutput, calls=%fused_computation.28 | convolution fusion | flops 1073741824 | bytes 10747904 | tf_op jit(solution)/shard_map/dot_general | solution.py:76
  229.2 1.4 fusion.1
  230.6 0.7 copy.44
  (11 shorter events, 0.1 us)
Async XLA Ops:
  7.2 29.7 %copy-start = (bf16[128,8192]{1,0:T(8,128)(2,1)S(1)}, bf16[128,8192]{1,0:T(8,128)(2,1)}, u32[]{:S(2)}) copy-start(bf16[128,8192]{1,0:T(8,128)(2,1)} %param.7) | copy-start | bytes 6291460
  7.2 19.9 %copy-start.2 = (s32[8]{0:T(128)S(1)}, s32[8]{0:T(128)}, u32[]{:S(2)}) copy-start(s32[8]{0:T(128)} %param.10) | copy-start | bytes 100
  9.0 14.6 %all-to-all-start.1 = ((bf16[64,8,128]{2,0,1:T(8,128)(2,1)}), bf16[64,8,128]{2,0,1:T(8,128)(2,1)S(1)}, u32[]{:S(2)}, u32[]{:S(2)}) async-start(bf16[64,8,128]{2,0,1:T(8,128)(2,1)} %copy.23), calls=%async_computation.1 | async-start | bytes 262144 | tf_op jit(solution)/shard_map/all_to_all | solution.py:45
  23.6 11.6 %all-to-all-start = ((bf16[128,8,128]{2,0,1:T(8,128)(2,1)}), bf16[128,8,128]{2,0,1:T(8,128)(2,1)S(1)}, u32[]{:S(2)}, u32[]{:S(2)}) async-start(bf16[128,8,128]{2,0,1:T(8,128)(2,1)} %copy.22), calls=%async_computation | async-start | bytes 524288 | tf_op jit(solution)/shard_map/all_to_all | solution.py:44
  27.0 69.3 %reduce-scatter.2.cloned.1.call-start = ((), (), s32[]{:S(2)}) async-start(), calls=%async_computation.5 | async-start | bytes 147456 | tf_op jit(solution)/shard_map/reduce_scatter | solution.py:51
  36.1 186.7 %all-gather.2.cloned.1.call-start = ((), (), s32[]{:S(2)}) async-start(), calls=%async_computation.4 | async-start | bytes 9437184 | tf_op jit(solution)/shard_map/all_gather | solution.py:75
  66.0 10.7 %all-to-all-start.2 = ((bf16[16,32,128]{2,1,0:T(8,128)(2,1)}), bf16[16,32,128]{2,1,0:T(8,128)(2,1)S(1)}, u32[]{:S(2)}, u32[]{:S(2)}) async-start(bf16[16,32,128]{2,1,0:T(8,128)(2,1)} %copy.27), calls=%async_computation.3 | async-start | bytes 262144 | tf_op jit(solution)/shard_map/all_to_all | solution.py:67
  222.8 6.4 %copy-start.1 = (bf16[8192,64]{0,1:T(8,128)(2,1)S(1)}, bf16[8192,64]{0,1:T(8,128)(2,1)}, u32[]{:S(2)}) copy-start(bf16[8192,64]{0,1:T(8,128)(2,1)} %param.12) | copy-start | bytes 3145732
Sparse Core Ops, SparseCore 0:
  36.2 60.0 reduce-scatter.1
  98.3 124.4 all-gather.1
where the time goes:
time: 239 us; the launch traced here: 238 us
  waiting for transfers between devices  162 us (68%)
  blocking collectives  29.8 us (12%)
  between operations  14.2 us (6%)
  starting transfers between devices  14.1 us (6%)
  matrix products  10.5 us (4%)
  local copies, waits for them, and re-layouts  6.39 us (3%)
    all_gather x1, waiting for transfers between devices, local(): whole_weight = lax.all_gather(frozen_value_weight, 'dp', axis=1, tiled=True)  124 us
    all_gather x1, blocking collectives, local(): all_codes = lax.all_gather(low_part, 'dp', axis=0, tiled=True)  26 us
    reduce_scatter x1, waiting for transfers between devices, local(): lax.psum_scatter(term.reshape(lax.axis_size('dp') * local_rows, shard_ran...  17.6 us
    all_to_all x1, waiting for transfers between devices, local(): lax.all_to_all(weighted, 'dp', split_axis=1, concat_axis=0, tiled=True)  7.51 us
    all_to_all x1, waiting for transfers between devices, local(): lax.all_to_all(tenant_part.astype(jnp.bfloat16), 'dp', split_axis=0, conc...  7.28 us
    all_to_all x1, starting transfers between devices, local(): lax.all_to_all(up_flat, 'dp', split_axis=1, concat_axis=0, tiled=True)  7.25 us
    dot_general x1, matrix products, local(): jnp.dot(weighted, whole_weight.T, preferred_element_type=jnp.float32)  6.39 us
  transfers between devices with their start and end apart: 5, of which 5 were waited for; matrix products, arithmetic and copies ran while one was open for 3% of the time, Pallas kernels for 0%

commit v1 on v0

v1 whole, which is shorter than its diff:
```python
import math

import jax
import jax.numpy as jnp
from jax import lax
from jax.sharding import PartitionSpec as P

adapter_scale = 2.0
ALL = ("groups", "dp", "mp")


def local(
    hidden_input,
    upstream,
    rollout_row_counts,
    tenant_of_block,
    frozen_value_weight,
    common_down_factor,
    adapter_up_factor,
):
    f32, bf16 = jnp.float32, jnp.bfloat16
    group_count = lax.axis_size("groups")
    dp_count = lax.axis_size("dp")
    mp_count = lax.axis_size("mp")
    g = lax.axis_index("groups")
    m = lax.axis_index("mp")
    half_width, cols = frozen_value_weight.shape
    tenants_here, rank, out_width = adapter_up_factor.shape
    part_rank = rank // mp_count
    rows = hidden_input.shape[0]
    blocks = tenant_of_block.shape[0]
    block_rows = rows * dp_count // blocks
    tenants = tenants_here * dp_count

    near = math.gcd(4, dp_count)
    team = group_count * near
    features = half_width // team
    teams = [
        [(gi * dp_count + base + k) * mp_count + mi for gi in range(group_count) for k in range(near)]
        for base in range(0, dp_count, near)
        for mi in range(mp_count)
    ]

    weighted = (rollout_row_counts[:, None].astype(f32) * upstream.astype(f32)).astype(bf16)

    group_weight = lax.dynamic_slice_in_dim(frozen_value_weight, g * near * features, near * features, 0)
    to_send = jnp.broadcast_to(
        group_weight.reshape(1, near, features, cols), (dp_count // near, near, features, cols)
    ).reshape(dp_count, features, cols)
    weight_slices = lax.all_to_all(to_send, "dp", split_axis=0, concat_axis=0, tiled=True)

    part_cols = out_width // mp_count
    my_cols = lax.dynamic_slice_in_dim(weighted, m * part_cols, part_cols, 1)
    row_parts = lax.all_to_all(
        jnp.broadcast_to(my_cols[None], (team, rows, part_cols)),
        ALL, split_axis=0, concat_axis=0, tiled=True, axis_index_groups=teams,
    )
    other_parts = lax.ppermute(row_parts, "mp", [(k, (k + 1) % mp_count) for k in range(mp_count)])

    down_part = lax.dynamic_slice_in_dim(common_down_factor, m * part_rank, part_rank, 1)
    low = lax.dot_general(
        down_part, hidden_input, (((0,), (1,)), ((), ())), preferred_element_type=f32
    ).astype(bf16)
    up_part = lax.dynamic_slice_in_dim(adapter_up_factor, m * part_rank, part_rank, 1)
    weighted_send = weighted.reshape(rows, dp_count, cols).transpose(1, 0, 2)
    up_send = up_part.reshape(tenants_here * part_rank, dp_count, cols).transpose(1, 0, 2)
    low_send = jnp.broadcast_to(low.reshape(1, -1, cols), (dp_count, part_rank * rows // cols, cols))
    first = lax.all_to_all(
        jnp.concatenate([weighted_send, up_send, low_send], axis=1),
        "dp", split_axis=0, concat_axis=0, tiled=True,
    )
    at_up, at_low = rows, rows + tenants_here * part_rank
    grad_blocks = first[:, :at_up].reshape(blocks, block_rows, cols)
    up_cols = first[:, at_up:at_low].reshape(tenants, part_rank, cols)
    low_blocks = (
        first[:, at_low:].reshape(dp_count, part_rank, blocks // dp_count, block_rows)
        .transpose(0, 2, 1, 3).reshape(blocks, part_rank, block_rows)
    )
    selected = up_cols[tenant_of_block]
    term = jnp.einsum("bkc,brc->bkr", selected, grad_blocks, preferred_element_type=f32)
    per_block = jnp.einsum("bkr,brc->bkc", low_blocks, grad_blocks, preferred_element_type=f32)
    onehot = (tenant_of_block[None, :] == jnp.arange(tenants, dtype=jnp.int32)[:, None]).astype(f32)
    tenant_sums = jnp.einsum("tb,bkc->tkc", onehot, per_block, precision=lax.Precision.HIGHEST)
    finished = (tenant_sums * (adapter_scale / block_rows)).astype(bf16)
    term_send = (
        term.astype(bf16).reshape(dp_count, blocks // dp_count, part_rank, block_rows)
        .transpose(0, 2, 1, 3).reshape(dp_count, part_rank * rows // cols, cols)
    )
    second = lax.all_to_all(
        jnp.concatenate([term_send, finished.reshape(dp_count, tenants_here * part_rank, cols)], axis=1),
        "dp", split_axis=0, concat_axis=0, tiled=True,
    )
    at_grad = term_send.shape[1]
    back_part = jnp.sum(second[:, :at_grad].astype(f32), axis=0).astype(bf16).reshape(part_rank, rows)
    grad_part = (
        second[:, at_grad:].reshape(dp_count, tenants_here, part_rank, cols)
        .transpose(1, 2, 0, 3).reshape(tenants_here, part_rank, out_width)
    )
    back_rank = lax.all_gather(back_part, "mp", axis=0, tiled=True)
    up_factor_gradient = lax.all_gather(grad_part, "mp", axis=1, tiled=True)

    def partial_term(parts, which):
        slices = lax.dynamic_slice_in_dim(weight_slices, which * (dp_count // mp_count), dp_count // mp_count, 0)
        return lax.dot_general(
            parts.reshape(team * rows, part_cols),
            slices.transpose(1, 0, 2).reshape(features, part_cols),
            (((1,), (1,)), ((), ())),
            preferred_element_type=f32,
        )

    frozen = (partial_term(row_parts, m) + partial_term(other_parts, (m + mp_count - 1) % mp_count)).astype(bf16)
    frozen_mine = lax.all_to_all(
        frozen.reshape(team, rows, features),
        ALL, split_axis=0, concat_axis=0, tiled=True, axis_index_groups=teams,
    )
    frozen_term = frozen_mine.transpose(1, 0, 2).reshape(rows, half_width)
    down_half = lax.dynamic_slice_in_dim(common_down_factor, m * half_width, half_width, 0)
    adapter_term = lax.dot_general(
        back_rank, down_half, (((0,), (1,)), ((), ())), preferred_element_type=f32
    )
    input_gradient = (frozen_term.astype(f32) + adapter_scale * adapter_term).astype(bf16)
    return (input_gradient, up_factor_gradient)


def solution(mesh):
    placed = (
        P(("groups", "dp"), None),
        P(("groups", "dp"), None),
        P(("groups", "dp")),
        P("groups"),
        P("mp", "dp"),
        P(),
        P(("groups", "dp"), None, None),
    )
    return jax.shard_map(
        local,
        mesh=mesh,
        in_specs=placed,
        out_specs=(P(("groups", "dp"), "mp"), P(("groups", "dp"), None, None)),
        check_vma=False,
    )
```

time: 239 us -> 113 us (0.47)
  waiting for transfers between devices: 162 us -> 58.1 us
  blocking collectives: 29.8 us -> 3.81 us
  between operations: 14.2 us -> 0.85 us
  starting transfers between devices: 14.1 us -> 22.3 us
  local copies, waits for them, and re-layouts: 6.39 us -> 13.5 us
    all_gather x1 -> x0, waiting for transfers between devices: 124 us -> none  [local(): whole_weight = lax.all_gather(frozen_value_weight, 'dp', axis=1, tiled=True)]
    all_to_all x3 -> x5, waiting for transfers between devices: 19.4 us -> 58.1 us  [the longest x1 20.8 us: local(): lax.all_to_all(to_send, 'dp', split_axis=0, concat_axis=0, tiled=True)]
    all_gather x3 -> x2, blocking collectives: 29.8 us -> 3.81 us  [the longest x1 1.99 us: local(): up_factor_gradient = lax.all_gather(grad_part, 'mp', axis=1, tiled=True)]
    reduce_scatter x1 -> x0, waiting for transfers between devices: 17.6 us -> none  [local(): lax.psum_scatter(term.reshape(lax.axis_size('dp') * local_rows, shard_ran...]
    all_to_all x3 -> x5, starting transfers between devices: 14 us -> 22.3 us  [the longest x1 7.25 us: local(): lax.all_to_all(jnp.concatenate([weighted_send, up_send, low_send], axis=1...]
    broadcast_in_dim x0 -> x4, local copies, waits for them, and re-layouts: none -> 5.29 us  [the longest x2 4.15 us: local(): jnp.broadcast_to(group_weight.reshape(1, near, features, cols), (dp_count...]
    dynamic_slice x1 -> x5, local copies, waits for them, and re-layouts: 1.07 us -> 4.17 us  [the longest x1 1.87 us: local(): lax.dynamic_slice_in_dim(frozen_value_weight, g * near * features, near *...]
    dot_general x5 -> x6, matrix products: 10.1 us -> 9.24 us  [the longest x2 3.6 us: partial_term(): lax.dot_general(parts.reshape(team * rows, part_cols), slices.transpose(1...]
  transfers between devices with their start and end apart: 5 -> 6, of which waited for: 5 -> 5; matrix products, arithmetic and copies ran while one was open for 3% -> 12% of each run, Pallas kernels for 0% -> 0%
where the time goes in v1:
time: 113 us; the launch traced here: 112 us
  waiting for transfers between devices  58.1 us (51%)
  starting transfers between devices  22.3 us (20%)
  local copies, waits for them, and re-layouts  13.5 us (12%)
  matrix products  9.62 us (9%)
  blocking collectives  3.81 us (3%)
  other arithmetic  3.37 us (3%)
    all_to_all x1, waiting for transfers between devices, local(): lax.all_to_all(to_send, 'dp', split_axis=0, concat_axis=0, tiled=True)  20.8 us
    all_to_all x1, waiting for transfers between devices, local(): lax.all_to_all(jnp.concatenate([weighted_send, up_send, low_send], axis=1...  12.9 us
    all_to_all x1, waiting for transfers between devices, local(): lax.all_to_all(jnp.broadcast_to(my_cols[None], (team, rows, part_cols)),...  11.2 us
    all_to_all x1, waiting for transfers between devices, local(): lax.all_to_all(frozen.reshape(team, rows, features), ALL, split_axis=0, c...  9.91 us
    all_to_all x1, starting transfers between devices, local(): lax.all_to_all(jnp.concatenate([weighted_send, up_send, low_send], axis=1...  7.25 us
    all_to_all x1, starting transfers between devices, local(): lax.all_to_all(to_send, 'dp', split_axis=0, concat_axis=0, tiled=True)  4.34 us
    broadcast_in_dim x2, local copies, waits for them, and re-layouts, local(): jnp.broadcast_to(group_weight.reshape(1, near, features, cols), (dp_count...  4.15 us
    all_to_all x1, starting transfers between devices, local(): lax.all_to_all(jnp.broadcast_to(my_cols[None], (team, rows, part_cols)),...  3.7 us
  transfers between devices with their start and end apart: 6, of which 5 were waited for; matrix products, arithmetic and copies ran while one was open for 12% of the time, Pallas kernels for 0%

profile of v1, /device:TPU:0, one launch (start us, length us, event | category | flops | bytes accessed | tf_op | source)
XLA Modules:
  0.0 111.6 jit_solution(366417408343914212)
XLA Ops:
  0.6 1.3 %copy.18 = bf16[128,1024]{0,1:T(8,128)(2,1)S(1)} copy(bf16[128,1024]{1,0:T(8,128)(2,1)} %param.8) | data formatting | bytes 524288 | tf_op args[1]
  1.9 0.7 convert_element_type.37
  2.6 0.9 constant_dynamic-slice_fusion
  3.8 1.8 %convolution_convert_fusion.1 = bf16[32,128]{1,0:T(8,128)(2,1)S(1)} fusion(bf16[128,8192]{1,0:T(8,128)(2,1)S(1)} %copy-done, bf16[8192,64]{0,1:T(8,128)(2,1)} %param.12, s32[]{:T(128)S(6)} %select_n.34), kind=kOutput, calls=%fused_computation.9 | convolution fusion | flops 67112960 | bytes 2629636 | tf_op jit(solution)/shard_map/dot_general | solution.py:61
  5.7 0.8 pad_maximum_fusion
  6.5 7.3 %all-to-all-start.3 = ((bf16[8,224,128]{2,1,0:T(8,128)(2,1)}), bf16[8,224,128]{2,1,0:T(8,128)(2,1)S(1)}, u32[]{:S(2)}, u32[]{:S(2)}) async-start(bf16[8,224,128]{2,1,0:T(8,128)(2,1)} %pad_maximum_fusion), calls=%async_computation.3 | async-start | bytes 917504 | tf_op jit(solution)/shard_map/all_to_all | solution.py:68
  13.9 12.9 %all-to-all-done.3 = bf16[8,224,128]{2,1,0:T(8,128)(2,1)S(1)} async-done(((bf16[8,224,128]{2,1,0:T(8,128)(2,1)}), bf16[8,224,128]{2,1,0:T(8,128)(2,1)S(1)}, u32[]{:S(2)}, u32[]{:S(2)}) %all-to-all-start.3) | async-done | bytes 458784 | tf_op jit(solution)/shard_map/all_to_all | solution.py:68
  26.8 1.1 %broadcast_in_dim.10 = bf16[8,128,512]{2,1,0:T(8,128)(2,1)} broadcast(bf16[128,512]{1,0:T(8,128)(2,1)S(1)} %copy.19), dimensions={1,2} | broadcast | bytes 1179648 | tf_op jit(solution)/shard_map/broadcast_in_dim | solution.py:55
  28.0 3.7 %all-to-all-start = ((bf16[8,128,512]{2,1,0:T(8,128)(2,1)}), bf16[8,128,512]{2,1,0:T(8,128)(2,1)S(1)}, u32[]{:S(2)}, u32[]{:S(2)}) async-start(bf16[8,128,512]{2,1,0:T(8,128)(2,1)} %broadcast_in_dim.10), calls=%async_computation | async-start | bytes 2097152 | tf_op jit(solution)/shard_map/all_to_all | solution.py:54
  31.6 1.9 %constant_dynamic-slice_fusion.3 = bf16[2048,128]{1,0:T(8,128)(2,1)} fusion(bf16[4096,128]{1,0:T(8,128)(2,1)} %param.11, s32[]{:T(128)S(6)} %select_n.30), kind=kLoop, calls=%fused_computation.33 | loop fusion | bytes 1048580 | tf_op jit(solution)/shard_map/dynamic_slice | solution.py:46
  33.5 2.0 %copy.20 = bf16[4,512,128]{1,2,0:T(8,128)(2,1)} copy(bf16[4,512,128]{2,1,0:T(8,128)(2,1)} %bitcast.49) | data formatting | bytes 1048576 | tf_op jit(solution)/shard_map/broadcast_in_dim | solution.py:47
  35.6 11.2 %all-to-all-done = bf16[8,128,512]{2,1,0:T(8,128)(2,1)S(1)} async-done(((bf16[8,128,512]{2,1,0:T(8,128)(2,1)}), bf16[8,128,512]{2,1,0:T(8,128)(2,1)S(1)}, u32[]{:S(2)}, u32[]{:S(2)}) %all-to-all-start) | async-done | bytes 1048608 | tf_op jit(solution)/shard_map/all_to_all | solution.py:54
  46.8 2.1 %broadcast_in_dim.12 = bf16[2,4,512,128]{2,3,1,0:T(8,128)(2,1)} broadcast(bf16[4,512,128]{1,2,0:T(8,128)(2,1)} %copy.20), dimensions={1,2,3} | broadcast | bytes 1572864 | tf_op jit(solution)/shard_map/broadcast_in_dim | solution.py:47
  48.9 4.3 %all-to-all-start.1 = ((bf16[8,512,128]{1,2,0:T(8,128)(2,1)}), bf16[8,512,128]{1,2,0:T(8,128)(2,1)}, u32[]{:S(2)}, u32[]{:S(2)}) async-start(bf16[8,512,128]{1,2,0:T(8,128)(2,1)} %bitcast.44), calls=%async_computation.1 | async-start | bytes 2097152 | tf_op jit(solution)/shard_map/all_to_all | solution.py:50
  53.4 1.2 %fusion.5 = f32[8,32,128]{2,1,0:T(8,128)S(1)} fusion(bf16[8,224,128]{2,1,0:T(8,128)(2,1)} %copy-done.1), kind=kOutput, calls=%fused_computation.14 | convolution fusion | flops 8388608 | bytes 458752 | tf_op jit(solution)/shard_map/bkr,brc->bkc/dot_general | solution.py:81
  55.0 0.6 gather_fusion
  55.5 1.2 %convolution_convert_fusion = bf16[8,32,128]{2,1,0:T(8,128)(2,1)S(1)} fusion(bf16[8,32,128]{2,1,0:T(8,128)(2,1)S(1)} %gather_fusion, bf16[8,224,128]{2,1,0:T(8,128)(2,1)} %copy-done.1), kind=kOutput, calls=%fused_computation.8 | convolution fusion | flops 8421376 | bytes 393216 | tf_op jit(solution)/shard_map/bkc,brc->bkr/dot_general | solution.py:80
  56.7 0.7 pad_maximum_fusion.1
  57.4 20.8 %all-to-all-done.1 = bf16[8,512,128]{1,2,0:T(8,128)(2,1)} async-done(((bf16[8,512,128]{1,2,0:T(8,128)(2,1)}), bf16[8,512,128]{1,2,0:T(8,128)(2,1)}, u32[]{:S(2)}, u32[]{:S(2)}) %all-to-all-start.1) | async-done | bytes 1048608 | tf_op jit(solution)/shard_map/all_to_all | solution.py:50
  78.2 3.4 %all-to-all-start.4 = ((bf16[8,96,128]{2,1,0:T(8,128)(2,1)}), bf16[8,96,128]{2,1,0:T(8,128)(2,1)S(1)}, u32[]{:S(2)}, u32[]{:S(2)}) async-start(bf16[8,96,128]{2,1,0:T(8,128)(2,1)} %pad_maximum_fusion.1), calls=%async_computation.4 | async-start | bytes 393216 | tf_op jit(solution)/shard_map/all_to_all | solution.py:89
  81.7 1.3 %constant_dynamic-slice_fusion.1 = (bf16[4,512,128]{1,2,0:T(8,128)(2,1)S(1)}, bf16[4,512,128]{1,2,0:T(8,128)(2,1)S(1)}) fusion(bf16[8,512,128]{1,2,0:T(8,128)(2,1)} %all-to-all-done.1, s32[]{:T(128)S(6)} %select_n.33, s32[]{:T(128)S(6)} %select_n.31), kind=kLoop, calls=%fused_computation.31 | loop fusion | bytes 2097160 | tf_op jit(solution)/shard_map/dynamic_slice | solution.py:103
  82.9 0.7 fusion.15
  83.6 2.9 %add_convert_fusion = bf16[1024,512]{1,0:T(8,128)(2,1)} fusion(f32[1024,512]{1,0:T(8,128)S(1)} %fusion.15, bf16[1024,512]{1,0:T(8,128)(2,1)} %bitcast.5, bf16[512,512]{0,1:T(8,128)(2,1)S(1)} %bitcast.47), kind=kOutput, calls=%fused_computation.5 | convolution fusion | flops 537919488 | bytes 4718592 | tf_op jit(solution)/shard_map/dot_general | solution.py:104
  86.5 3.2 %all-to-all-done.4 = bf16[8,96,128]{2,1,0:T(8,128)(2,1)S(1)} async-done(((bf16[8,96,128]{2,1,0:T(8,128)(2,1)}), bf16[8,96,128]{2,1,0:T(8,128)(2,1)S(1)}, u32[]{:S(2)}, u32[]{:S(2)}) %all-to-all-start.4) | async-done | bytes 196640 | tf_op jit(solution)/shard_map/all_to_all | solution.py:89
  89.8 3.6 %all-to-all-start.2 = ((bf16[8,128,512]{2,1,0:T(8,128)(2,1)}), bf16[8,128,512]{2,1,0:T(8,128)(2,1)S(1)}, u32[]{:S(2)}, u32[]{:S(2)}) async-start(bf16[8,128,512]{2,1,0:T(8,128)(2,1)} %bitcast.45), calls=%async_computation.2 | async-start | bytes 2097152 | tf_op jit(solution)/shard_map/all_to_all | solution.py:112
  93.4 2.0 %all_gather.7 = bf16[2,64,1024]{2,1,0:T(8,128)(2,1)S(1)} all-gather(bf16[2,32,1024]{2,1,0:T(8,128)(2,1)S(1)} %bitcast.54), channel_id=1, replica_groups=mesh['groups'=2,'dp'=8,'mp'=2] {'mp'}, dimensions={1}, use_global_device_ids=true | all-gather | bytes 393216 | tf_op jit(solution)/shard_map/all_gather | solution.py:100
  95.4 0.9 slice_reduce_fusion
  96.3 1.8 %all_gather.6 = bf16[64,128]{1,0:T(8,128)(2,1)S(1)} all-gather(bf16[32,128]{1,0:T(8,128)(2,1)S(1)} %slice_reduce_fusion), channel_id=1, replica_groups=mesh['groups'=2,'dp'=8,'mp'=2] {'mp'}, dimensions={0}, use_global_device_ids=true | all-gather | bytes 24576 | tf_op jit(solution)/shard_map/all_gather | solution.py:99
  98.1 9.9 %all-to-all-done.2 = bf16[8,128,512]{2,1,0:T(8,128)(2,1)S(1)} async-done(((bf16[8,128,512]{2,1,0:T(8,128)(2,1)}), bf16[8,128,512]{2,1,0:T(8,128)(2,1)S(1)}, u32[]{:S(2)}, u32[]{:S(2)}) %all-to-all-start.2) | async-done | bytes 1048608 | tf_op jit(solution)/shard_map/all_to_all | solution.py:112
  108.5 1.0 copy-done.2
  109.5 1.4 %fusion.1 = bf16[128,4096]{1,0:T(8,128)(2,1)} fusion(f32[128,4096]{1,0:T(8,128)S(1)} %bitcast.42, bf16[64,128]{1,0:T(8,128)(2,1)S(1)} %all_gather.6, bf16[8192,64]{0,1:T(8,128)(2,1)S(1)} %copy-done.2, s32[]{:T(128)S(6)} %select_n.36), kind=kOutput, calls=%fused_computation.3 | convolution fusion | flops 68681728 | bytes 3686404 | tf_op jit(solution)/shard_map/dot_general | solution.py:118
  110.9 0.7 copy.37
  (28 shorter events, 1.5 us)
Async XLA Ops:
  0.6 3.2 %copy-start = (bf16[128,8192]{1,0:T(8,128)(2,1)S(1)}, bf16[128,8192]{1,0:T(8,128)(2,1)}, u32[]{:S(2)}) copy-start(bf16[128,8192]{1,0:T(8,128)(2,1)} %param.7) | copy-start | bytes 6291460
  6.5 20.3 %all-to-all-start.3 = ((bf16[8,224,128]{2,1,0:T(8,128)(2,1)}), bf16[8,224,128]{2,1,0:T(8,128)(2,1)S(1)}, u32[]{:S(2)}, u32[]{:S(2)}) async-start(bf16[8,224,128]{2,1,0:T(8,128)(2,1)} %pad_maximum_fusion), calls=%async_computation.3 | async-start | bytes 917504 | tf_op jit(solution)/shard_map/all_to_all | solution.py:68
  26.8 1.1 %copy-start.1 = (bf16[8,224,128]{2,1,0:T(8,128)(2,1)}, bf16[8,224,128]{2,1,0:T(8,128)(2,1)S(1)}, u32[]{:S(2)}) copy-start(bf16[8,224,128]{2,1,0:T(8,128)(2,1)S(1)} %all-to-all-done.3) | copy-start | bytes 1376260
  28.0 18.9 %all-to-all-start = ((bf16[8,128,512]{2,1,0:T(8,128)(2,1)}), bf16[8,128,512]{2,1,0:T(8,128)(2,1)S(1)}, u32[]{:S(2)}, u32[]{:S(2)}) async-start(bf16[8,128,512]{2,1,0:T(8,128)(2,1)} %broadcast_in_dim.10), calls=%async_computation | async-start | bytes 2097152 | tf_op jit(solution)/shard_map/all_to_all | solution.py:54
  35.6 17.7 %copy-start.4 = (s32[8]{0:T(128)S(1)}, s32[8]{0:T(128)}, u32[]{:S(2)}) copy-start(s32[8]{0:T(128)} %param.10) | copy-start | bytes 100
  35.6 19.4 %slice-start = ((bf16[8,224,128]{2,1,0:T(8,128)(2,1)}), bf16[8,64,128]{2,1,0:T(8,128)(2,1)S(1)}, s32[]{:S(2)}) async-start(bf16[8,224,128]{2,1,0:T(8,128)(2,1)} %copy-done.1), calls=%async_computation.5 | async-start | bytes 262144 | tf_op jit(solution)/shard_map/slice | solution.py:74
  48.9 29.3 %all-to-all-start.1 = ((bf16[8,512,128]{1,2,0:T(8,128)(2,1)}), bf16[8,512,128]{1,2,0:T(8,128)(2,1)}, u32[]{:S(2)}, u32[]{:S(2)}) async-start(bf16[8,512,128]{1,2,0:T(8,128)(2,1)} %bitcast.44), calls=%async_computation.1 | async-start | bytes 2097152 | tf_op jit(solution)/shard_map/all_to_all | solution.py:50
  53.3 30.3 %collective-permute-start = (bf16[8,128,512]{2,1,0:T(8,128)(2,1)S(1)}, bf16[8,128,512]{2,1,0:T(8,128)(2,1)}, u32[]{:S(2)}, u32[]{:S(2)}) collective-permute-start(bf16[8,128,512]{2,1,0:T(8,128)(2,1)S(1)} %all-to-all-done), channel_id=1, source_target_pairs={{0,1},{1,0},{2,3},{3,2},{4,5},{5,4},{6,7},{7,6},{8,9},{9,8},{10,11... | collective-permute-start | bytes 3145736 | tf_op jit(solution)/shard_map/ppermute | solution.py:58
  78.2 11.6 %all-to-all-start.4 = ((bf16[8,96,128]{2,1,0:T(8,128)(2,1)}), bf16[8,96,128]{2,1,0:T(8,128)(2,1)S(1)}, u32[]{:S(2)}, u32[]{:S(2)}) async-start(bf16[8,96,128]{2,1,0:T(8,128)(2,1)} %pad_maximum_fusion.1), calls=%async_computation.4 | async-start | bytes 393216 | tf_op jit(solution)/shard_map/all_to_all | solution.py:89
  89.8 3.6 %copy-start.3 = (bf16[8,96,128]{2,1,0:T(8,128)(2,1)}, bf16[8,96,128]{2,1,0:T(8,128)(2,1)S(1)}, u32[]{:S(2)}) copy-start(bf16[8,96,128]{2,1,0:T(8,128)(2,1)S(1)} %all-to-all-done.4) | copy-start | bytes 589828
  89.8 18.2 %all-to-all-start.2 = ((bf16[8,128,512]{2,1,0:T(8,128)(2,1)}), bf16[8,128,512]{2,1,0:T(8,128)(2,1)S(1)}, u32[]{:S(2)}, u32[]{:S(2)}) async-start(bf16[8,128,512]{2,1,0:T(8,128)(2,1)} %bitcast.45), calls=%async_computation.2 | async-start | bytes 2097152 | tf_op jit(solution)/shard_map/all_to_all | solution.py:112
  108.3 1.2 %copy-start.2 = (bf16[8192,64]{0,1:T(8,128)(2,1)S(1)}, bf16[8192,64]{0,1:T(8,128)(2,1)}, u32[]{:S(2)}) copy-start(bf16[8192,64]{0,1:T(8,128)(2,1)} %param.12) | copy-start | bytes 3145732

commit v2 on v1

v2 whole, which is shorter than its diff:
```python
import functools
import math

import jax
import jax.numpy as jnp
from jax import lax
from jax.experimental import pallas as pl
from jax.experimental.pallas import tpu as pltpu
from jax.sharding import PartitionSpec as P

adapter_scale = 2.0
ALL = ("groups", "dp", "mp")
f32, bf16 = jnp.float32, jnp.bfloat16
VMEM = pl.BlockSpec(memory_space=pltpu.VMEM)
SMEM = pl.BlockSpec(memory_space=pltpu.SMEM)
HBM = pl.BlockSpec(memory_space=pltpu.HBM)
PARAMS = pltpu.CompilerParams(vmem_limit_bytes=16 * 1024 * 1024)


def place():
    return lax.axis_index("groups"), lax.axis_index("dp"), lax.axis_index("mp")


def piece(index, size):
    return pl.ds(pl.multiple_of(index * size, size), size)


def prepare_kernel(
    leaving, weight, upstream, counts, tenants, up, to_send, weighted, my_cols, picked,
    held_weight, held_upstream, held_counts, held_tenants, held_up, in_sem, out_sem, other_sem,
):
    g, _, m = place()
    copies, depth = to_send.shape[0], to_send.shape[1]
    chunks = in_sem.shape[0]
    size = depth // chunks
    others = [
        pltpu.make_async_copy(source, target, other_sem.at[i])
        for i, (source, target) in enumerate(
            [(counts, held_counts), (upstream, held_upstream), (tenants, held_tenants), (up, held_up)]
        )
    ]
    for load in others:
        load.start()
    loads, stores = [], []
    for c in range(chunks):
        at = pl.ds(pl.multiple_of(g * depth + c * size, size), size)
        loads.append(pltpu.make_async_copy(weight.at[at], held_weight.at[pl.ds(c * size, size)], in_sem.at[c]))
        loads[-1].start()
    rows, part = my_cols.shape
    diagonal = lax.broadcasted_iota(jnp.int32, (rows, rows), 0) == lax.broadcasted_iota(jnp.int32, (rows, rows), 1)
    others[0].wait()
    scale = jnp.where(diagonal, held_counts[...].astype(f32), 0.0).astype(bf16)
    others[1].wait()
    weighted[...] = jnp.dot(scale, held_upstream[...], preferred_element_type=f32).astype(bf16)
    my_cols[...] = weighted[:, piece(m, part)]
    for c in range(chunks):
        loads[c].wait()
        for k in range(copies):
            at = pl.ds(c * size, size)
            stores.append(pltpu.make_async_copy(held_weight.at[at], to_send.at[k, at], out_sem.at[k, c]))
            stores[-1].start()
    others[2].wait()
    others[3].wait()
    for i, k in enumerate(leaving):
        for n in range(picked.shape[1]):
            picked[i, n] = chosen(held_tenants, held_up, k, n, picked.shape[1], picked.shape[2])
    for store in stores:
        store.wait()


def chosen(tenants, up, distance, n, own_blocks, part_rank):
    _, d, m = place()
    wanted = tenants[(d ^ distance) * own_blocks + n] - d * up.shape[0]
    total = jnp.zeros((part_rank, up.shape[2]), bf16)
    for t in range(up.shape[0]):
        total = jnp.where(wanted == t, up[t, piece(m, part_rank)], total)
    return total


def pick_kernel(leaving, held, tenants, up, *refs):
    out = refs[-1]
    for i, k in enumerate(leaving):
        for n in range(out.shape[1]):
            value = chosen(tenants, up, k, n, out.shape[1], out.shape[2])
            for kept, got in zip(held, refs[:-1]):
                value = value + got[kept.index(k), n]
            out[i, n] = value


def back_kernel(held, tenants, up, weighted, *refs):
    out = refs[-1]
    part_rank, rows = out.shape
    own_blocks = refs[0].shape[1]
    size = rows // own_blocks
    for n in range(own_blocks):
        value = chosen(tenants, up, 0, n, own_blocks, part_rank)
        for kept, got in zip(held, refs[:-1]):
            value = value + got[kept.index(0), n]
        at = slice(n * size, (n + 1) * size)
        out[:, at] = lax.dot_general(
            value, weighted[at], (((1,), (1,)), ((), ())), preferred_element_type=f32
        ).astype(bf16)


def block_kernel(down, hidden, weighted, out):
    _, own_blocks, part_rank, _ = out.shape
    size = weighted.shape[0] // own_blocks
    _, _, m = place()
    low = lax.dot_general(
        down[piece(m, part_rank)], hidden[...], (((1,), (1,)), ((), ())), preferred_element_type=f32
    ).astype(bf16)
    for n in range(own_blocks):
        at = slice(n * size, (n + 1) * size)
        out[0, n] = jnp.dot(low[:, at], weighted[at], preferred_element_type=f32).astype(bf16)


def gradient_kernel(orders, scale, tenants, *refs):
    out = refs[-1]
    _, d, _ = place()
    for t in range(out.shape[0]):
        total = jnp.zeros(out.shape[1:], f32)
        for order, got in zip(orders, refs[:-1]):
            own_blocks = got.shape[1]
            for i, k in enumerate(order):
                for n in range(own_blocks):
                    wanted = tenants[(d ^ k) * own_blocks + n] - d * out.shape[0]
                    total = total + jnp.where(wanted == t, got[i, n].astype(f32), 0.0)
        out[t] = (total * scale).astype(bf16)


def frozen_kernel(near, distances, mine, other, slices, out, held):
    team, rows, part = mine.shape
    count, features, width = slices.shape
    per_part = count // 2
    g, d, m = place()
    own = g * near + lax.rem(d, near)
    for half in range(2):
        at = lax.rem(m + half, 2) * per_part
        for j in range(per_part):
            held[half, :, j * width : (j + 1) * width] = slices[at + j]
    dims = (((1,), (1,)), ((), ()))
    for k, distance in enumerate(distances):
        total = lax.dot_general(mine[k], held[0], dims, preferred_element_type=f32)
        total += lax.dot_general(other[k], held[1], dims, preferred_element_type=f32)
        out[own ^ distance] = total.astype(bf16)


def last_kernel(frozen, back, down, out, held, sem):
    team, rows, features = frozen.shape
    _, _, m = place()
    stores = []
    for k in range(team):
        at = pl.ds(pl.multiple_of(m * (team * features) + k * features, features), features)
        adapter = lax.dot_general(back[...], down[:, at], (((0,), (0,)), ((), ())), preferred_element_type=f32)
        held[k] = (frozen[k].astype(f32) + adapter_scale * adapter).astype(bf16)
        stores.append(pltpu.make_async_copy(held.at[k], out.at[:, pl.ds(k * features, features)], sem.at[k]))
        stores[-1].start()
    for store in stores:
        store.wait()


def local(
    hidden_input,
    upstream,
    rollout_row_counts,
    tenant_of_block,
    frozen_value_weight,
    common_down_factor,
    adapter_up_factor,
):
    group_count = lax.axis_size("groups")
    dp_count = lax.axis_size("dp")
    mp_count = lax.axis_size("mp")
    half_width, cols = frozen_value_weight.shape
    tenants_here, rank, out_width = adapter_up_factor.shape
    part_rank = rank // mp_count
    part_cols = out_width // mp_count
    rows = hidden_input.shape[0]
    own_blocks = tenant_of_block.shape[0] // dp_count
    block_rows = rows // own_blocks

    near = math.gcd(4, dp_count)
    team = group_count * near
    features = half_width // team
    teams = [
        [(gi * dp_count + base + k) * mp_count + mi for gi in range(group_count) for k in range(near)]
        for base in range(0, dp_count, near)
        for mi in range(mp_count)
    ]

    def swap(value, axis, bit):
        size = lax.axis_size(axis)
        return lax.ppermute(value, axis, [(k, k ^ bit) for k in range(size)])

    def shape(*dims):
        return jax.ShapeDtypeStruct(dims, bf16)

    def call(kernel, name, outs, in_specs, *values, scratch=(), out_specs=VMEM, params=PARAMS):
        return pl.pallas_call(
            kernel, in_specs=in_specs, out_specs=out_specs, out_shape=outs, scratch_shapes=list(scratch),
            compiler_params=params, name=name,
        )(*values)

    dp_bits = [1 << k for k in range(dp_count.bit_length() - 1)]
    near_bits = [bit for bit in dp_bits if bit < near]
    tie = lax.optimization_barrier

    repeats = dp_count // near
    leaving = [k for k in range(dp_count) if k & 1]
    remaining = [k for k in range(dp_count) if not k & 1]
    to_send, weighted, my_cols, picked = call(
        functools.partial(prepare_kernel, leaving), "prepare",
        [
            shape(repeats, near * features, cols),
            shape(rows, out_width),
            shape(rows, part_cols),
            shape(len(leaving), own_blocks, part_rank, out_width),
        ],
        [HBM] * 5,
        frozen_value_weight, upstream, rollout_row_counts[None], tenant_of_block, adapter_up_factor,
        out_specs=[HBM, VMEM, VMEM, VMEM],
        params=pltpu.CompilerParams(),
        scratch=[
            pltpu.VMEM((near * features, cols), bf16),
            pltpu.VMEM((rows, out_width), bf16),
            pltpu.VMEM((1, rows), jnp.int32),
            pltpu.SMEM(tenant_of_block.shape, jnp.int32),
            pltpu.VMEM(adapter_up_factor.shape, bf16),
            pltpu.SemaphoreType.DMA((4,)),
            pltpu.SemaphoreType.DMA((repeats, 4)),
            pltpu.SemaphoreType.DMA((4,)),
        ],
    )
    row_steps = [("dp", bit, bit) for bit in near_bits[1:] + near_bits[:1]] + [
        ("groups", 1 << k, near << k) for k in range(group_count.bit_length() - 1)
    ]
    team_rows, distances = my_cols[None], [0]
    held, got = [list(remaining)], [swap(picked, "dp", 1)]
    pieces = [
        call(
            block_kernel, "block", shape(1, own_blocks, part_rank, out_width), [VMEM, VMEM, VMEM],
            common_down_factor.T, hidden_input, weighted,
        )
    ]
    orders = [[0]]

    last = []

    def up_step(bit):
        leaving = [k for k in remaining if k & bit]
        value = call(
            functools.partial(pick_kernel, leaving, list(held)), "pick",
            shape(len(leaving), own_blocks, part_rank, out_width), [SMEM, VMEM] + [VMEM] * len(got),
            tenant_of_block, adapter_up_factor, *got,
        )
        last.append(value)
        remaining[:] = [k for k in remaining if not k & bit]
        held.append(list(remaining))
        got.append(swap(value, "dp", bit))

    def block_step(bit):
        value = jnp.concatenate(pieces) if len(pieces) > 1 else pieces[0]
        last.append(value)
        orders.append([k | bit for order in orders for k in order])
        pieces.append(swap(value, "dp", bit))

    up_bits, block_bits = dp_bits[1:], dp_bits[::-1]
    for step, (axis, bit, distance) in enumerate(row_steps):
        new_rows = swap(team_rows, axis, bit)
        if step:
            up_step(up_bits.pop(0))
        block_step(block_bits.pop(0))
        if step == 1:
            to_send, *_ = tie((to_send, team_rows, *last))
        if step == 0:
            team_rows, new_rows, got = tie((team_rows, new_rows, got))
        elif step < len(row_steps) - 1:
            team_rows, new_rows, got, pieces = tie((team_rows, new_rows, got, pieces))
        team_rows = jnp.concatenate([team_rows, new_rows])
        distances = distances + [k | distance for k in distances]
    other_rows = swap(team_rows, "mp", 1)
    weight_slices = lax.all_to_all(
        to_send.reshape(dp_count, features, cols), "dp", split_axis=0, concat_axis=0, tiled=True
    )

    weight_slices, got, pieces = tie((weight_slices, got, pieces))
    if cols % 128:
        slices = weight_slices.transpose(1, 0, 2).reshape(features, 2, part_cols).transpose(1, 0, 2)
    else:
        slices = weight_slices
    frozen = call(
        functools.partial(frozen_kernel, near, distances), "frozen", shape(team, rows, features), [VMEM, VMEM, VMEM],
        team_rows, other_rows, slices, scratch=[pltpu.VMEM((2, features, part_cols), bf16)],
    )
    frozen_mine = lax.all_to_all(
        frozen, ALL, split_axis=0, concat_axis=0, tiled=True, axis_index_groups=teams
    )
    got, pieces, _ = tie((got, pieces, frozen))
    for bit in up_bits:
        up_step(bit)
    for bit in block_bits:
        block_step(bit)
    back_part = call(
        functools.partial(back_kernel, held), "back", shape(part_rank, rows), [SMEM, VMEM, VMEM] + [VMEM] * len(got),
        tenant_of_block, adapter_up_factor, weighted, *got,
    )

    back_rank = lax.all_gather(back_part, "mp", axis=0, tiled=True)

    grad_part = call(
        functools.partial(gradient_kernel, orders, adapter_scale / block_rows), "gradient",
        shape(tenants_here, part_rank, out_width), [SMEM] + [VMEM] * len(pieces), tenant_of_block, *pieces,
    )
    up_factor_gradient = lax.all_gather(grad_part, "mp", axis=1, tiled=True)

    input_gradient = call(
        last_kernel, "last", shape(rows, half_width), [VMEM, VMEM, VMEM],
        frozen_mine, back_rank, common_down_factor.T, out_specs=HBM,
        scratch=[pltpu.VMEM((team, rows, features), bf16), pltpu.SemaphoreType.DMA((team,))],
    )
    return (input_gradient, up_factor_gradient)


def solution(mesh):
    placed = (
        P(("groups", "dp"), None),
        P(("groups", "dp"), None),
        P(("groups", "dp")),
        P("groups"),
        P("mp", "dp"),
        P(),
        P(("groups", "dp"), None, None),
    )
    return jax.shard_map(
        local,
        mesh=mesh,
        in_specs=placed,
        out_specs=(P(("groups", "dp"), "mp"), P(("groups", "dp"), None, None)),
        check_vma=False,
    )
```

time: 113 us -> 77.1 us (0.68)
  waiting for transfers between devices: 58.1 us -> 26.5 us
  Pallas kernels: 0 us -> 13.5 us
  matrix products: 9.62 us -> 0 us
  local copies, waits for them, and re-layouts: 13.5 us -> 7.95 us
  other arithmetic: 3.37 us -> 1.04 us
    all_to_all x5 -> x2, waiting for transfers between devices: 58.1 us -> 8.01 us  [the longest x1 8.01 us: local(): lax.all_to_all(frozen, ALL, split_axis=0, concat_axis=0, tiled=True, axis...]
    ppermute x1 -> x10, waiting for transfers between devices: 0.01 us -> 18.5 us  [swap(): return lax.ppermute(value, axis, [(k, k ^ bit) for k in range(size)])]
    ppermute x1 -> x10, starting transfers between devices: 0.07 us -> 15.7 us  [swap(): return lax.ppermute(value, axis, [(k, k ^ bit) for k in range(size)])]
    all_to_all x5 -> x2, starting transfers between devices: 22.3 us -> 7.34 us  [the longest x1 3.78 us: local(): lax.all_to_all(frozen, ALL, split_axis=0, concat_axis=0, tiled=True, axis...]
    pallas_call x0 -> x8, Pallas kernels: none -> 13.5 us  [call(): pl.pallas_call(kernel, in_specs=in_specs, out_specs=out_specs, out_shape=...]
    dot_general x7 -> x0, matrix products: 9.62 us -> none  [the longest x2 3.6 us: partial_term(): lax.dot_general(parts.reshape(team * rows, part_cols), slices.transpose(1...]
    broadcast_in_dim x4 -> x0, local copies, waits for them, and re-layouts: 5.29 us -> none  [the longest x2 4.15 us: local(): jnp.broadcast_to(group_weight.reshape(1, near, features, cols), (dp_count...]
    dynamic_slice x5 -> x0, local copies, waits for them, and re-layouts: 4.17 us -> none  [the longest x1 1.87 us: local(): lax.dynamic_slice_in_dim(frozen_value_weight, g * near * features, near *...]
  transfers between devices with their start and end apart: 6 -> 12, of which waited for: 5 -> 5; matrix products, arithmetic and copies ran while one was open for 12% -> 6% of each run, Pallas kernels for 0% -> 5%
where the time goes in v2:
time: 77.1 us; the launch traced here: 76.6 us
  waiting for transfers between devices  26.5 us (34%)
  starting transfers between devices  23 us (30%)
  Pallas kernels  13.5 us (18%)
  local copies, waits for them, and re-layouts  7.95 us (10%)
  blocking collectives  3.83 us (5%)
  other arithmetic  1.04 us (1%)
  between operations  0.78 us (1%)
    ppermute x10, waiting for transfers between devices, swap(): return lax.ppermute(value, axis, [(k, k ^ bit) for k in range(size)])  18.5 us
    ppermute x10, starting transfers between devices, swap(): return lax.ppermute(value, axis, [(k, k ^ bit) for k in range(size)])  15.7 us
    pallas_call x8, Pallas kernels, call(): pl.pallas_call(kernel, in_specs=in_specs, out_specs=out_specs, out_shape=...  13.5 us
    all_to_all x1, waiting for transfers between devices, local(): lax.all_to_all(frozen, ALL, split_axis=0, concat_axis=0, tiled=True, axis...  8.01 us
    unnamed x22, local copies, waits for them, and re-layouts  7.11 us
    all_to_all x1, starting transfers between devices, local(): lax.all_to_all(frozen, ALL, split_axis=0, concat_axis=0, tiled=True, axis...  3.78 us
    all_to_all x1, starting transfers between devices, local(): lax.all_to_all(to_send.reshape(dp_count, features, cols), 'dp', split_axi...  3.56 us
    all_gather x1, blocking collectives, local(): up_factor_gradient = lax.all_gather(grad_part, 'mp', axis=1, tiled=True)  1.99 us
  transfers between devices with their start and end apart: 12, of which 5 were waited for; matrix products, arithmetic and copies ran while one was open for 6% of the time, Pallas kernels for 5%

profile of v2, /device:TPU:0, one launch (start us, length us, event | category | flops | bytes accessed | tf_op | source)
XLA Modules:
  0.0 76.6 jit_solution(17106001394113902239)
XLA Ops:
  0.6 3.2 %prepare.1 = (bf16[2,2048,128]{2,1,0:T(8,128)(2,1)}, bf16[128,1024]{1,0:T(8,128)(2,1)}, bf16[128,512]{1,0:T(8,128)(2,1)}, bf16[4,1,32,1024]{3,2,1,0:T(8,128)(2,1)}) custom-call(bf16[4096,128]{1,0:T(8,128)(2,1)} %weight.1, bf16[128,1024]{1,0:T(8,128)(2,1)} %upstream.1, s32[1,128]{1,0:T(1,128)} %bitcast.9, s32[8]{0:T(128)} %tenants.9, bf16[2,64,1024]{2,1,0:T(8,128)(2,1)} %up.7), custom_call_target="tpu_custom_call" | custom-call | tf_op jit(solution)/shard_map/prepare/pallas_call | solution.py:199
  3.9 3.0 %collective-permute-start.1 = (bf16[4,1,32,1024]{3,2,1,0:T(8,128)(2,1)}, bf16[4,1,32,1024]{3,2,1,0:T(8,128)(2,1)S(1)}, u32[]{:S(2)}, u32[]{:S(2)}) collective-permute-start(bf16[4,1,32,1024]{3,2,1,0:T(8,128)(2,1)} %get-tuple-element.33), channel_id=1, source_target_pairs={{0,2},{2,0},{4,6},{6,4},{8,10},{10,8},{12,14},{14,12},{1,3},{3,1},... | collective-permute-start | bytes 786440 | tf_op jit(solution)/shard_map/ppermute | solution.py:193
  6.9 1.6 %collective-permute-start = (bf16[1,128,512]{2,1,0:T(8,128)(2,1)}, bf16[1,128,512]{2,1,0:T(8,128)(2,1)S(1)}, u32[]{:S(2)}, u32[]{:S(2)}) collective-permute-start(bf16[1,128,512]{2,1,0:T(8,128)(2,1)} %bitcast.7), channel_id=1, source_target_pairs={{0,4},{2,6},{4,0},{6,2},{8,12},{10,14},{12,8},{14,10},{1,5},{3,7},... | collective-permute-start | bytes 393224 | tf_op jit(solution)/shard_map/ppermute | solution.py:193
  8.4 1.6 %copy-done.2 = bf16[128,8192]{1,0:T(8,128)(2,1)S(1)} copy-done((bf16[128,8192]{1,0:T(8,128)(2,1)S(1)}, bf16[128,8192]{1,0:T(8,128)(2,1)}, u32[]{:S(2)}) %copy-start.2) | copy-done | bytes 2097176
  10.0 0.9 %copy-done.3 = bf16[128,1024]{1,0:T(8,128)(2,1)S(1)} copy-done((bf16[128,1024]{1,0:T(8,128)(2,1)S(1)}, bf16[128,1024]{1,0:T(8,128)(2,1)}, u32[]{:S(2)}) %copy-start.3) | copy-done | bytes 262168
  11.0 1.0 %block.1.refs_0_ = bf16[1,1,32,1024]{3,2,1,0:T(8,128)(2,1)S(1)} custom-call(bf16[64,8192]{1,0:T(8,128)(2,1)S(1)} %bitcast.4, bf16[128,8192]{1,0:T(8,128)(2,1)S(1)} %copy-done.2, bf16[128,1024]{1,0:T(8,128)(2,1)S(1)} %copy-done.3), custom_call_target="tpu_custom_call" | custom-call | tf_op jit(solution)/shard_map/block/pallas_call | solution.py:199
  12.0 2.7 %collective-permute-start.4 = (bf16[1,1,32,1024]{3,2,1,0:T(8,128)(2,1)S(1)}, bf16[1,1,32,1024]{3,2,1,0:T(8,128)(2,1)S(1)}, u32[]{:S(2)}, u32[]{:S(2)}) collective-permute-start(bf16[1,1,32,1024]{3,2,1,0:T(8,128)(2,1)S(1)} %block.1.refs_0_), channel_id=1, source_target_pairs={{0,8},{2,10},{4,12},{6,14},{8,0},{10,2},{12,4},{14,6},{1,9},{3,11}... | collective-permute-start | bytes 196616 | tf_op jit(solution)/shard_map/ppermute | solution.py:193
  14.7 0.6 collective-permute-start.2
  15.3 2.5 %collective-permute-done.4.refs_1_ = bf16[1,1,32,1024]{3,2,1,0:T(8,128)(2,1)S(1)} collective-permute-done((bf16[1,1,32,1024]{3,2,1,0:T(8,128)(2,1)S(1)}, bf16[1,1,32,1024]{3,2,1,0:T(8,128)(2,1)S(1)}, u32[]{:S(2)}, u32[]{:S(2)}) %collective-permute-start.4) | collective-permute-done | bytes 65568 | tf_op jit(solution)/shard_map/ppermute | solution.py:193
  17.9 0.6 pick.2
  18.5 2.1 %collective-permute-start.3 = (bf16[2,1,32,1024]{3,2,1,0:T(8,128)(2,1)S(1)}, bf16[2,1,32,1024]{3,2,1,0:T(8,128)(2,1)S(1)}, u32[]{:S(2)}, u32[]{:S(2)}) collective-permute-start(bf16[2,1,32,1024]{3,2,1,0:T(8,128)(2,1)S(1)} %pick.2), channel_id=1, source_target_pairs={{0,4},{2,6},{4,0},{6,2},{8,12},{10,14},{12,8},{14,10},{1,5},{3,7},... | collective-permute-start | bytes 393224 | tf_op jit(solution)/shard_map/ppermute | solution.py:193
  20.6 3.6 %all-to-all-start = ((bf16[8,512,128]{2,1,0:T(8,128)(2,1)}), bf16[8,512,128]{2,1,0:T(8,128)(2,1)S(1)}, u32[]{:S(2)}, u32[]{:S(2)}) async-start(bf16[8,512,128]{2,1,0:T(8,128)(2,1)} %bitcast.6), calls=%async_computation | async-start | bytes 2097152 | tf_op jit(solution)/shard_map/all_to_all | solution.py:282
  24.2 1.0 %pad_maximum_fusion = bf16[4,128,512]{2,1,0:T(8,128)(2,1)S(1)} fusion(bf16[2,128,512]{2,1,0:T(8,128)(2,1)} %collective-permute-done.2, bf16[2,128,512]{2,1,0:T(8,128)(2,1)S(1)} %constant_dynamic-update-slice_fusion), kind=kLoop, calls=%fused_computation | loop fusion | flops 262144 | bytes 1048576 | tf_op jit(solution)/shard_map/concatenate | solution.py:279
  25.3 1.6 %collective-permute-start.6 = (bf16[4,128,512]{2,1,0:T(8,128)(2,1)S(1)}, bf16[4,128,512]{2,1,0:T(8,128)(2,1)S(1)}, u32[]{:S(2)}, u32[]{:S(2)}) collective-permute-start(bf16[4,128,512]{2,1,0:T(8,128)(2,1)S(1)} %pad_maximum_fusion), channel_id=1, source_target_pairs={{0,16},{16,0},{1,17},{17,1},{2,18},{18,2},{3,19},{19,3},{4,20},{20... | collective-permute-start | bytes 1572872 | tf_op jit(solution)/shard_map/ppermute | solution.py:193
  26.8 0.7 constant_dynamic-update-slice_fusion.4
  27.6 1.7 %constant_dynamic-update-slice_fusion.3 = bf16[8,128,512]{2,1,0:T(8,128)(2,1)} fusion(bf16[8,128,512]{2,1,0:T(8,128)(2,1)} %constant_dynamic-update-slice_fusion.4, bf16[2,128,512]{2,1,0:T(8,128)(2,1)} %collective-permute-done.2), kind=kLoop, calls=%fused_computation.6 | loop fusion | bytes 524288
  29.2 7.4 %collective-permute-done.6 = bf16[4,128,512]{2,1,0:T(8,128)(2,1)S(1)} collective-permute-done((bf16[4,128,512]{2,1,0:T(8,128)(2,1)S(1)}, bf16[4,128,512]{2,1,0:T(8,128)(2,1)S(1)}, u32[]{:S(2)}, u32[]{:S(2)}) %collective-permute-start.6) | collective-permute-done | bytes 524320 | tf_op jit(solution)/shard_map/ppermute | solution.py:193
  36.6 0.8 %constant_dynamic-update-slice_fusion.2.mine = bf16[8,128,512]{2,1,0:T(8,128)(2,1)} fusion(bf16[8,128,512]{2,1,0:T(8,128)(2,1)} %constant_dynamic-update-slice_fusion.3, bf16[4,128,512]{2,1,0:T(8,128)(2,1)S(1)} %collective-permute-done.6), kind=kLoop, calls=%fused_computation.5 | loop fusion | bytes 1048576 | tf_op jit(solution)/shard_map/concatenate | solution.py:279
  37.5 1.7 %collective-permute-start.9 = (bf16[4,1,32,1024]{3,2,1,0:T(8,128)(2,1)S(1)}, bf16[4,1,32,1024]{3,2,1,0:T(8,128)(2,1)S(1)}, u32[]{:S(2)}, u32[]{:S(2)}) collective-permute-start(bf16[4,1,32,1024]{3,2,1,0:T(8,128)(2,1)S(1)} %pad_maximum_fusion.1), channel_id=1, source_target_pairs={{0,2},{2,0},{4,6},{6,4},{8,10},{10,8},{12,14},{14,12},{1,3},{3,1},... | collective-permute-start | bytes 786440 | tf_op jit(solution)/shard_map/ppermute | solution.py:193
  39.8 2.5 %collective-permute-start.8 = (bf16[1,1,32,1024]{3,2,1,0:T(8,128)(2,1)S(1)}, bf16[1,1,32,1024]{3,2,1,0:T(8,128)(2,1)S(1)}, u32[]{:S(2)}, u32[]{:S(2)}) collective-permute-start(bf16[1,1,32,1024]{3,2,1,0:T(8,128)(2,1)S(1)} %pick.3), channel_id=1, source_target_pairs={{0,8},{2,10},{4,12},{6,14},{8,0},{10,2},{12,4},{14,6},{1,9},{3,11}... | collective-permute-start | bytes 196616 | tf_op jit(solution)/shard_map/ppermute | solution.py:193
  42.2 8.4 %collective-permute-done.8.refs_2_ = bf16[1,1,32,1024]{3,2,1,0:T(8,128)(2,1)S(1)} collective-permute-done((bf16[1,1,32,1024]{3,2,1,0:T(8,128)(2,1)S(1)}, bf16[1,1,32,1024]{3,2,1,0:T(8,128)(2,1)S(1)}, u32[]{:S(2)}, u32[]{:S(2)}) %collective-permute-start.8) | collective-permute-done | bytes 65568 | tf_op jit(solution)/shard_map/ppermute | solution.py:193
  50.6 0.6 copy-done.5
  51.3 5.4 %frozen.1 = bf16[8,128,512]{2,1,0:T(8,128)(2,1)} custom-call(bf16[8,128,512]{2,1,0:T(8,128)(2,1)} %constant_dynamic-update-slice_fusion.2.mine, bf16[8,128,512]{2,1,0:T(8,128)(2,1)} %collective-permute-done.7.other, bf16[8,512,128]{2,1,0:T(8,128)(2,1)S(1)} %all-to-all-done.slices), custom_call_target="tpu_custom_call" | custom-call | tf_op jit(solution)/shard_map/frozen/pallas_call | solution.py:199
  56.7 3.8 %all-to-all-start.1 = ((bf16[8,128,512]{2,1,0:T(8,128)(2,1)}), bf16[8,128,512]{2,1,0:T(8,128)(2,1)S(1)}, u32[]{:S(2)}, u32[]{:S(2)}) async-start(bf16[8,128,512]{2,1,0:T(8,128)(2,1)} %frozen.1), calls=%async_computation.1 | async-start | bytes 2097152 | tf_op jit(solution)/shard_map/all_to_all | solution.py:295
  60.5 0.8 %gradient.1 = bf16[2,32,1024]{2,1,0:T(8,128)(2,1)S(1)} custom-call(s32[8]{0:T(128)S(1)} %copy-done.7, bf16[1,1,32,1024]{3,2,1,0:T(8,128)(2,1)S(1)} %block.1.refs_0_, bf16[1,1,32,1024]{3,2,1,0:T(8,128)(2,1)S(1)} %collective-permute-done.4.refs_1_, bf16[2,1,32,1024]{3,2,1,0:T(8,128)(2,1)S(1)} %collective-permute-done.5.refs_2_, ...), custom_call_target="tpu_custom_call" | custom-call | tf_op jit(solution)/shard_map/gradient/pallas_call | solution.py:199
  61.2 2.0 %all_gather.7 = bf16[2,64,1024]{2,1,0:T(8,128)(2,1)S(1)} all-gather(bf16[2,32,1024]{2,1,0:T(8,128)(2,1)S(1)} %gradient.1), channel_id=1, replica_groups=mesh['groups'=2,'dp'=8,'mp'=2] {'mp'}, dimensions={1}, use_global_device_ids=true | all-gather | bytes 393216 | tf_op jit(solution)/shard_map/all_gather | solution.py:314
  63.2 0.8 %copy-done.6 = bf16[1,1,32,1024]{3,2,1,0:T(8,128)(2,1)S(1)} copy-done((bf16[1,1,32,1024]{3,2,1,0:T(8,128)(2,1)S(1)}, bf16[1,1,32,1024]{3,2,1,0:T(8,128)(2,1)}, u32[]{:S(2)}) %copy-start.6) | copy-done | bytes 65560
  64.1 0.7 back.1
  64.8 1.8 %all_gather.6.back = bf16[64,128]{1,0:T(8,128)(2,1)S(1)} all-gather(bf16[32,128]{1,0:T(8,128)(2,1)S(1)} %back.1), channel_id=1, replica_groups=mesh['groups'=2,'dp'=8,'mp'=2] {'mp'}, dimensions={0}, use_global_device_ids=true | all-gather | bytes 24576 | tf_op jit(solution)/shard_map/all_gather | solution.py:308
  66.6 8.0 %all-to-all-done.1.frozen = bf16[8,128,512]{2,1,0:T(8,128)(2,1)S(1)} async-done(((bf16[8,128,512]{2,1,0:T(8,128)(2,1)}), bf16[8,128,512]{2,1,0:T(8,128)(2,1)S(1)}, u32[]{:S(2)}, u32[]{:S(2)}) %all-to-all-start.1) | async-done | bytes 1048608 | tf_op jit(solution)/shard_map/all_to_all | solution.py:295
  74.6 1.2 %last.1 = bf16[128,4096]{1,0:T(8,128)(2,1)} custom-call(bf16[8,128,512]{2,1,0:T(8,128)(2,1)S(1)} %all-to-all-done.1.frozen, bf16[64,128]{1,0:T(8,128)(2,1)S(1)} %all_gather.6.back, bf16[64,8192]{1,0:T(8,128)(2,1)S(1)} %bitcast.5), custom_call_target="tpu_custom_call" | custom-call | tf_op jit(solution)/shard_map/last/pallas_call | solution.py:199
  75.9 0.7 copy.13
  (29 shorter events, 0.9 us)
Async XLA Ops:
  0.6 7.8 %copy-start = (bf16[8192,64]{0,1:T(8,128)(2,1)S(1)}, bf16[8192,64]{0,1:T(8,128)(2,1)}, u32[]{:S(2)}) copy-start(bf16[8192,64]{0,1:T(8,128)(2,1)} %param.12) | copy-start | bytes 3145732
  3.9 10.8 %collective-permute-start.1 = (bf16[4,1,32,1024]{3,2,1,0:T(8,128)(2,1)}, bf16[4,1,32,1024]{3,2,1,0:T(8,128)(2,1)S(1)}, u32[]{:S(2)}, u32[]{:S(2)}) collective-permute-start(bf16[4,1,32,1024]{3,2,1,0:T(8,128)(2,1)} %get-tuple-element.33), channel_id=1, source_target_pairs={{0,2},{2,0},{4,6},{6,4},{8,10},{10,8},{12,14},{14,12},{1,3},{3,1},... | collective-permute-start | bytes 786440 | tf_op jit(solution)/shard_map/ppermute | solution.py:193
  6.9 7.8 %collective-permute-start = (bf16[1,128,512]{2,1,0:T(8,128)(2,1)}, bf16[1,128,512]{2,1,0:T(8,128)(2,1)S(1)}, u32[]{:S(2)}, u32[]{:S(2)}) collective-permute-start(bf16[1,128,512]{2,1,0:T(8,128)(2,1)} %bitcast.7), channel_id=1, source_target_pairs={{0,4},{2,6},{4,0},{6,2},{8,12},{10,14},{12,8},{14,10},{1,5},{3,7},... | collective-permute-start | bytes 393224 | tf_op jit(solution)/shard_map/ppermute | solution.py:193
  8.4 1.6 %copy-start.2 = (bf16[128,8192]{1,0:T(8,128)(2,1)S(1)}, bf16[128,8192]{1,0:T(8,128)(2,1)}, u32[]{:S(2)}) copy-start(bf16[128,8192]{1,0:T(8,128)(2,1)} %hidden.1) | copy-start | bytes 6291460
  10.0 0.9 %copy-start.3 = (bf16[128,1024]{1,0:T(8,128)(2,1)S(1)}, bf16[128,1024]{1,0:T(8,128)(2,1)}, u32[]{:S(2)}) copy-start(bf16[128,1024]{1,0:T(8,128)(2,1)} %get-tuple-element.37.weighted) | copy-start | bytes 786436
  11.0 3.7 %copy-start.8 = (bf16[128,512]{1,0:T(8,128)(2,1)S(1)}, bf16[128,512]{1,0:T(8,128)(2,1)}, u32[]{:S(2)}) copy-start(bf16[128,512]{1,0:T(8,128)(2,1)} %get-tuple-element.32) | copy-start | bytes 393220
  11.0 6.9 %copy-start.1 = (bf16[2,64,1024]{2,1,0:T(8,128)(2,1)S(1)}, bf16[2,64,1024]{2,1,0:T(8,128)(2,1)}, u32[]{:S(2)}) copy-start(bf16[2,64,1024]{2,1,0:T(8,128)(2,1)} %up.7) | copy-start | bytes 786436
  11.0 6.9 %copy-start.7 = (s32[8]{0:T(128)S(1)}, s32[8]{0:T(128)}, u32[]{:S(2)}) copy-start(s32[8]{0:T(128)} %tenants.9) | copy-start | bytes 100
  12.0 5.8 %collective-permute-start.4 = (bf16[1,1,32,1024]{3,2,1,0:T(8,128)(2,1)S(1)}, bf16[1,1,32,1024]{3,2,1,0:T(8,128)(2,1)S(1)}, u32[]{:S(2)}, u32[]{:S(2)}) collective-permute-start(bf16[1,1,32,1024]{3,2,1,0:T(8,128)(2,1)S(1)} %block.1.refs_0_), channel_id=1, source_target_pairs={{0,8},{2,10},{4,12},{6,14},{8,0},{10,2},{12,4},{14,6},{1,9},{3,11}... | collective-permute-start | bytes 196616 | tf_op jit(solution)/shard_map/ppermute | solution.py:193
  14.7 9.6 %collective-permute-start.2 = (bf16[2,128,512]{2,1,0:T(8,128)(2,1)S(1)}, bf16[2,128,512]{2,1,0:T(8,128)(2,1)}, u32[]{:S(2)}, u32[]{:S(2)}) collective-permute-start(bf16[2,128,512]{2,1,0:T(8,128)(2,1)S(1)} %constant_dynamic-update-slice_fusion), channel_id=1, source_target_pairs={{0,2},{2,0},{4,6},{6,4},{8,10},{10,8},{12,14},{14,12},{1,3},{3,1},... | collective-permute-start | bytes 786440 | tf_op jit(solution)/shard_map/ppermute | solution.py:193
  17.8 6.3 %collective-permute-start.5 = (bf16[2,1,32,1024]{3,2,1,0:T(8,128)(2,1)S(1)}, bf16[2,1,32,1024]{3,2,1,0:T(8,128)(2,1)S(1)}, u32[]{:S(2)}, u32[]{:S(2)}) collective-permute-start(bf16[2,1,32,1024]{3,2,1,0:T(8,128)(2,1)S(1)} %pad_maximum_fusion.2), channel_id=1, source_target_pairs={{0,4},{2,6},{4,0},{6,2},{8,12},{10,14},{12,8},{14,10},{1,5},{3,7},... | collective-permute-start | bytes 393224 | tf_op jit(solution)/shard_map/ppermute | solution.py:193
  18.5 5.8 %collective-permute-start.3 = (bf16[2,1,32,1024]{3,2,1,0:T(8,128)(2,1)S(1)}, bf16[2,1,32,1024]{3,2,1,0:T(8,128)(2,1)S(1)}, u32[]{:S(2)}, u32[]{:S(2)}) collective-permute-start(bf16[2,1,32,1024]{3,2,1,0:T(8,128)(2,1)S(1)} %pick.2), channel_id=1, source_target_pairs={{0,4},{2,6},{4,0},{6,2},{8,12},{10,14},{12,8},{14,10},{1,5},{3,7},... | collective-permute-start | bytes 393224 | tf_op jit(solution)/shard_map/ppermute | solution.py:193
  20.6 30.7 %all-to-all-start = ((bf16[8,512,128]{2,1,0:T(8,128)(2,1)}), bf16[8,512,128]{2,1,0:T(8,128)(2,1)S(1)}, u32[]{:S(2)}, u32[]{:S(2)}) async-start(bf16[8,512,128]{2,1,0:T(8,128)(2,1)} %bitcast.6), calls=%async_computation | async-start | bytes 2097152 | tf_op jit(solution)/shard_map/all_to_all | solution.py:282
  25.3 11.4 %collective-permute-start.6 = (bf16[4,128,512]{2,1,0:T(8,128)(2,1)S(1)}, bf16[4,128,512]{2,1,0:T(8,128)(2,1)S(1)}, u32[]{:S(2)}, u32[]{:S(2)}) collective-permute-start(bf16[4,128,512]{2,1,0:T(8,128)(2,1)S(1)} %pad_maximum_fusion), channel_id=1, source_target_pairs={{0,16},{16,0},{1,17},{17,1},{2,18},{18,2},{3,19},{19,3},{4,20},{20... | collective-permute-start | bytes 1572872 | tf_op jit(solution)/shard_map/ppermute | solution.py:193
  37.5 13.8 %collective-permute-start.7 = (bf16[8,128,512]{2,1,0:T(8,128)(2,1)}, bf16[8,128,512]{2,1,0:T(8,128)(2,1)}, u32[]{:S(2)}, u32[]{:S(2)}) collective-permute-start(bf16[8,128,512]{2,1,0:T(8,128)(2,1)} %constant_dynamic-update-slice_fusion.2.mine), channel_id=1, source_target_pairs={{0,1},{1,0},{2,3},{3,2},{4,5},{5,4},{6,7},{7,6},{8,9},{9,8},{10,11... | collective-permute-start | bytes 3145736 | tf_op jit(solution)/shard_map/ppermute | solution.py:193
  37.5 13.8 %collective-permute-start.9 = (bf16[4,1,32,1024]{3,2,1,0:T(8,128)(2,1)S(1)}, bf16[4,1,32,1024]{3,2,1,0:T(8,128)(2,1)S(1)}, u32[]{:S(2)}, u32[]{:S(2)}) collective-permute-start(bf16[4,1,32,1024]{3,2,1,0:T(8,128)(2,1)S(1)} %pad_maximum_fusion.1), channel_id=1, source_target_pairs={{0,2},{2,0},{4,6},{6,4},{8,10},{10,8},{12,14},{14,12},{1,3},{3,1},... | collective-permute-start | bytes 786440 | tf_op jit(solution)/shard_map/ppermute | solution.py:193
  39.8 10.9 %collective-permute-start.8 = (bf16[1,1,32,1024]{3,2,1,0:T(8,128)(2,1)S(1)}, bf16[1,1,32,1024]{3,2,1,0:T(8,128)(2,1)S(1)}, u32[]{:S(2)}, u32[]{:S(2)}) collective-permute-start(bf16[1,1,32,1024]{3,2,1,0:T(8,128)(2,1)S(1)} %pick.3), channel_id=1, source_target_pairs={{0,8},{2,10},{4,12},{6,14},{8,0},{10,2},{12,4},{14,6},{1,9},{3,11}... | collective-permute-start | bytes 196616 | tf_op jit(solution)/shard_map/ppermute | solution.py:193
  50.6 0.6 copy-start.5
  56.7 6.6 %copy-start.4 = (bf16[128,1024]{1,0:T(8,128)(2,1)S(1)}, bf16[128,1024]{1,0:T(8,128)(2,1)}, u32[]{:S(2)}) copy-start(bf16[128,1024]{1,0:T(8,128)(2,1)} %get-tuple-element.37.weighted) | copy-start | bytes 786436
  56.7 18.0 %all-to-all-start.1 = ((bf16[8,128,512]{2,1,0:T(8,128)(2,1)}), bf16[8,128,512]{2,1,0:T(8,128)(2,1)S(1)}, u32[]{:S(2)}, u32[]{:S(2)}) async-start(bf16[8,128,512]{2,1,0:T(8,128)(2,1)} %frozen.1), calls=%async_computation.1 | async-start | bytes 2097152 | tf_op jit(solution)/shard_map/all_to_all | solution.py:295
  63.2 0.8 %copy-start.6 = (bf16[1,1,32,1024]{3,2,1,0:T(8,128)(2,1)S(1)}, bf16[1,1,32,1024]{3,2,1,0:T(8,128)(2,1)}, u32[]{:S(2)}) copy-start(bf16[1,1,32,1024]{3,2,1,0:T(8,128)(2,1)} %copy-done.5) | copy-start | bytes 196612

commit v3 on v2

--- a/solution.py
+++ b/solution.py
@@ -87,6 +87,15 @@
             out[i, n] = value
 
 
+def both_kernel(leaving, held, tenants, up, *refs):
+    out = refs[-1]
+    pick_kernel(leaving, held, tenants, up, *refs[: len(held)], out.at[: len(leaving)])
+    at = len(leaving)
+    for blocks in refs[len(held) : -1]:
+        out[at : at + blocks.shape[0]] = blocks[...]
+        at += blocks.shape[0]
+
+
 def back_kernel(held, tenants, up, weighted, *refs):
     out = refs[-1]
     part_rank, rows = out.shape
@@ -122,13 +131,13 @@
         for order, got in zip(orders, refs[:-1]):
             own_blocks = got.shape[1]
             for i, k in enumerate(order):
-                for n in range(own_blocks):
+                for n in range(own_blocks if k is not None else 0):
                     wanted = tenants[(d ^ k) * own_blocks + n] - d * out.shape[0]
                     total = total + jnp.where(wanted == t, got[i, n].astype(f32), 0.0)
         out[t] = (total * scale).astype(bf16)
 
 
-def frozen_kernel(near, distances, mine, other, slices, out, held):
+def frozen_kernel(near, distances, mine, other, slices, out, held, ready, sem):
     team, rows, part = mine.shape
     count, features, width = slices.shape
     per_part = count // 2
@@ -139,10 +148,16 @@
         for j in range(per_part):
             held[half, :, j * width : (j + 1) * width] = slices[at + j]
     dims = (((1,), (1,)), ((), ()))
-    for k, distance in enumerate(distances):
-        total = lax.dot_general(mine[k], held[0], dims, preferred_element_type=f32)
-        total += lax.dot_general(other[k], held[1], dims, preferred_element_type=f32)
-        out[own ^ distance] = total.astype(bf16)
+    stores = []
+    for c in range(0, team, 2):
+        total = lax.dot_general(mine[c : c + 2].reshape(2 * rows, part), held[0], dims, preferred_element_type=f32)
+        total += lax.dot_general(other[c : c + 2].reshape(2 * rows, part), held[1], dims, preferred_element_type=f32)
+        ready[c : c + 2] = total.astype(bf16).reshape(2, rows, features)
+        for k in range(c, c + 2):
+            stores.append(pltpu.make_async_copy(ready.at[k], out.at[own ^ distances[k]], sem.at[k]))
+            stores[-1].start()
+    for store in stores:
+        store.wait()
 
 
 def last_kernel(frozen, back, down, out, held, sem):
@@ -258,18 +273,43 @@
         held.append(list(remaining))
         got.append(swap(value, "dp", bit))
 
+    def gathered():
+        return [k for order in orders for k in order if k is not None]
+
     def block_step(bit):
-        value = jnp.concatenate(pieces) if len(pieces) > 1 else pieces[0]
+        kept = [value[order.count(None) :] for value, order in zip(pieces, orders)]
+        value = jnp.concatenate(kept) if len(kept) > 1 else kept[0]
         last.append(value)
-        orders.append([k | bit for order in orders for k in order])
+        orders.append([k | bit for k in gathered()])
         pieces.append(swap(value, "dp", bit))
+
+    def both_step(bit):
+        leaving = [k for k in remaining if k & bit]
+        blocks = gathered()
+        value = call(
+            functools.partial(both_kernel, leaving, list(held)), "both",
+            shape(len(leaving) + len(blocks), own_blocks, part_rank, out_width),
+            [SMEM, VMEM] + [VMEM] * (len(got) + len(pieces)),
+            tenant_of_block, adapter_up_factor, *got, *pieces,
+        )
+        last.append(value)
+        remaining[:] = [k for k in remaining if not k & bit]
+        arrived = swap(value, "dp", bit)
+        held.append(list(remaining))
+        got.append(arrived)
+        orders.append([None] * len(leaving) + [k | bit for k in blocks])
+        pieces.append(arrived)
 
     up_bits, block_bits = dp_bits[1:], dp_bits[::-1]
     for step, (axis, bit, distance) in enumerate(row_steps):
         new_rows = swap(team_rows, axis, bit)
-        if step:
-            up_step(up_bits.pop(0))
-        block_step(block_bits.pop(0))
+        if step == 1 and up_bits[0] == block_bits[0]:
+            both_step(up_bits.pop(0))
+            block_bits.pop(0)
+        else:
+            if step:
+                up_step(up_bits.pop(0))
+            block_step(block_bits.pop(0))
         if step == 1:
             to_send, *_ = tie((to_send, team_rows, *last))
         if step == 0:
@@ -290,7 +330,12 @@
         slices = weight_slices
     frozen = call(
         functools.partial(frozen_kernel, near, distances), "frozen", shape(team, rows, features), [VMEM, VMEM, VMEM],
-        team_rows, other_rows, slices, scratch=[pltpu.VMEM((2, features, part_cols), bf16)],
+        team_rows, other_rows, slices, out_specs=HBM,
+        scratch=[
+            pltpu.VMEM((2, features, part_cols), bf16),
+            pltpu.VMEM((team, rows, features), bf16),
+            pltpu.SemaphoreType.DMA((team,)),
+        ],
     )
     frozen_mine = lax.all_to_all(
         frozen, ALL, split_axis=0, concat_axis=0, tiled=True, axis_index_groups=teams

time: 77.1 us -> 75.5 us (0.979)
  Pallas kernels: 13.5 us -> 11.7 us
    ppermute x10 -> x9, starting transfers between devices: 15.7 us -> 13.3 us  [swap(): return lax.ppermute(value, axis, [(k, k ^ bit) for k in range(size)])]
    all_to_all x1, starting transfers between devices: 3.56 us -> 5.96 us  [local(): lax.all_to_all(to_send.reshape(dp_count, features, cols), 'dp', split_axi...]
    pallas_call x8, Pallas kernels: 13.5 us -> 11.7 us  [call(): pl.pallas_call(kernel, in_specs=in_specs, out_specs=out_specs, out_shape=...]
    ppermute x10 -> x9, waiting for transfers between devices: 18.5 us -> 19.2 us  [swap(): return lax.ppermute(value, axis, [(k, k ^ bit) for k in range(size)])]
  transfers between devices with their start and end apart: 12 -> 11, of which waited for: 5 -> 6; matrix products, arithmetic and copies ran while one was open for 6% -> 6% of each run, Pallas kernels for 5% -> 4%
where the time goes in v3:
time: 75.5 us; the launch traced here: 75.1 us
  waiting for transfers between devices  26.8 us (35%)
  starting transfers between devices  22.9 us (30%)
  Pallas kernels  11.7 us (15%)
  local copies, waits for them, and re-layouts  7.97 us (11%)
  blocking collectives  3.83 us (5%)
  other arithmetic  1.03 us (1%)
  between operations  0.79 us (1%)
    ppermute x9, waiting for transfers between devices, swap(): return lax.ppermute(value, axis, [(k, k ^ bit) for k in range(size)])  19.2 us
    ppermute x9, starting transfers between devices, swap(): return lax.ppermute(value, axis, [(k, k ^ bit) for k in range(size)])  13.3 us
    pallas_call x8, Pallas kernels, call(): pl.pallas_call(kernel, in_specs=in_specs, out_specs=out_specs, out_shape=...  11.7 us
    all_to_all x1, waiting for transfers between devices, local(): lax.all_to_all(frozen, ALL, split_axis=0, concat_axis=0, tiled=True, axis...  7.6 us
    unnamed x22, local copies, waits for them, and re-layouts  7.12 us
    all_to_all x1, starting transfers between devices, local(): lax.all_to_all(to_send.reshape(dp_count, features, cols), 'dp', split_axi...  5.96 us
    all_to_all x1, starting transfers between devices, local(): lax.all_to_all(frozen, ALL, split_axis=0, concat_axis=0, tiled=True, axis...  3.7 us
    all_gather x1, blocking collectives, local(): up_factor_gradient = lax.all_gather(grad_part, 'mp', axis=1, tiled=True)  1.99 us
  transfers between devices with their start and end apart: 11, of which 6 were waited for; matrix products, arithmetic and copies ran while one was open for 6% of the time, Pallas kernels for 4%

profile of v3, /device:TPU:0, one launch (start us, length us, event | category | flops | bytes accessed | tf_op | source)
XLA Modules:
  0.0 75.1 jit_solution(14842926108379975849)
XLA Ops:
  0.7 3.2 %prepare.1 = (bf16[2,2048,128]{2,1,0:T(8,128)(2,1)}, bf16[128,1024]{1,0:T(8,128)(2,1)}, bf16[128,512]{1,0:T(8,128)(2,1)}, bf16[4,1,32,1024]{3,2,1,0:T(8,128)(2,1)}) custom-call(bf16[4096,128]{1,0:T(8,128)(2,1)} %weight.1, bf16[128,1024]{1,0:T(8,128)(2,1)} %upstream.1, s32[1,128]{1,0:T(1,128)} %bitcast.9, s32[8]{0:T(128)} %tenants.9, bf16[2,64,1024]{2,1,0:T(8,128)(2,1)} %up.7), custom_call_target="tpu_custom_call" | custom-call | tf_op jit(solution)/shard_map/prepare/pallas_call | solution.py:214
  3.9 3.0 %collective-permute-start.1 = (bf16[4,1,32,1024]{3,2,1,0:T(8,128)(2,1)}, bf16[4,1,32,1024]{3,2,1,0:T(8,128)(2,1)S(1)}, u32[]{:S(2)}, u32[]{:S(2)}) collective-permute-start(bf16[4,1,32,1024]{3,2,1,0:T(8,128)(2,1)} %get-tuple-element.33), channel_id=1, source_target_pairs={{0,2},{2,0},{4,6},{6,4},{8,10},{10,8},{12,14},{14,12},{1,3},{3,1},... | collective-permute-start | bytes 786440 | tf_op jit(solution)/shard_map/ppermute | solution.py:208
  6.9 1.6 %collective-permute-start = (bf16[1,128,512]{2,1,0:T(8,128)(2,1)}, bf16[1,128,512]{2,1,0:T(8,128)(2,1)S(1)}, u32[]{:S(2)}, u32[]{:S(2)}) collective-permute-start(bf16[1,128,512]{2,1,0:T(8,128)(2,1)} %bitcast.7), channel_id=1, source_target_pairs={{0,4},{2,6},{4,0},{6,2},{8,12},{10,14},{12,8},{14,10},{1,5},{3,7},... | collective-permute-start | bytes 393224 | tf_op jit(solution)/shard_map/ppermute | solution.py:208
  8.5 1.6 %copy-done.2 = bf16[128,8192]{1,0:T(8,128)(2,1)S(1)} copy-done((bf16[128,8192]{1,0:T(8,128)(2,1)S(1)}, bf16[128,8192]{1,0:T(8,128)(2,1)}, u32[]{:S(2)}) %copy-start.2) | copy-done | bytes 2097176
  10.1 0.9 %copy-done.3 = bf16[128,1024]{1,0:T(8,128)(2,1)S(1)} copy-done((bf16[128,1024]{1,0:T(8,128)(2,1)S(1)}, bf16[128,1024]{1,0:T(8,128)(2,1)}, u32[]{:S(2)}) %copy-start.3) | copy-done | bytes 262168
  11.0 1.0 %block.1.refs_1_.refs_0_ = bf16[1,1,32,1024]{3,2,1,0:T(8,128)(2,1)S(1)} custom-call(bf16[64,8192]{1,0:T(8,128)(2,1)S(1)} %bitcast.4, bf16[128,8192]{1,0:T(8,128)(2,1)S(1)} %copy-done.2, bf16[128,1024]{1,0:T(8,128)(2,1)S(1)} %copy-done.3), custom_call_target="tpu_custom_call" | custom-call | tf_op jit(solution)/shard_map/block/pallas_call | solution.py:214
  12.0 2.7 %collective-permute-start.3 = (bf16[1,1,32,1024]{3,2,1,0:T(8,128)(2,1)S(1)}, bf16[1,1,32,1024]{3,2,1,0:T(8,128)(2,1)S(1)}, u32[]{:S(2)}, u32[]{:S(2)}) collective-permute-start(bf16[1,1,32,1024]{3,2,1,0:T(8,128)(2,1)S(1)} %block.1.refs_1_.refs_0_), channel_id=1, source_target_pairs={{0,8},{2,10},{4,12},{6,14},{8,0},{10,2},{12,4},{14,6},{1,9},{3,11}... | collective-permute-start | bytes 196616 | tf_op jit(solution)/shard_map/ppermute | solution.py:208
  14.7 3.1 %collective-permute-done.3.refs_2_.refs_1_ = bf16[1,1,32,1024]{3,2,1,0:T(8,128)(2,1)S(1)} collective-permute-done((bf16[1,1,32,1024]{3,2,1,0:T(8,128)(2,1)S(1)}, bf16[1,1,32,1024]{3,2,1,0:T(8,128)(2,1)S(1)}, u32[]{:S(2)}, u32[]{:S(2)}) %collective-permute-start.3) | collective-permute-done | bytes 65568 | tf_op jit(solution)/shard_map/ppermute | solution.py:208
  17.8 0.6 both.1
  18.5 0.3 collective-permute-start.2
  18.8 6.0 %all-to-all-start = ((bf16[8,512,128]{2,1,0:T(8,128)(2,1)}), bf16[8,512,128]{2,1,0:T(8,128)(2,1)S(1)}, u32[]{:S(2)}, u32[]{:S(2)}) async-start(bf16[8,512,128]{2,1,0:T(8,128)(2,1)} %bitcast.6), calls=%async_computation | async-start | bytes 2097152 | tf_op jit(solution)/shard_map/all_to_all | solution.py:322
  25.1 1.0 %pad_maximum_fusion = bf16[4,128,512]{2,1,0:T(8,128)(2,1)S(1)} fusion(bf16[2,128,512]{2,1,0:T(8,128)(2,1)} %collective-permute-done.2, bf16[2,128,512]{2,1,0:T(8,128)(2,1)S(1)} %constant_dynamic-update-slice_fusion), kind=kLoop, calls=%fused_computation | loop fusion | flops 262144 | bytes 1048576 | tf_op jit(solution)/shard_map/concatenate | solution.py:319
  26.1 1.6 %collective-permute-start.5 = (bf16[4,128,512]{2,1,0:T(8,128)(2,1)S(1)}, bf16[4,128,512]{2,1,0:T(8,128)(2,1)S(1)}, u32[]{:S(2)}, u32[]{:S(2)}) collective-permute-start(bf16[4,128,512]{2,1,0:T(8,128)(2,1)S(1)} %pad_maximum_fusion), channel_id=1, source_target_pairs={{0,16},{16,0},{1,17},{17,1},{2,18},{18,2},{3,19},{19,3},{4,20},{20... | collective-permute-start | bytes 1572872 | tf_op jit(solution)/shard_map/ppermute | solution.py:208
  27.6 0.7 constant_dynamic-update-slice_fusion.4
  28.4 1.7 %constant_dynamic-update-slice_fusion.3 = bf16[8,128,512]{2,1,0:T(8,128)(2,1)} fusion(bf16[8,128,512]{2,1,0:T(8,128)(2,1)} %constant_dynamic-update-slice_fusion.4, bf16[2,128,512]{2,1,0:T(8,128)(2,1)} %collective-permute-done.2), kind=kLoop, calls=%fused_computation.5 | loop fusion | bytes 524288
  30.0 7.1 %collective-permute-done.5 = bf16[4,128,512]{2,1,0:T(8,128)(2,1)S(1)} collective-permute-done((bf16[4,128,512]{2,1,0:T(8,128)(2,1)S(1)}, bf16[4,128,512]{2,1,0:T(8,128)(2,1)S(1)}, u32[]{:S(2)}, u32[]{:S(2)}) %collective-permute-start.5) | collective-permute-done | bytes 524320 | tf_op jit(solution)/shard_map/ppermute | solution.py:208
  37.1 0.8 %constant_dynamic-update-slice_fusion.2.mine = bf16[8,128,512]{2,1,0:T(8,128)(2,1)} fusion(bf16[8,128,512]{2,1,0:T(8,128)(2,1)} %constant_dynamic-update-slice_fusion.3, bf16[4,128,512]{2,1,0:T(8,128)(2,1)S(1)} %collective-permute-done.5), kind=kLoop, calls=%fused_computation.4 | loop fusion | bytes 1048576 | tf_op jit(solution)/shard_map/concatenate | solution.py:319
  38.0 1.7 %collective-permute-start.8 = (bf16[4,1,32,1024]{3,2,1,0:T(8,128)(2,1)S(1)}, bf16[4,1,32,1024]{3,2,1,0:T(8,128)(2,1)S(1)}, u32[]{:S(2)}, u32[]{:S(2)}) collective-permute-start(bf16[4,1,32,1024]{3,2,1,0:T(8,128)(2,1)S(1)} %pad_maximum_fusion.1), channel_id=1, source_target_pairs={{0,2},{2,0},{4,6},{6,4},{8,10},{10,8},{12,14},{14,12},{1,3},{3,1},... | collective-permute-start | bytes 786440 | tf_op jit(solution)/shard_map/ppermute | solution.py:208
  39.6 0.6 pick.1
  40.2 2.4 %collective-permute-start.7 = (bf16[1,1,32,1024]{3,2,1,0:T(8,128)(2,1)S(1)}, bf16[1,1,32,1024]{3,2,1,0:T(8,128)(2,1)S(1)}, u32[]{:S(2)}, u32[]{:S(2)}) collective-permute-start(bf16[1,1,32,1024]{3,2,1,0:T(8,128)(2,1)S(1)} %pick.1), channel_id=1, source_target_pairs={{0,8},{2,10},{4,12},{6,14},{8,0},{10,2},{12,4},{14,6},{1,9},{3,11}... | collective-permute-start | bytes 196616 | tf_op jit(solution)/shard_map/ppermute | solution.py:208
  42.7 8.6 %collective-permute-done.7.refs_2_ = bf16[1,1,32,1024]{3,2,1,0:T(8,128)(2,1)S(1)} collective-permute-done((bf16[1,1,32,1024]{3,2,1,0:T(8,128)(2,1)S(1)}, bf16[1,1,32,1024]{3,2,1,0:T(8,128)(2,1)S(1)}, u32[]{:S(2)}, u32[]{:S(2)}) %collective-permute-start.7) | collective-permute-done | bytes 65568 | tf_op jit(solution)/shard_map/ppermute | solution.py:208
  51.3 0.6 copy-done.5
  51.9 3.7 %frozen.1 = bf16[8,128,512]{2,1,0:T(8,128)(2,1)} custom-call(bf16[8,128,512]{2,1,0:T(8,128)(2,1)} %constant_dynamic-update-slice_fusion.2.mine, bf16[8,128,512]{2,1,0:T(8,128)(2,1)} %collective-permute-done.6.other, bf16[8,512,128]{2,1,0:T(8,128)(2,1)S(1)} %all-to-all-done.slices), custom_call_target="tpu_custom_call" | custom-call | tf_op jit(solution)/shard_map/frozen/pallas_call | solution.py:214
  55.6 3.7 %all-to-all-start.1 = ((bf16[8,128,512]{2,1,0:T(8,128)(2,1)}), bf16[8,128,512]{2,1,0:T(8,128)(2,1)S(1)}, u32[]{:S(2)}, u32[]{:S(2)}) async-start(bf16[8,128,512]{2,1,0:T(8,128)(2,1)} %frozen.1), calls=%async_computation.1 | async-start | bytes 2097152 | tf_op jit(solution)/shard_map/all_to_all | solution.py:340
  59.3 0.8 %gradient.1 = bf16[2,32,1024]{2,1,0:T(8,128)(2,1)S(1)} custom-call(s32[8]{0:T(128)S(1)} %copy-done.7, bf16[1,1,32,1024]{3,2,1,0:T(8,128)(2,1)S(1)} %block.1.refs_1_.refs_0_, bf16[1,1,32,1024]{3,2,1,0:T(8,128)(2,1)S(1)} %collective-permute-done.3.refs_2_.refs_1_, bf16[4,1,32,1024]{3,2,1,0:T(8,128)(2,1)S(1)} %collective-permute-done.4.refs_1_.refs_2_, ...), custom_call_target="tpu_custom_call" | custom-call | tf_op jit(solution)/shard_map/gradient/pallas_call | solution.py:214
  60.1 2.0 %all_gather.7 = bf16[2,64,1024]{2,1,0:T(8,128)(2,1)S(1)} all-gather(bf16[2,32,1024]{2,1,0:T(8,128)(2,1)S(1)} %gradient.1), channel_id=1, replica_groups=mesh['groups'=2,'dp'=8,'mp'=2] {'mp'}, dimensions={1}, use_global_device_ids=true | all-gather | bytes 393216 | tf_op jit(solution)/shard_map/all_gather | solution.py:359
  62.1 0.8 %copy-done.6 = bf16[1,1,32,1024]{3,2,1,0:T(8,128)(2,1)S(1)} copy-done((bf16[1,1,32,1024]{3,2,1,0:T(8,128)(2,1)S(1)}, bf16[1,1,32,1024]{3,2,1,0:T(8,128)(2,1)}, u32[]{:S(2)}) %copy-start.6) | copy-done | bytes 65560
  63.0 0.7 back.1
  63.7 1.8 %all_gather.6.back = bf16[64,128]{1,0:T(8,128)(2,1)S(1)} all-gather(bf16[32,128]{1,0:T(8,128)(2,1)S(1)} %back.1), channel_id=1, replica_groups=mesh['groups'=2,'dp'=8,'mp'=2] {'mp'}, dimensions={0}, use_global_device_ids=true | all-gather | bytes 24576 | tf_op jit(solution)/shard_map/all_gather | solution.py:353
  65.5 7.6 %all-to-all-done.1.frozen = bf16[8,128,512]{2,1,0:T(8,128)(2,1)S(1)} async-done(((bf16[8,128,512]{2,1,0:T(8,128)(2,1)}), bf16[8,128,512]{2,1,0:T(8,128)(2,1)S(1)}, u32[]{:S(2)}, u32[]{:S(2)}) %all-to-all-start.1) | async-done | bytes 1048608 | tf_op jit(solution)/shard_map/all_to_all | solution.py:340
  73.1 1.2 %last.1 = bf16[128,4096]{1,0:T(8,128)(2,1)} custom-call(bf16[8,128,512]{2,1,0:T(8,128)(2,1)S(1)} %all-to-all-done.1.frozen, bf16[64,128]{1,0:T(8,128)(2,1)S(1)} %all_gather.6.back, bf16[64,8192]{1,0:T(8,128)(2,1)S(1)} %bitcast.5), custom_call_target="tpu_custom_call" | custom-call | tf_op jit(solution)/shard_map/last/pallas_call | solution.py:214
  74.4 0.7 copy.13
  (27 shorter events, 0.5 us)
Async XLA Ops:
  0.6 7.8 %copy-start = (bf16[8192,64]{0,1:T(8,128)(2,1)S(1)}, bf16[8192,64]{0,1:T(8,128)(2,1)}, u32[]{:S(2)}) copy-start(bf16[8192,64]{0,1:T(8,128)(2,1)} %param.12) | copy-start | bytes 3145732
  0.6 17.2 %copy-start.7 = (s32[8]{0:T(128)S(1)}, s32[8]{0:T(128)}, u32[]{:S(2)}) copy-start(s32[8]{0:T(128)} %tenants.9) | copy-start | bytes 100
  3.9 13.9 %copy-start.1 = (bf16[2,64,1024]{2,1,0:T(8,128)(2,1)S(1)}, bf16[2,64,1024]{2,1,0:T(8,128)(2,1)}, u32[]{:S(2)}) copy-start(bf16[2,64,1024]{2,1,0:T(8,128)(2,1)} %up.7) | copy-start | bytes 786436
  3.9 10.8 %collective-permute-start.1 = (bf16[4,1,32,1024]{3,2,1,0:T(8,128)(2,1)}, bf16[4,1,32,1024]{3,2,1,0:T(8,128)(2,1)S(1)}, u32[]{:S(2)}, u32[]{:S(2)}) collective-permute-start(bf16[4,1,32,1024]{3,2,1,0:T(8,128)(2,1)} %get-tuple-element.33), channel_id=1, source_target_pairs={{0,2},{2,0},{4,6},{6,4},{8,10},{10,8},{12,14},{14,12},{1,3},{3,1},... | collective-permute-start | bytes 786440 | tf_op jit(solution)/shard_map/ppermute | solution.py:208
  6.9 7.8 %collective-permute-start = (bf16[1,128,512]{2,1,0:T(8,128)(2,1)}, bf16[1,128,512]{2,1,0:T(8,128)(2,1)S(1)}, u32[]{:S(2)}, u32[]{:S(2)}) collective-permute-start(bf16[1,128,512]{2,1,0:T(8,128)(2,1)} %bitcast.7), channel_id=1, source_target_pairs={{0,4},{2,6},{4,0},{6,2},{8,12},{10,14},{12,8},{14,10},{1,5},{3,7},... | collective-permute-start | bytes 393224 | tf_op jit(solution)/shard_map/ppermute | solution.py:208
  8.5 1.6 %copy-start.2 = (bf16[128,8192]{1,0:T(8,128)(2,1)S(1)}, bf16[128,8192]{1,0:T(8,128)(2,1)}, u32[]{:S(2)}) copy-start(bf16[128,8192]{1,0:T(8,128)(2,1)} %hidden.1) | copy-start | bytes 6291460
  10.1 0.9 %copy-start.3 = (bf16[128,1024]{1,0:T(8,128)(2,1)S(1)}, bf16[128,1024]{1,0:T(8,128)(2,1)}, u32[]{:S(2)}) copy-start(bf16[128,1024]{1,0:T(8,128)(2,1)} %get-tuple-element.37.weighted) | copy-start | bytes 786436
  11.0 3.7 %copy-start.8 = (bf16[128,512]{1,0:T(8,128)(2,1)S(1)}, bf16[128,512]{1,0:T(8,128)(2,1)}, u32[]{:S(2)}) copy-start(bf16[128,512]{1,0:T(8,128)(2,1)} %get-tuple-element.32) | copy-start | bytes 393220
  12.0 5.8 %collective-permute-start.3 = (bf16[1,1,32,1024]{3,2,1,0:T(8,128)(2,1)S(1)}, bf16[1,1,32,1024]{3,2,1,0:T(8,128)(2,1)S(1)}, u32[]{:S(2)}, u32[]{:S(2)}) collective-permute-start(bf16[1,1,32,1024]{3,2,1,0:T(8,128)(2,1)S(1)} %block.1.refs_1_.refs_0_), channel_id=1, source_target_pairs={{0,8},{2,10},{4,12},{6,14},{8,0},{10,2},{12,4},{14,6},{1,9},{3,11}... | collective-permute-start | bytes 196616 | tf_op jit(solution)/shard_map/ppermute | solution.py:208
  18.4 6.4 %collective-permute-start.4 = (bf16[4,1,32,1024]{3,2,1,0:T(8,128)(2,1)S(1)}, bf16[4,1,32,1024]{3,2,1,0:T(8,128)(2,1)S(1)}, u32[]{:S(2)}, u32[]{:S(2)}) collective-permute-start(bf16[4,1,32,1024]{3,2,1,0:T(8,128)(2,1)S(1)} %both.1), channel_id=1, source_target_pairs={{0,4},{2,6},{4,0},{6,2},{8,12},{10,14},{12,8},{14,10},{1,5},{3,7},... | collective-permute-start | bytes 786440 | tf_op jit(solution)/shard_map/ppermute | solution.py:208
  18.5 6.6 %collective-permute-start.2 = (bf16[2,128,512]{2,1,0:T(8,128)(2,1)S(1)}, bf16[2,128,512]{2,1,0:T(8,128)(2,1)}, u32[]{:S(2)}, u32[]{:S(2)}) collective-permute-start(bf16[2,128,512]{2,1,0:T(8,128)(2,1)S(1)} %constant_dynamic-update-slice_fusion), channel_id=1, source_target_pairs={{0,2},{2,0},{4,6},{6,4},{8,10},{10,8},{12,14},{14,12},{1,3},{3,1},... | collective-permute-start | bytes 786440 | tf_op jit(solution)/shard_map/ppermute | solution.py:208
  18.8 33.1 %all-to-all-start = ((bf16[8,512,128]{2,1,0:T(8,128)(2,1)}), bf16[8,512,128]{2,1,0:T(8,128)(2,1)S(1)}, u32[]{:S(2)}, u32[]{:S(2)}) async-start(bf16[8,512,128]{2,1,0:T(8,128)(2,1)} %bitcast.6), calls=%async_computation | async-start | bytes 2097152 | tf_op jit(solution)/shard_map/all_to_all | solution.py:322
  26.1 11.1 %collective-permute-start.5 = (bf16[4,128,512]{2,1,0:T(8,128)(2,1)S(1)}, bf16[4,128,512]{2,1,0:T(8,128)(2,1)S(1)}, u32[]{:S(2)}, u32[]{:S(2)}) collective-permute-start(bf16[4,128,512]{2,1,0:T(8,128)(2,1)S(1)} %pad_maximum_fusion), channel_id=1, source_target_pairs={{0,16},{16,0},{1,17},{17,1},{2,18},{18,2},{3,19},{19,3},{4,20},{20... | collective-permute-start | bytes 1572872 | tf_op jit(solution)/shard_map/ppermute | solution.py:208
  37.9 14.0 %collective-permute-start.6 = (bf16[8,128,512]{2,1,0:T(8,128)(2,1)}, bf16[8,128,512]{2,1,0:T(8,128)(2,1)}, u32[]{:S(2)}, u32[]{:S(2)}) collective-permute-start(bf16[8,128,512]{2,1,0:T(8,128)(2,1)} %constant_dynamic-update-slice_fusion.2.mine), channel_id=1, source_target_pairs={{0,1},{1,0},{2,3},{3,2},{4,5},{5,4},{6,7},{7,6},{8,9},{9,8},{10,11... | collective-permute-start | bytes 3145736 | tf_op jit(solution)/shard_map/ppermute | solution.py:208
  38.0 13.9 %collective-permute-start.8 = (bf16[4,1,32,1024]{3,2,1,0:T(8,128)(2,1)S(1)}, bf16[4,1,32,1024]{3,2,1,0:T(8,128)(2,1)S(1)}, u32[]{:S(2)}, u32[]{:S(2)}) collective-permute-start(bf16[4,1,32,1024]{3,2,1,0:T(8,128)(2,1)S(1)} %pad_maximum_fusion.1), channel_id=1, source_target_pairs={{0,2},{2,0},{4,6},{6,4},{8,10},{10,8},{12,14},{14,12},{1,3},{3,1},... | collective-permute-start | bytes 786440 | tf_op jit(solution)/shard_map/ppermute | solution.py:208
  40.2 11.1 %collective-permute-start.7 = (bf16[1,1,32,1024]{3,2,1,0:T(8,128)(2,1)S(1)}, bf16[1,1,32,1024]{3,2,1,0:T(8,128)(2,1)S(1)}, u32[]{:S(2)}, u32[]{:S(2)}) collective-permute-start(bf16[1,1,32,1024]{3,2,1,0:T(8,128)(2,1)S(1)} %pick.1), channel_id=1, source_target_pairs={{0,8},{2,10},{4,12},{6,14},{8,0},{10,2},{12,4},{14,6},{1,9},{3,11}... | collective-permute-start | bytes 196616 | tf_op jit(solution)/shard_map/ppermute | solution.py:208
  51.3 0.6 copy-start.5
  55.6 6.5 %copy-start.4 = (bf16[128,1024]{1,0:T(8,128)(2,1)S(1)}, bf16[128,1024]{1,0:T(8,128)(2,1)}, u32[]{:S(2)}) copy-start(bf16[128,1024]{1,0:T(8,128)(2,1)} %get-tuple-element.37.weighted) | copy-start | bytes 786436
  55.6 17.5 %all-to-all-start.1 = ((bf16[8,128,512]{2,1,0:T(8,128)(2,1)}), bf16[8,128,512]{2,1,0:T(8,128)(2,1)S(1)}, u32[]{:S(2)}, u32[]{:S(2)}) async-start(bf16[8,128,512]{2,1,0:T(8,128)(2,1)} %frozen.1), calls=%async_computation.1 | async-start | bytes 2097152 | tf_op jit(solution)/shard_map/all_to_all | solution.py:340
  62.1 0.8 %copy-start.6 = (bf16[1,1,32,1024]{3,2,1,0:T(8,128)(2,1)S(1)}, bf16[1,1,32,1024]{3,2,1,0:T(8,128)(2,1)}, u32[]{:S(2)}) copy-start(bf16[1,1,32,1024]{3,2,1,0:T(8,128)(2,1)} %copy-done.5) | copy-start | bytes 196612

commit v4 on v3

--- a/solution.py
+++ b/solution.py
@@ -26,44 +26,65 @@
 
 
 def prepare_kernel(
-    leaving, weight, upstream, counts, tenants, up, to_send, weighted, my_cols, picked,
-    held_weight, held_upstream, held_counts, held_tenants, held_up, in_sem, out_sem, other_sem,
+    leaving, counts, upstream, tenants, up, down, hidden, weighted, my_cols, picked, block,
+    held_counts, held_upstream, held_tenants, held_up, held_down, held_hidden, sem,
 ):
-    g, _, m = place()
+    _, _, m = place()
+    _, own_blocks, part_rank, _ = block.shape
+    loads = [
+        pltpu.make_async_copy(source, target, sem.at[i])
+        for i, (source, target) in enumerate(
+            [
+                (counts, held_counts),
+                (upstream, held_upstream),
+                (tenants, held_tenants),
+                (up, held_up),
+                (down.at[piece(m, part_rank)], held_down),
+                (hidden, held_hidden),
+            ]
+        )
+    ]
+    for load in loads:
+        load.start()
+    rows, part = my_cols.shape
+    diagonal = lax.broadcasted_iota(jnp.int32, (rows, rows), 0) == lax.broadcasted_iota(jnp.int32, (rows, rows), 1)
+    loads[0].wait()
+    scale = jnp.where(diagonal, held_counts[...].astype(f32), 0.0).astype(bf16)
+    loads[1].wait()
+    weighted[...] = jnp.dot(scale, held_upstream[...], preferred_element_type=f32).astype(bf16)
+    my_cols[...] = weighted[:, piece(m, part)]
+    loads[2].wait()
+    loads[3].wait()
+    for i, k in enumerate(leaving):
+        for n in range(own_blocks):
+            picked[i, n] = chosen(held_tenants, held_up, k, n, own_blocks, part_rank)
+    loads[4].wait()
+    loads[5].wait()
+    low = lax.dot_general(
+        held_down[...], held_hidden[...], (((1,), (1,)), ((), ())), preferred_element_type=f32
+    ).astype(bf16)
+    size = rows // own_blocks
+    for n in range(own_blocks):
+        at = slice(n * size, (n + 1) * size)
+        block[0, n] = jnp.dot(low[:, at], weighted[at], preferred_element_type=f32).astype(bf16)
+
+
+def spread_kernel(weight, _, to_send, held, in_sem, out_sem):
+    g, _, _ = place()
     copies, depth = to_send.shape[0], to_send.shape[1]
     chunks = in_sem.shape[0]
     size = depth // chunks
-    others = [
-        pltpu.make_async_copy(source, target, other_sem.at[i])
-        for i, (source, target) in enumerate(
-            [(counts, held_counts), (upstream, held_upstream), (tenants, held_tenants), (up, held_up)]
-        )
-    ]
-    for load in others:
-        load.start()
     loads, stores = [], []
     for c in range(chunks):
         at = pl.ds(pl.multiple_of(g * depth + c * size, size), size)
-        loads.append(pltpu.make_async_copy(weight.at[at], held_weight.at[pl.ds(c * size, size)], in_sem.at[c]))
+        loads.append(pltpu.make_async_copy(weight.at[at], held.at[pl.ds(c * size, size)], in_sem.at[c]))
         loads[-1].start()
-    rows, part = my_cols.shape
-    diagonal = lax.broadcasted_iota(jnp.int32, (rows, rows), 0) == lax.broadcasted_iota(jnp.int32, (rows, rows), 1)
-    others[0].wait()
-    scale = jnp.where(diagonal, held_counts[...].astype(f32), 0.0).astype(bf16)
-    others[1].wait()
-    weighted[...] = jnp.dot(scale, held_upstream[...], preferred_element_type=f32).astype(bf16)
-    my_cols[...] = weighted[:, piece(m, part)]
     for c in range(chunks):
         loads[c].wait()
         for k in range(copies):
             at = pl.ds(c * size, size)
-            stores.append(pltpu.make_async_copy(held_weight.at[at], to_send.at[k, at], out_sem.at[k, c]))
+            stores.append(pltpu.make_async_copy(held.at[at], to_send.at[k, at], out_sem.at[k, c]))
             stores[-1].start()
-    others[2].wait()
-    others[3].wait()
-    for i, k in enumerate(leaving):
-        for n in range(picked.shape[1]):
-            picked[i, n] = chosen(held_tenants, held_up, k, n, picked.shape[1], picked.shape[2])
     for store in stores:
         store.wait()
 
@@ -109,18 +130,6 @@
         out[:, at] = lax.dot_general(
             value, weighted[at], (((1,), (1,)), ((), ())), preferred_element_type=f32
         ).astype(bf16)
-
-
-def block_kernel(down, hidden, weighted, out):
-    _, own_blocks, part_rank, _ = out.shape
-    size = weighted.shape[0] // own_blocks
-    _, _, m = place()
-    low = lax.dot_general(
-        down[piece(m, part_rank)], hidden[...], (((1,), (1,)), ((), ())), preferred_element_type=f32
-    ).astype(bf16)
-    for n in range(own_blocks):
-        at = slice(n * size, (n + 1) * size)
-        out[0, n] = jnp.dot(low[:, at], weighted[at], preferred_element_type=f32).astype(bf16)
 
 
 def gradient_kernel(orders, scale, tenants, *refs):
@@ -223,27 +232,33 @@
     repeats = dp_count // near
     leaving = [k for k in range(dp_count) if k & 1]
     remaining = [k for k in range(dp_count) if not k & 1]
-    to_send, weighted, my_cols, picked = call(
+    weighted, my_cols, picked, block = call(
         functools.partial(prepare_kernel, leaving), "prepare",
         [
-            shape(repeats, near * features, cols),
             shape(rows, out_width),
             shape(rows, part_cols),
             shape(len(leaving), own_blocks, part_rank, out_width),
+            shape(1, own_blocks, part_rank, out_width),
         ],
-        [HBM] * 5,
-        frozen_value_weight, upstream, rollout_row_counts[None], tenant_of_block, adapter_up_factor,
-        out_specs=[HBM, VMEM, VMEM, VMEM],
-        params=pltpu.CompilerParams(),
+        [HBM] * 6, rollout_row_counts[None], upstream, tenant_of_block, adapter_up_factor, common_down_factor.T,
+        hidden_input, out_specs=[VMEM] * 4, params=pltpu.CompilerParams(),
+        scratch=[
+            pltpu.VMEM((1, rows), jnp.int32),
+            pltpu.VMEM((rows, out_width), bf16),
+            pltpu.SMEM(tenant_of_block.shape, jnp.int32),
+            pltpu.VMEM(adapter_up_factor.shape, bf16),
+            pltpu.VMEM((part_rank, common_down_factor.shape[0]), bf16),
+            pltpu.VMEM(hidden_input.shape, bf16),
+            pltpu.SemaphoreType.DMA((6,)),
+        ],
+    )
+    to_send = call(
+        spread_kernel, "spread", shape(repeats, near * features, cols), [HBM] * 2, frozen_value_weight, block,
+        out_specs=HBM, params=pltpu.CompilerParams(),
         scratch=[
             pltpu.VMEM((near * features, cols), bf16),
-            pltpu.VMEM((rows, out_width), bf16),
-            pltpu.VMEM((1, rows), jnp.int32),
-            pltpu.SMEM(tenant_of_block.shape, jnp.int32),
-            pltpu.VMEM(adapter_up_factor.shape, bf16),
             pltpu.SemaphoreType.DMA((4,)),
             pltpu.SemaphoreType.DMA((repeats, 4)),
-            pltpu.SemaphoreType.DMA((4,)),
         ],
     )
     row_steps = [("dp", bit, bit) for bit in near_bits[1:] + near_bits[:1]] + [
@@ -251,14 +266,7 @@
     ]
     team_rows, distances = my_cols[None], [0]
     held, got = [list(remaining)], [swap(picked, "dp", 1)]
-    pieces = [
-        call(
-            block_kernel, "block", shape(1, own_blocks, part_rank, out_width), [VMEM, VMEM, VMEM],
-            common_down_factor.T, hidden_input, weighted,
-        )
-    ]
-    orders = [[0]]
-
+    pieces, orders = [block], [[0]]
     last = []
 
     def up_step(bit):
@@ -313,7 +321,7 @@
         if step == 1:
             to_send, *_ = tie((to_send, team_rows, *last))
         if step == 0:
-            team_rows, new_rows, got = tie((team_rows, new_rows, got))
+            team_rows, new_rows, got, to_send = tie((team_rows, new_rows, got, to_send))
         elif step < len(row_steps) - 1:
             team_rows, new_rows, got, pieces = tie((team_rows, new_rows, got, pieces))
         team_rows = jnp.concatenate([team_rows, new_rows])
@@ -323,7 +331,7 @@
         to_send.reshape(dp_count, features, cols), "dp", split_axis=0, concat_axis=0, tiled=True
     )
 
-    weight_slices, got, pieces = tie((weight_slices, got, pieces))
+    weight_slices, _ = tie((weight_slices, last))
     if cols % 128:
         slices = weight_slices.transpose(1, 0, 2).reshape(features, 2, part_cols).transpose(1, 0, 2)
     else:
@@ -337,10 +345,10 @@
             pltpu.SemaphoreType.DMA((team,)),
         ],
     )
+    frozen, got, pieces = tie((frozen, got, pieces))
     frozen_mine = lax.all_to_all(
         frozen, ALL, split_axis=0, concat_axis=0, tiled=True, axis_index_groups=teams
     )
-    got, pieces, _ = tie((got, pieces, frozen))
     for bit in up_bits:
         up_step(bit)
     for bit in block_bits:

time: 75.5 us -> 72.4 us (0.959)
  local copies, waits for them, and re-layouts: 7.97 us -> 0.84 us
  starting transfers between devices: 22.9 us -> 25.1 us
  Pallas kernels: 11.7 us -> 13.7 us
    unnamed x22 -> x16, local copies, waits for them, and re-layouts: 7.12 us -> 0.79 us
    ppermute x9, starting transfers between devices: 13.3 us -> 17.1 us  [swap(): return lax.ppermute(value, axis, [(k, k ^ bit) for k in range(size)])]
    ppermute x9, waiting for transfers between devices: 19.2 us -> 15.8 us  [swap(): return lax.ppermute(value, axis, [(k, k ^ bit) for k in range(size)])]
    all_to_all x1, waiting for transfers between devices: 0.01 us -> 2.14 us  [local(): lax.all_to_all(to_send.reshape(dp_count, features, cols), 'dp', split_axi...]
    all_to_all x1, starting transfers between devices: 5.96 us -> 3.89 us  [local(): lax.all_to_all(to_send.reshape(dp_count, features, cols), 'dp', split_axi...]
    pallas_call x8, Pallas kernels: 11.7 us -> 13.7 us  [call(): pl.pallas_call(kernel, in_specs=in_specs, out_specs=out_specs, out_shape=...]
    all_to_all x1, waiting for transfers between devices: 7.6 us -> 9.02 us  [local(): lax.all_to_all(frozen, ALL, split_axis=0, concat_axis=0, tiled=True, axis...]
    concatenate x1, other arithmetic: 1 us -> 0.05 us  [local(): team_rows = jnp.concatenate([team_rows, new_rows])]
  transfers between devices with their start and end apart: 11 -> 11, of which waited for: 6 -> 7; matrix products, arithmetic and copies ran while one was open for 6% -> 1% of each run, Pallas kernels for 4% -> 11%
where the time goes in v4:
time: 72.4 us; the launch traced here: 72 us
  waiting for transfers between devices  26.9 us (37%)
  starting transfers between devices  25.1 us (35%)
  Pallas kernels  13.7 us (19%)
  blocking collectives  3.83 us (5%)
  local copies, waits for them, and re-layouts  0.84 us (1%)
  between operations  0.81 us (1%)
  other arithmetic  0.8 us (1%)
    ppermute x9, starting transfers between devices, swap(): return lax.ppermute(value, axis, [(k, k ^ bit) for k in range(size)])  17.1 us
    ppermute x9, waiting for transfers between devices, swap(): return lax.ppermute(value, axis, [(k, k ^ bit) for k in range(size)])  15.8 us
    pallas_call x8, Pallas kernels, call(): pl.pallas_call(kernel, in_specs=in_specs, out_specs=out_specs, out_shape=...  13.7 us
    all_to_all x1, waiting for transfers between devices, local(): lax.all_to_all(frozen, ALL, split_axis=0, concat_axis=0, tiled=True, axis...  9.02 us
    all_to_all x1, starting transfers between devices, local(): lax.all_to_all(frozen, ALL, split_axis=0, concat_axis=0, tiled=True, axis...  4.1 us
    all_to_all x1, starting transfers between devices, local(): lax.all_to_all(to_send.reshape(dp_count, features, cols), 'dp', split_axi...  3.89 us
    all_to_all x1, waiting for transfers between devices, local(): lax.all_to_all(to_send.reshape(dp_count, features, cols), 'dp', split_axi...  2.14 us
    all_gather x1, blocking collectives, local(): up_factor_gradient = lax.all_gather(grad_part, 'mp', axis=1, tiled=True)  1.99 us
  transfers between devices with their start and end apart: 11, of which 7 were waited for; matrix products, arithmetic and copies ran while one was open for 1% of the time, Pallas kernels for 11%

profile of v4, /device:TPU:0, one launch (start us, length us, event | category | flops | bytes accessed | tf_op | source)
XLA Modules:
  0.0 72.0 jit_solution(16877845544205499433)
XLA Ops:
  0.6 3.6 %prepare.1 = (bf16[128,1024]{1,0:T(8,128)(2,1)}, bf16[128,512]{1,0:T(8,128)(2,1)}, bf16[4,1,32,1024]{3,2,1,0:T(8,128)(2,1)}, bf16[1,1,32,1024]{3,2,1,0:T(8,128)(2,1)}) custom-call(s32[1,128]{1,0:T(1,128)} %bitcast.9, bf16[128,1024]{1,0:T(8,128)(2,1)} %upstream.1, s32[8]{0:T(128)} %tenants.9, bf16[2,64,1024]{2,1,0:T(8,128)(2,1)} %up.7, ...), custom_call_target="tpu_custom_call" | custom-call | tf_op jit(solution)/shard_map/prepare/pallas_call | solution.py:223
  4.3 0.0 copy-start.1
  4.3 0.0 copy-start.4
  4.3 3.0 %collective-permute-start.1 = (bf16[4,1,32,1024]{3,2,1,0:T(8,128)(2,1)}, bf16[4,1,32,1024]{3,2,1,0:T(8,128)(2,1)S(1)}, u32[]{:S(2)}, u32[]{:S(2)}) collective-permute-start(bf16[4,1,32,1024]{3,2,1,0:T(8,128)(2,1)} %get-tuple-element.28), channel_id=1, source_target_pairs={{0,2},{2,0},{4,6},{6,4},{8,10},{10,8},{12,14},{14,12},{1,3},{3,1},... | collective-permute-start | bytes 786440 | tf_op jit(solution)/shard_map/ppermute | solution.py:217
  7.3 1.6 %collective-permute-start = (bf16[1,128,512]{2,1,0:T(8,128)(2,1)}, bf16[1,128,512]{2,1,0:T(8,128)(2,1)S(1)}, u32[]{:S(2)}, u32[]{:S(2)}) collective-permute-start(bf16[1,128,512]{2,1,0:T(8,128)(2,1)} %bitcast.7), channel_id=1, source_target_pairs={{0,4},{2,6},{4,0},{6,2},{8,12},{10,14},{12,8},{14,10},{1,5},{3,7},... | collective-permute-start | bytes 393224 | tf_op jit(solution)/shard_map/ppermute | solution.py:217
  8.9 2.6 %collective-permute-start.3 = (bf16[1,1,32,1024]{3,2,1,0:T(8,128)(2,1)}, bf16[1,1,32,1024]{3,2,1,0:T(8,128)(2,1)S(1)}, u32[]{:S(2)}, u32[]{:S(2)}) collective-permute-start(bf16[1,1,32,1024]{3,2,1,0:T(8,128)(2,1)} %get-tuple-element.48._.refs_1_.refs_0_), channel_id=1, source_target_pairs={{0,8},{2,10},{4,12},{6,14},{8,0},{10,2},{12,4},{14,6},{1,9},{3,11}... | collective-permute-start | bytes 196616 | tf_op jit(solution)/shard_map/ppermute | solution.py:217
  11.5 2.0 %spread.1 = bf16[2,2048,128]{2,1,0:T(8,128)(2,1)} custom-call(bf16[4096,128]{1,0:T(8,128)(2,1)} %weight.1, bf16[1,1,32,1024]{3,2,1,0:T(8,128)(2,1)} %get-tuple-element.48._.refs_1_.refs_0_), custom_call_target="tpu_custom_call" | custom-call | tf_op jit(solution)/shard_map/spread/pallas_call | solution.py:223
  13.4 0.4 collective-permute-done.1.refs_0_
  13.8 0.9 %collective-permute-done.3.refs_2_.refs_1_ = bf16[1,1,32,1024]{3,2,1,0:T(8,128)(2,1)S(1)} collective-permute-done((bf16[1,1,32,1024]{3,2,1,0:T(8,128)(2,1)}, bf16[1,1,32,1024]{3,2,1,0:T(8,128)(2,1)S(1)}, u32[]{:S(2)}, u32[]{:S(2)}) %collective-permute-start.3) | collective-permute-done | bytes 65568 | tf_op jit(solution)/shard_map/ppermute | solution.py:217
  14.7 0.6 both.1
  15.3 1.8 %collective-permute-start.4 = (bf16[4,1,32,1024]{3,2,1,0:T(8,128)(2,1)S(1)}, bf16[4,1,32,1024]{3,2,1,0:T(8,128)(2,1)S(1)}, u32[]{:S(2)}, u32[]{:S(2)}) collective-permute-start(bf16[4,1,32,1024]{3,2,1,0:T(8,128)(2,1)S(1)} %both.1), channel_id=1, source_target_pairs={{0,4},{2,6},{4,0},{6,2},{8,12},{10,14},{12,8},{14,10},{1,5},{3,7},... | collective-permute-start | bytes 786440 | tf_op jit(solution)/shard_map/ppermute | solution.py:217
  17.1 0.8 %collective-permute-start.2 = (bf16[2,128,512]{2,1,0:T(8,128)(2,1)S(1)}, bf16[2,128,512]{2,1,0:T(8,128)(2,1)S(1)}, u32[]{:S(2)}, u32[]{:S(2)}) collective-permute-start(bf16[2,128,512]{2,1,0:T(8,128)(2,1)S(1)} %constant_dynamic-update-slice_fusion), channel_id=1, source_target_pairs={{0,2},{2,0},{4,6},{6,4},{8,10},{10,8},{12,14},{14,12},{1,3},{3,1},... | collective-permute-start | bytes 786440 | tf_op jit(solution)/shard_map/ppermute | solution.py:217
  17.9 3.9 %all-to-all-start = ((bf16[8,512,128]{2,1,0:T(8,128)(2,1)}), bf16[8,512,128]{2,1,0:T(8,128)(2,1)S(1)}, u32[]{:S(2)}, u32[]{:S(2)}) async-start(bf16[8,512,128]{2,1,0:T(8,128)(2,1)} %bitcast.6), calls=%async_computation | async-start | bytes 2097152 | tf_op jit(solution)/shard_map/all_to_all | solution.py:330
  21.8 0.2 collective-permute-done.4.refs_1_.refs_2_
  22.0 6.7 %collective-permute-done.2 = bf16[2,128,512]{2,1,0:T(8,128)(2,1)S(1)} collective-permute-done((bf16[2,128,512]{2,1,0:T(8,128)(2,1)S(1)}, bf16[2,128,512]{2,1,0:T(8,128)(2,1)S(1)}, u32[]{:S(2)}, u32[]{:S(2)}) %collective-permute-start.2) | collective-permute-done | bytes 262176 | tf_op jit(solution)/shard_map/ppermute | solution.py:217
  28.8 1.6 %collective-permute-start.5 = (bf16[4,128,512]{2,1,0:T(8,128)(2,1)S(1)}, bf16[4,128,512]{2,1,0:T(8,128)(2,1)S(1)}, u32[]{:S(2)}, u32[]{:S(2)}) collective-permute-start(bf16[4,128,512]{2,1,0:T(8,128)(2,1)S(1)} %pad_maximum_fusion), channel_id=1, source_target_pairs={{0,16},{16,0},{1,17},{17,1},{2,18},{18,2},{3,19},{19,3},{4,20},{20... | collective-permute-start | bytes 1572872 | tf_op jit(solution)/shard_map/ppermute | solution.py:217
  30.4 7.6 %collective-permute-done.5 = bf16[4,128,512]{2,1,0:T(8,128)(2,1)S(1)} collective-permute-done((bf16[4,128,512]{2,1,0:T(8,128)(2,1)S(1)}, bf16[4,128,512]{2,1,0:T(8,128)(2,1)S(1)}, u32[]{:S(2)}, u32[]{:S(2)}) %collective-permute-start.5) | collective-permute-done | bytes 524320 | tf_op jit(solution)/shard_map/ppermute | solution.py:217
  38.1 0.1 collective-permute-start.6
  38.2 0.8 %pad_maximum_fusion.1 = bf16[4,1,32,1024]{3,2,1,0:T(8,128)(2,1)} fusion(bf16[2,1,32,1024]{3,2,1,0:T(8,128)(2,1)S(1)} %slice.3, bf16[1,1,32,1024]{3,2,1,0:T(8,128)(2,1)S(1)} %collective-permute-done.3.refs_2_.refs_1_, bf16[1,1,32,1024]{3,2,1,0:T(8,128)(2,1)S(1)} %copy-done.2), kind=kLoop, calls=%fused_computation.1 | loop fusion | flops 262144 | bytes 524288 | tf_op jit(solution)/shard_map/concatenate | solution.py:289
  38.9 2.6 %collective-permute-start.8 = (bf16[4,1,32,1024]{3,2,1,0:T(8,128)(2,1)}, bf16[4,1,32,1024]{3,2,1,0:T(8,128)(2,1)S(1)}, u32[]{:S(2)}, u32[]{:S(2)}) collective-permute-start(bf16[4,1,32,1024]{3,2,1,0:T(8,128)(2,1)} %pad_maximum_fusion.1), channel_id=1, source_target_pairs={{0,2},{2,0},{4,6},{6,4},{8,10},{10,8},{12,14},{14,12},{1,3},{3,1},... | collective-permute-start | bytes 786440 | tf_op jit(solution)/shard_map/ppermute | solution.py:217
  41.5 1.2 %pick.1 = bf16[1,1,32,1024]{3,2,1,0:T(8,128)(2,1)} custom-call(s32[8]{0:T(128)S(1)} %copy-done.4, bf16[2,64,1024]{2,1,0:T(8,128)(2,1)S(1)} %copy-done.1, bf16[4,1,32,1024]{3,2,1,0:T(8,128)(2,1)S(1)} %collective-permute-done.1.refs_0_, bf16[4,1,32,1024]{3,2,1,0:T(8,128)(2,1)S(1)} %collective-permute-done.4.refs_1_.refs_2_), custom_call_target="tpu_custom_call" | custom-call | tf_op jit(solution)/shard_map/pick/pallas_call | solution.py:223
  42.7 3.1 %collective-permute-start.7 = (bf16[1,1,32,1024]{3,2,1,0:T(8,128)(2,1)}, bf16[1,1,32,1024]{3,2,1,0:T(8,128)(2,1)}, u32[]{:S(2)}, u32[]{:S(2)}) collective-permute-start(bf16[1,1,32,1024]{3,2,1,0:T(8,128)(2,1)} %pick.1), channel_id=1, source_target_pairs={{0,8},{2,10},{4,12},{6,14},{8,0},{10,2},{12,4},{14,6},{1,9},{3,11}... | collective-permute-start | bytes 196616 | tf_op jit(solution)/shard_map/ppermute | solution.py:217
  45.8 2.1 %all-to-all-done.slices = bf16[8,512,128]{2,1,0:T(8,128)(2,1)S(1)} async-done(((bf16[8,512,128]{2,1,0:T(8,128)(2,1)}), bf16[8,512,128]{2,1,0:T(8,128)(2,1)S(1)}, u32[]{:S(2)}, u32[]{:S(2)}) %all-to-all-start) | async-done | bytes 1048608 | tf_op jit(solution)/shard_map/all_to_all | solution.py:330
  47.9 3.3 %frozen.1 = bf16[8,128,512]{2,1,0:T(8,128)(2,1)} custom-call(bf16[8,128,512]{2,1,0:T(8,128)(2,1)S(1)} %constant_dynamic-update-slice_fusion.2.mine, bf16[8,128,512]{2,1,0:T(8,128)(2,1)} %collective-permute-done.6.other, bf16[8,512,128]{2,1,0:T(8,128)(2,1)S(1)} %all-to-all-done.slices), custom_call_target="tpu_custom_call" | custom-call | tf_op jit(solution)/shard_map/frozen/pallas_call | solution.py:223
  51.3 4.1 %all-to-all-start.1 = ((bf16[8,128,512]{2,1,0:T(8,128)(2,1)}), bf16[8,128,512]{2,1,0:T(8,128)(2,1)S(1)}, u32[]{:S(2)}, u32[]{:S(2)}) async-start(bf16[8,128,512]{2,1,0:T(8,128)(2,1)} %frozen.1), calls=%async_computation.1 | async-start | bytes 2097152 | tf_op jit(solution)/shard_map/all_to_all | solution.py:349
  55.4 0.8 %gradient.1 = bf16[2,32,1024]{2,1,0:T(8,128)(2,1)S(1)} custom-call(s32[8]{0:T(128)S(1)} %copy-done.4, bf16[1,1,32,1024]{3,2,1,0:T(8,128)(2,1)S(1)} %copy-done.2, bf16[1,1,32,1024]{3,2,1,0:T(8,128)(2,1)S(1)} %collective-permute-done.3.refs_2_.refs_1_, bf16[4,1,32,1024]{3,2,1,0:T(8,128)(2,1)S(1)} %collective-permute-done.4.refs_1_.refs_2_, ...), custom_call_target="tpu_custom_call" | custom-call | tf_op jit(solution)/shard_map/gradient/pallas_call | solution.py:223
  56.2 2.0 %all_gather.7 = bf16[2,64,1024]{2,1,0:T(8,128)(2,1)S(1)} all-gather(bf16[2,32,1024]{2,1,0:T(8,128)(2,1)S(1)} %gradient.1), channel_id=1, replica_groups=mesh['groups'=2,'dp'=8,'mp'=2] {'mp'}, dimensions={1}, use_global_device_ids=true | all-gather | bytes 393216 | tf_op jit(solution)/shard_map/all_gather | solution.py:367
  58.2 1.0 %back.1 = bf16[32,128]{1,0:T(8,128)(2,1)S(1)} custom-call(s32[8]{0:T(128)S(1)} %copy-done.4, bf16[2,64,1024]{2,1,0:T(8,128)(2,1)S(1)} %copy-done.1, bf16[128,1024]{1,0:T(8,128)(2,1)S(1)} %copy-done.3, bf16[4,1,32,1024]{3,2,1,0:T(8,128)(2,1)S(1)} %collective-permute-done.1.refs_0_, bf16[4,1,32,1024]{3,2,1,0:T(8,128)(2,1)S(1)} %collective-permute-done.4.refs_1_.refs_2_, ...), custom_call_target="tpu_custom_call" | custom-call | tf_op jit(solution)/shard_map/back/pallas_call | solution.py:223
  59.2 1.8 %all_gather.6.back = bf16[64,128]{1,0:T(8,128)(2,1)S(1)} all-gather(bf16[32,128]{1,0:T(8,128)(2,1)S(1)} %back.1), channel_id=1, replica_groups=mesh['groups'=2,'dp'=8,'mp'=2] {'mp'}, dimensions={0}, use_global_device_ids=true | all-gather | bytes 24576 | tf_op jit(solution)/shard_map/all_gather | solution.py:361
  61.0 9.0 %all-to-all-done.1.frozen = bf16[8,128,512]{2,1,0:T(8,128)(2,1)S(1)} async-done(((bf16[8,128,512]{2,1,0:T(8,128)(2,1)}), bf16[8,128,512]{2,1,0:T(8,128)(2,1)S(1)}, u32[]{:S(2)}, u32[]{:S(2)}) %all-to-all-start.1) | async-done | bytes 1048608 | tf_op jit(solution)/shard_map/all_to_all | solution.py:349
  70.0 1.3 %last.1 = bf16[128,4096]{1,0:T(8,128)(2,1)} custom-call(bf16[8,128,512]{2,1,0:T(8,128)(2,1)S(1)} %all-to-all-done.1.frozen, bf16[64,128]{1,0:T(8,128)(2,1)S(1)} %all_gather.6.back, bf16[64,8192]{1,0:T(8,128)(2,1)S(1)} %bitcast.5), custom_call_target="tpu_custom_call" | custom-call | tf_op jit(solution)/shard_map/last/pallas_call | solution.py:223
  71.3 0.7 copy.13
  (21 shorter events, 0.2 us)
Async XLA Ops:
  4.2 9.6 %copy-start.5 = (bf16[128,512]{1,0:T(8,128)(2,1)S(1)}, bf16[128,512]{1,0:T(8,128)(2,1)}, u32[]{:S(2)}) copy-start(bf16[128,512]{1,0:T(8,128)(2,1)} %get-tuple-element.27) | copy-start | bytes 393220
  4.3 10.4 %copy-start.1 = (bf16[2,64,1024]{2,1,0:T(8,128)(2,1)S(1)}, bf16[2,64,1024]{2,1,0:T(8,128)(2,1)}, u32[]{:S(2)}) copy-start(bf16[2,64,1024]{2,1,0:T(8,128)(2,1)} %up.7) | copy-start | bytes 786436
  4.3 10.4 %copy-start.2 = (bf16[1,1,32,1024]{3,2,1,0:T(8,128)(2,1)S(1)}, bf16[1,1,32,1024]{3,2,1,0:T(8,128)(2,1)}, u32[]{:S(2)}) copy-start(bf16[1,1,32,1024]{3,2,1,0:T(8,128)(2,1)} %get-tuple-element.48._.refs_1_.refs_0_) | copy-start | bytes 196612
  4.3 10.4 %copy-start.4 = (s32[8]{0:T(128)S(1)}, s32[8]{0:T(128)}, u32[]{:S(2)}) copy-start(s32[8]{0:T(128)} %tenants.9) | copy-start | bytes 100
  4.3 9.5 %collective-permute-start.1 = (bf16[4,1,32,1024]{3,2,1,0:T(8,128)(2,1)}, bf16[4,1,32,1024]{3,2,1,0:T(8,128)(2,1)S(1)}, u32[]{:S(2)}, u32[]{:S(2)}) collective-permute-start(bf16[4,1,32,1024]{3,2,1,0:T(8,128)(2,1)} %get-tuple-element.28), channel_id=1, source_target_pairs={{0,2},{2,0},{4,6},{6,4},{8,10},{10,8},{12,14},{14,12},{1,3},{3,1},... | collective-permute-start | bytes 786440 | tf_op jit(solution)/shard_map/ppermute | solution.py:217
  7.3 6.1 %collective-permute-start = (bf16[1,128,512]{2,1,0:T(8,128)(2,1)}, bf16[1,128,512]{2,1,0:T(8,128)(2,1)S(1)}, u32[]{:S(2)}, u32[]{:S(2)}) collective-permute-start(bf16[1,128,512]{2,1,0:T(8,128)(2,1)} %bitcast.7), channel_id=1, source_target_pairs={{0,4},{2,6},{4,0},{6,2},{8,12},{10,14},{12,8},{14,10},{1,5},{3,7},... | collective-permute-start | bytes 393224 | tf_op jit(solution)/shard_map/ppermute | solution.py:217
  8.9 5.8 %collective-permute-start.3 = (bf16[1,1,32,1024]{3,2,1,0:T(8,128)(2,1)}, bf16[1,1,32,1024]{3,2,1,0:T(8,128)(2,1)S(1)}, u32[]{:S(2)}, u32[]{:S(2)}) collective-permute-start(bf16[1,1,32,1024]{3,2,1,0:T(8,128)(2,1)} %get-tuple-element.48._.refs_1_.refs_0_), channel_id=1, source_target_pairs={{0,8},{2,10},{4,12},{6,14},{8,0},{10,2},{12,4},{14,6},{1,9},{3,11}... | collective-permute-start | bytes 196616 | tf_op jit(solution)/shard_map/ppermute | solution.py:217
  15.3 6.7 %collective-permute-start.4 = (bf16[4,1,32,1024]{3,2,1,0:T(8,128)(2,1)S(1)}, bf16[4,1,32,1024]{3,2,1,0:T(8,128)(2,1)S(1)}, u32[]{:S(2)}, u32[]{:S(2)}) collective-permute-start(bf16[4,1,32,1024]{3,2,1,0:T(8,128)(2,1)S(1)} %both.1), channel_id=1, source_target_pairs={{0,4},{2,6},{4,0},{6,2},{8,12},{10,14},{12,8},{14,10},{1,5},{3,7},... | collective-permute-start | bytes 786440 | tf_op jit(solution)/shard_map/ppermute | solution.py:217
  17.1 11.6 %collective-permute-start.2 = (bf16[2,128,512]{2,1,0:T(8,128)(2,1)S(1)}, bf16[2,128,512]{2,1,0:T(8,128)(2,1)S(1)}, u32[]{:S(2)}, u32[]{:S(2)}) collective-permute-start(bf16[2,128,512]{2,1,0:T(8,128)(2,1)S(1)} %constant_dynamic-update-slice_fusion), channel_id=1, source_target_pairs={{0,2},{2,0},{4,6},{6,4},{8,10},{10,8},{12,14},{14,12},{1,3},{3,1},... | collective-permute-start | bytes 786440 | tf_op jit(solution)/shard_map/ppermute | solution.py:217
  17.9 30.0 %all-to-all-start = ((bf16[8,512,128]{2,1,0:T(8,128)(2,1)}), bf16[8,512,128]{2,1,0:T(8,128)(2,1)S(1)}, u32[]{:S(2)}, u32[]{:S(2)}) async-start(bf16[8,512,128]{2,1,0:T(8,128)(2,1)} %bitcast.6), calls=%async_computation | async-start | bytes 2097152 | tf_op jit(solution)/shard_map/all_to_all | solution.py:330
  28.8 9.2 %collective-permute-start.5 = (bf16[4,128,512]{2,1,0:T(8,128)(2,1)S(1)}, bf16[4,128,512]{2,1,0:T(8,128)(2,1)S(1)}, u32[]{:S(2)}, u32[]{:S(2)}) collective-permute-start(bf16[4,128,512]{2,1,0:T(8,128)(2,1)S(1)} %pad_maximum_fusion), channel_id=1, source_target_pairs={{0,16},{16,0},{1,17},{17,1},{2,18},{18,2},{3,19},{19,3},{4,20},{20... | collective-permute-start | bytes 1572872 | tf_op jit(solution)/shard_map/ppermute | solution.py:217
  38.1 9.9 %collective-permute-start.6 = (bf16[8,128,512]{2,1,0:T(8,128)(2,1)S(1)}, bf16[8,128,512]{2,1,0:T(8,128)(2,1)}, u32[]{:S(2)}, u32[]{:S(2)}) collective-permute-start(bf16[8,128,512]{2,1,0:T(8,128)(2,1)S(1)} %constant_dynamic-update-slice_fusion.2.mine), channel_id=1, source_target_pairs={{0,1},{1,0},{2,3},{3,2},{4,5},{5,4},{6,7},{7,6},{8,9},{9,8},{10,11... | collective-permute-start | bytes 3145736 | tf_op jit(solution)/shard_map/ppermute | solution.py:217
  38.9 12.4 %collective-permute-start.8 = (bf16[4,1,32,1024]{3,2,1,0:T(8,128)(2,1)}, bf16[4,1,32,1024]{3,2,1,0:T(8,128)(2,1)S(1)}, u32[]{:S(2)}, u32[]{:S(2)}) collective-permute-start(bf16[4,1,32,1024]{3,2,1,0:T(8,128)(2,1)} %pad_maximum_fusion.1), channel_id=1, source_target_pairs={{0,2},{2,0},{4,6},{6,4},{8,10},{10,8},{12,14},{14,12},{1,3},{3,1},... | collective-permute-start | bytes 786440 | tf_op jit(solution)/shard_map/ppermute | solution.py:217
  42.7 8.6 %collective-permute-start.7 = (bf16[1,1,32,1024]{3,2,1,0:T(8,128)(2,1)}, bf16[1,1,32,1024]{3,2,1,0:T(8,128)(2,1)}, u32[]{:S(2)}, u32[]{:S(2)}) collective-permute-start(bf16[1,1,32,1024]{3,2,1,0:T(8,128)(2,1)} %pick.1), channel_id=1, source_target_pairs={{0,8},{2,10},{4,12},{6,14},{8,0},{10,2},{12,4},{14,6},{1,9},{3,11}... | collective-permute-start | bytes 196616 | tf_op jit(solution)/shard_map/ppermute | solution.py:217
  51.2 6.9 %copy-start.3 = (bf16[128,1024]{1,0:T(8,128)(2,1)S(1)}, bf16[128,1024]{1,0:T(8,128)(2,1)}, u32[]{:S(2)}) copy-start(bf16[128,1024]{1,0:T(8,128)(2,1)} %get-tuple-element.44.weighted) | copy-start | bytes 786436
  51.3 18.8 %copy-start = (bf16[8192,64]{0,1:T(8,128)(2,1)S(1)}, bf16[8192,64]{0,1:T(8,128)(2,1)}, u32[]{:S(2)}) copy-start(bf16[8192,64]{0,1:T(8,128)(2,1)} %param.12) | copy-start | bytes 3145732
  51.3 18.7 %all-to-all-start.1 = ((bf16[8,128,512]{2,1,0:T(8,128)(2,1)}), bf16[8,128,512]{2,1,0:T(8,128)(2,1)S(1)}, u32[]{:S(2)}, u32[]{:S(2)}) async-start(bf16[8,128,512]{2,1,0:T(8,128)(2,1)} %frozen.1), calls=%async_computation.1 | async-start | bytes 2097152 | tf_op jit(solution)/shard_map/all_to_all | solution.py:349

commit v5 on v4

--- a/solution.py
+++ b/solution.py
@@ -169,10 +169,18 @@
         store.wait()
 
 
-def last_kernel(frozen, back, down, out, held, sem):
+def last_kernel(frozen, mine, other, down, gradient, other_gradient, out, whole, back, held, sem, gradient_sem):
     team, rows, features = frozen.shape
+    part_rank, _ = mine.shape
     _, _, m = place()
-    stores = []
+    stores = [
+        pltpu.make_async_copy(gradient, whole.at[:, piece(m, part_rank)], gradient_sem.at[0]),
+        pltpu.make_async_copy(other_gradient, whole.at[:, piece(1 - m, part_rank)], gradient_sem.at[1]),
+    ]
+    for store in stores:
+        store.start()
+    back[piece(m, part_rank)] = mine[...]
+    back[piece(1 - m, part_rank)] = other[...]
     for k in range(team):
         at = pl.ds(pl.multiple_of(m * (team * features) + k * features, features), features)
         adapter = lax.dot_general(back[...], down[:, at], (((0,), (0,)), ((), ())), preferred_element_type=f32)
@@ -358,18 +366,20 @@
         tenant_of_block, adapter_up_factor, weighted, *got,
     )
 
-    back_rank = lax.all_gather(back_part, "mp", axis=0, tiled=True)
-
     grad_part = call(
         functools.partial(gradient_kernel, orders, adapter_scale / block_rows), "gradient",
         shape(tenants_here, part_rank, out_width), [SMEM] + [VMEM] * len(pieces), tenant_of_block, *pieces,
     )
-    up_factor_gradient = lax.all_gather(grad_part, "mp", axis=1, tiled=True)
-
-    input_gradient = call(
-        last_kernel, "last", shape(rows, half_width), [VMEM, VMEM, VMEM],
-        frozen_mine, back_rank, common_down_factor.T, out_specs=HBM,
-        scratch=[pltpu.VMEM((team, rows, features), bf16), pltpu.SemaphoreType.DMA((team,))],
+    input_gradient, up_factor_gradient = call(
+        last_kernel, "last", [shape(rows, half_width), shape(*adapter_up_factor.shape)], [VMEM] * 6,
+        frozen_mine, back_part, swap(back_part, "mp", 1), common_down_factor.T, grad_part, swap(grad_part, "mp", 1),
+        out_specs=[HBM, HBM],
+        scratch=[
+            pltpu.VMEM((rank, rows), bf16),
+            pltpu.VMEM((team, rows, features), bf16),
+            pltpu.SemaphoreType.DMA((team,)),
+            pltpu.SemaphoreType.DMA((2,)),
+        ],
     )
     return (input_gradient, up_factor_gradient)
 

time: 72.4 us -> 71.8 us (level)
  waiting for transfers between devices: 26.9 us -> 30.9 us
  blocking collectives: 3.83 us -> 0 us
    all_gather x2 -> x0, blocking collectives: 3.83 us -> none  [the longest x1 1.99 us: local(): up_factor_gradient = lax.all_gather(grad_part, 'mp', axis=1, tiled=True)]
    all_to_all x1, waiting for transfers between devices: 9.02 us -> 11.3 us  [local(): lax.all_to_all(frozen, ALL, split_axis=0, concat_axis=0, tiled=True, axis...]
    all_to_all x1, waiting for transfers between devices: 2.14 us -> 3 us  [local(): lax.all_to_all(to_send.reshape(dp_count, features, cols), 'dp', split_axi...]
    ppermute x9 -> x11, waiting for transfers between devices: 15.8 us -> 16.6 us  [swap(): return lax.ppermute(value, axis, [(k, k ^ bit) for k in range(size)])]
    ppermute x9 -> x11, starting transfers between devices: 17.1 us -> 17.8 us  [swap(): return lax.ppermute(value, axis, [(k, k ^ bit) for k in range(size)])]
  transfers between devices with their start and end apart: 11 -> 13, of which waited for: 7 -> 8; matrix products, arithmetic and copies ran while one was open for 1% -> 1% of each run, Pallas kernels for 11% -> 11%
where the time goes in v5:
time: 71.8 us; the launch traced here: 71.5 us
  waiting for transfers between devices  30.9 us (43%)
  starting transfers between devices  25.5 us (36%)
  Pallas kernels  13.3 us (19%)
  between operations  0.81 us (1%)
  other arithmetic  0.78 us (1%)
    ppermute x11, starting transfers between devices, swap(): return lax.ppermute(value, axis, [(k, k ^ bit) for k in range(size)])  17.8 us
    ppermute x11, waiting for transfers between devices, swap(): return lax.ppermute(value, axis, [(k, k ^ bit) for k in range(size)])  16.6 us
    pallas_call x8, Pallas kernels, call(): pl.pallas_call(kernel, in_specs=in_specs, out_specs=out_specs, out_shape=...  13.3 us
    all_to_all x1, waiting for transfers between devices, local(): lax.all_to_all(frozen, ALL, split_axis=0, concat_axis=0, tiled=True, axis...  11.3 us
    all_to_all x1, starting transfers between devices, local(): lax.all_to_all(to_send.reshape(dp_count, features, cols), 'dp', split_axi...  3.89 us
    all_to_all x1, starting transfers between devices, local(): lax.all_to_all(frozen, ALL, split_axis=0, concat_axis=0, tiled=True, axis...  3.79 us
    all_to_all x1, waiting for transfers between devices, local(): lax.all_to_all(to_send.reshape(dp_count, features, cols), 'dp', split_axi...  3 us
  transfers between devices with their start and end apart: 13, of which 8 were waited for; matrix products, arithmetic and copies ran while one was open for 1% of the time, Pallas kernels for 11%

profile of v5, /device:TPU:0, one launch (start us, length us, event | category | flops | bytes accessed | tf_op | source)
XLA Modules:
  0.0 71.5 jit_solution(10006305314065198445)
XLA Ops:
  0.6 3.6 %prepare.1 = (bf16[128,1024]{1,0:T(8,128)(2,1)}, bf16[128,512]{1,0:T(8,128)(2,1)}, bf16[4,1,32,1024]{3,2,1,0:T(8,128)(2,1)}, bf16[1,1,32,1024]{3,2,1,0:T(8,128)(2,1)}) custom-call(s32[1,128]{1,0:T(1,128)} %bitcast.9, bf16[128,1024]{1,0:T(8,128)(2,1)} %upstream.1, s32[8]{0:T(128)} %tenants.9, bf16[2,64,1024]{2,1,0:T(8,128)(2,1)} %up.7, ...), custom_call_target="tpu_custom_call" | custom-call | tf_op jit(solution)/shard_map/prepare/pallas_call | solution.py:231
  4.2 0.0 copy-start.1
  4.3 3.0 %collective-permute-start.1 = (bf16[4,1,32,1024]{3,2,1,0:T(8,128)(2,1)}, bf16[4,1,32,1024]{3,2,1,0:T(8,128)(2,1)S(1)}, u32[]{:S(2)}, u32[]{:S(2)}) collective-permute-start(bf16[4,1,32,1024]{3,2,1,0:T(8,128)(2,1)} %get-tuple-element.28), channel_id=1, source_target_pairs={{0,2},{2,0},{4,6},{6,4},{8,10},{10,8},{12,14},{14,12},{1,3},{3,1},... | collective-permute-start | bytes 786440 | tf_op jit(solution)/shard_map/ppermute | solution.py:225
  7.3 1.6 %collective-permute-start = (bf16[1,128,512]{2,1,0:T(8,128)(2,1)}, bf16[1,128,512]{2,1,0:T(8,128)(2,1)S(1)}, u32[]{:S(2)}, u32[]{:S(2)}) collective-permute-start(bf16[1,128,512]{2,1,0:T(8,128)(2,1)} %bitcast.7), channel_id=1, source_target_pairs={{0,4},{2,6},{4,0},{6,2},{8,12},{10,14},{12,8},{14,10},{1,5},{3,7},... | collective-permute-start | bytes 393224 | tf_op jit(solution)/shard_map/ppermute | solution.py:225
  8.9 2.6 %collective-permute-start.3 = (bf16[1,1,32,1024]{3,2,1,0:T(8,128)(2,1)}, bf16[1,1,32,1024]{3,2,1,0:T(8,128)(2,1)S(1)}, u32[]{:S(2)}, u32[]{:S(2)}) collective-permute-start(bf16[1,1,32,1024]{3,2,1,0:T(8,128)(2,1)} %get-tuple-element.48._.refs_1_.refs_0_), channel_id=1, source_target_pairs={{0,8},{2,10},{4,12},{6,14},{8,0},{10,2},{12,4},{14,6},{1,9},{3,11}... | collective-permute-start | bytes 196616 | tf_op jit(solution)/shard_map/ppermute | solution.py:225
  11.5 2.0 %spread.1 = bf16[2,2048,128]{2,1,0:T(8,128)(2,1)} custom-call(bf16[4096,128]{1,0:T(8,128)(2,1)} %weight.1, bf16[1,1,32,1024]{3,2,1,0:T(8,128)(2,1)} %get-tuple-element.48._.refs_1_.refs_0_), custom_call_target="tpu_custom_call" | custom-call | tf_op jit(solution)/shard_map/spread/pallas_call | solution.py:231
  13.4 0.4 collective-permute-done.1.refs_0_
  13.8 0.9 %collective-permute-done.3.refs_2_.refs_1_ = bf16[1,1,32,1024]{3,2,1,0:T(8,128)(2,1)S(1)} collective-permute-done((bf16[1,1,32,1024]{3,2,1,0:T(8,128)(2,1)}, bf16[1,1,32,1024]{3,2,1,0:T(8,128)(2,1)S(1)}, u32[]{:S(2)}, u32[]{:S(2)}) %collective-permute-start.3) | collective-permute-done | bytes 65568 | tf_op jit(solution)/shard_map/ppermute | solution.py:225
  14.7 0.6 both.1
  15.3 1.8 %collective-permute-start.4 = (bf16[4,1,32,1024]{3,2,1,0:T(8,128)(2,1)S(1)}, bf16[4,1,32,1024]{3,2,1,0:T(8,128)(2,1)S(1)}, u32[]{:S(2)}, u32[]{:S(2)}) collective-permute-start(bf16[4,1,32,1024]{3,2,1,0:T(8,128)(2,1)S(1)} %both.1), channel_id=1, source_target_pairs={{0,4},{2,6},{4,0},{6,2},{8,12},{10,14},{12,8},{14,10},{1,5},{3,7},... | collective-permute-start | bytes 786440 | tf_op jit(solution)/shard_map/ppermute | solution.py:225
  17.1 0.8 %collective-permute-start.2 = (bf16[2,128,512]{2,1,0:T(8,128)(2,1)S(1)}, bf16[2,128,512]{2,1,0:T(8,128)(2,1)S(1)}, u32[]{:S(2)}, u32[]{:S(2)}) collective-permute-start(bf16[2,128,512]{2,1,0:T(8,128)(2,1)S(1)} %constant_dynamic-update-slice_fusion), channel_id=1, source_target_pairs={{0,2},{2,0},{4,6},{6,4},{8,10},{10,8},{12,14},{14,12},{1,3},{3,1},... | collective-permute-start | bytes 786440 | tf_op jit(solution)/shard_map/ppermute | solution.py:225
  17.9 3.9 %all-to-all-start = ((bf16[8,512,128]{2,1,0:T(8,128)(2,1)}), bf16[8,512,128]{2,1,0:T(8,128)(2,1)S(1)}, u32[]{:S(2)}, u32[]{:S(2)}) async-start(bf16[8,512,128]{2,1,0:T(8,128)(2,1)} %bitcast.6), calls=%async_computation | async-start | bytes 2097152 | tf_op jit(solution)/shard_map/all_to_all | solution.py:338
  21.8 0.2 collective-permute-done.4.refs_1_.refs_2_
  22.0 6.7 %collective-permute-done.2 = bf16[2,128,512]{2,1,0:T(8,128)(2,1)S(1)} collective-permute-done((bf16[2,128,512]{2,1,0:T(8,128)(2,1)S(1)}, bf16[2,128,512]{2,1,0:T(8,128)(2,1)S(1)}, u32[]{:S(2)}, u32[]{:S(2)}) %collective-permute-start.2) | collective-permute-done | bytes 262176 | tf_op jit(solution)/shard_map/ppermute | solution.py:225
  28.8 1.6 %collective-permute-start.5 = (bf16[4,128,512]{2,1,0:T(8,128)(2,1)S(1)}, bf16[4,128,512]{2,1,0:T(8,128)(2,1)S(1)}, u32[]{:S(2)}, u32[]{:S(2)}) collective-permute-start(bf16[4,128,512]{2,1,0:T(8,128)(2,1)S(1)} %pad_maximum_fusion), channel_id=1, source_target_pairs={{0,16},{16,0},{1,17},{17,1},{2,18},{18,2},{3,19},{19,3},{4,20},{20... | collective-permute-start | bytes 1572872 | tf_op jit(solution)/shard_map/ppermute | solution.py:225
  30.4 7.6 %collective-permute-done.5 = bf16[4,128,512]{2,1,0:T(8,128)(2,1)S(1)} collective-permute-done((bf16[4,128,512]{2,1,0:T(8,128)(2,1)S(1)}, bf16[4,128,512]{2,1,0:T(8,128)(2,1)S(1)}, u32[]{:S(2)}, u32[]{:S(2)}) %collective-permute-start.5) | collective-permute-done | bytes 524320 | tf_op jit(solution)/shard_map/ppermute | solution.py:225
  38.1 0.1 collective-permute-start.6
  38.2 0.7 %pad_maximum_fusion.1 = bf16[4,1,32,1024]{3,2,1,0:T(8,128)(2,1)} fusion(bf16[2,1,32,1024]{3,2,1,0:T(8,128)(2,1)S(1)} %slice.3, bf16[1,1,32,1024]{3,2,1,0:T(8,128)(2,1)S(1)} %collective-permute-done.3.refs_2_.refs_1_, bf16[1,1,32,1024]{3,2,1,0:T(8,128)(2,1)S(1)} %copy-done.2), kind=kLoop, calls=%fused_computation.1 | loop fusion | flops 262144 | bytes 524288 | tf_op jit(solution)/shard_map/concatenate | solution.py:297
  38.9 2.6 %collective-permute-start.8 = (bf16[4,1,32,1024]{3,2,1,0:T(8,128)(2,1)}, bf16[4,1,32,1024]{3,2,1,0:T(8,128)(2,1)}, u32[]{:S(2)}, u32[]{:S(2)}) collective-permute-start(bf16[4,1,32,1024]{3,2,1,0:T(8,128)(2,1)} %pad_maximum_fusion.1), channel_id=1, source_target_pairs={{0,2},{2,0},{4,6},{6,4},{8,10},{10,8},{12,14},{14,12},{1,3},{3,1},... | collective-permute-start | bytes 786440 | tf_op jit(solution)/shard_map/ppermute | solution.py:225
  41.5 0.6 pick.1
  42.1 3.1 %collective-permute-start.7 = (bf16[1,1,32,1024]{3,2,1,0:T(8,128)(2,1)S(1)}, bf16[1,1,32,1024]{3,2,1,0:T(8,128)(2,1)S(1)}, u32[]{:S(2)}, u32[]{:S(2)}) collective-permute-start(bf16[1,1,32,1024]{3,2,1,0:T(8,128)(2,1)S(1)} %pick.1), channel_id=1, source_target_pairs={{0,8},{2,10},{4,12},{6,14},{8,0},{10,2},{12,4},{14,6},{1,9},{3,11}... | collective-permute-start | bytes 196616 | tf_op jit(solution)/shard_map/ppermute | solution.py:225
  45.2 3.0 %all-to-all-done.slices = bf16[8,512,128]{2,1,0:T(8,128)(2,1)S(1)} async-done(((bf16[8,512,128]{2,1,0:T(8,128)(2,1)}), bf16[8,512,128]{2,1,0:T(8,128)(2,1)S(1)}, u32[]{:S(2)}, u32[]{:S(2)}) %all-to-all-start) | async-done | bytes 1048608 | tf_op jit(solution)/shard_map/all_to_all | solution.py:338
  48.2 3.4 %frozen.1 = bf16[8,128,512]{2,1,0:T(8,128)(2,1)} custom-call(bf16[8,128,512]{2,1,0:T(8,128)(2,1)S(1)} %constant_dynamic-update-slice_fusion.2.mine, bf16[8,128,512]{2,1,0:T(8,128)(2,1)} %collective-permute-done.6.other, bf16[8,512,128]{2,1,0:T(8,128)(2,1)S(1)} %all-to-all-done.slices), custom_call_target="tpu_custom_call" | custom-call | tf_op jit(solution)/shard_map/frozen/pallas_call | solution.py:231
  51.6 0.0 copy-start.3
  51.6 3.8 %all-to-all-start.1 = ((bf16[8,128,512]{2,1,0:T(8,128)(2,1)}), bf16[8,128,512]{2,1,0:T(8,128)(2,1)S(1)}, u32[]{:S(2)}, u32[]{:S(2)}) async-start(bf16[8,128,512]{2,1,0:T(8,128)(2,1)} %frozen.1), calls=%async_computation.1 | async-start | bytes 2097152 | tf_op jit(solution)/shard_map/all_to_all | solution.py:357
  55.4 1.2 %gradient.1 = bf16[2,32,1024]{2,1,0:T(8,128)(2,1)S(1)} custom-call(s32[8]{0:T(128)S(1)} %copy-done.4, bf16[1,1,32,1024]{3,2,1,0:T(8,128)(2,1)S(1)} %copy-done.2, bf16[1,1,32,1024]{3,2,1,0:T(8,128)(2,1)S(1)} %collective-permute-done.3.refs_2_.refs_1_, bf16[4,1,32,1024]{3,2,1,0:T(8,128)(2,1)S(1)} %collective-permute-done.4.refs_1_.refs_2_, ...), custom_call_target="tpu_custom_call" | custom-call | tf_op jit(solution)/shard_map/gradient/pallas_call | solution.py:231
  56.6 0.1 collective-permute-start.10
  56.7 0.7 back.1.mine
  57.4 0.5 collective-permute-start.9
  58.0 0.8 %collective-permute-done.9.other = bf16[32,128]{1,0:T(8,128)(2,1)S(1)} collective-permute-done((bf16[32,128]{1,0:T(8,128)(2,1)S(1)}, bf16[32,128]{1,0:T(8,128)(2,1)S(1)}, u32[]{:S(2)}, u32[]{:S(2)}) %collective-permute-start.9) | collective-permute-done | bytes 8224 | tf_op jit(solution)/shard_map/ppermute | solution.py:225
  58.8 11.3 %all-to-all-done.1.frozen = bf16[8,128,512]{2,1,0:T(8,128)(2,1)S(1)} async-done(((bf16[8,128,512]{2,1,0:T(8,128)(2,1)}), bf16[8,128,512]{2,1,0:T(8,128)(2,1)S(1)}, u32[]{:S(2)}, u32[]{:S(2)}) %all-to-all-start.1) | async-done | bytes 1048608 | tf_op jit(solution)/shard_map/all_to_all | solution.py:357
  70.1 1.4 %last.1 = (bf16[128,4096]{1,0:T(8,128)(2,1)}, bf16[2,64,1024]{2,1,0:T(8,128)(2,1)}) custom-call(bf16[8,128,512]{2,1,0:T(8,128)(2,1)S(1)} %all-to-all-done.1.frozen, bf16[32,128]{1,0:T(8,128)(2,1)S(1)} %back.1.mine, bf16[32,128]{1,0:T(8,128)(2,1)S(1)} %collective-permute-done.9.other, bf16[64,8192]{1,0:T(8,128)(2,1)S(1)} %bitcast.5, ...), custom_call_target="tpu_custom_call" | custom-call | tf_op jit(solution)/shard_map/last/pallas_call | solution.py:231
  (22 shorter events, 0.2 us)
Async XLA Ops:
  4.2 9.6 %copy-start.5 = (bf16[128,512]{1,0:T(8,128)(2,1)S(1)}, bf16[128,512]{1,0:T(8,128)(2,1)}, u32[]{:S(2)}) copy-start(bf16[128,512]{1,0:T(8,128)(2,1)} %get-tuple-element.27) | copy-start | bytes 393220
  4.2 10.4 %copy-start.1 = (bf16[2,64,1024]{2,1,0:T(8,128)(2,1)S(1)}, bf16[2,64,1024]{2,1,0:T(8,128)(2,1)}, u32[]{:S(2)}) copy-start(bf16[2,64,1024]{2,1,0:T(8,128)(2,1)} %up.7) | copy-start | bytes 786436
  4.3 10.4 %copy-start.2 = (bf16[1,1,32,1024]{3,2,1,0:T(8,128)(2,1)S(1)}, bf16[1,1,32,1024]{3,2,1,0:T(8,128)(2,1)}, u32[]{:S(2)}) copy-start(bf16[1,1,32,1024]{3,2,1,0:T(8,128)(2,1)} %get-tuple-element.48._.refs_1_.refs_0_) | copy-start | bytes 196612
  4.3 10.4 %copy-start.4 = (s32[8]{0:T(128)S(1)}, s32[8]{0:T(128)}, u32[]{:S(2)}) copy-start(s32[8]{0:T(128)} %tenants.9) | copy-start | bytes 100
  4.3 9.5 %collective-permute-start.1 = (bf16[4,1,32,1024]{3,2,1,0:T(8,128)(2,1)}, bf16[4,1,32,1024]{3,2,1,0:T(8,128)(2,1)S(1)}, u32[]{:S(2)}, u32[]{:S(2)}) collective-permute-start(bf16[4,1,32,1024]{3,2,1,0:T(8,128)(2,1)} %get-tuple-element.28), channel_id=1, source_target_pairs={{0,2},{2,0},{4,6},{6,4},{8,10},{10,8},{12,14},{14,12},{1,3},{3,1},... | collective-permute-start | bytes 786440 | tf_op jit(solution)/shard_map/ppermute | solution.py:225
  7.3 6.1 %collective-permute-start = (bf16[1,128,512]{2,1,0:T(8,128)(2,1)}, bf16[1,128,512]{2,1,0:T(8,128)(2,1)S(1)}, u32[]{:S(2)}, u32[]{:S(2)}) collective-permute-start(bf16[1,128,512]{2,1,0:T(8,128)(2,1)} %bitcast.7), channel_id=1, source_target_pairs={{0,4},{2,6},{4,0},{6,2},{8,12},{10,14},{12,8},{14,10},{1,5},{3,7},... | collective-permute-start | bytes 393224 | tf_op jit(solution)/shard_map/ppermute | solution.py:225
  8.9 5.8 %collective-permute-start.3 = (bf16[1,1,32,1024]{3,2,1,0:T(8,128)(2,1)}, bf16[1,1,32,1024]{3,2,1,0:T(8,128)(2,1)S(1)}, u32[]{:S(2)}, u32[]{:S(2)}) collective-permute-start(bf16[1,1,32,1024]{3,2,1,0:T(8,128)(2,1)} %get-tuple-element.48._.refs_1_.refs_0_), channel_id=1, source_target_pairs={{0,8},{2,10},{4,12},{6,14},{8,0},{10,2},{12,4},{14,6},{1,9},{3,11}... | collective-permute-start | bytes 196616 | tf_op jit(solution)/shard_map/ppermute | solution.py:225
  15.3 6.7 %collective-permute-start.4 = (bf16[4,1,32,1024]{3,2,1,0:T(8,128)(2,1)S(1)}, bf16[4,1,32,1024]{3,2,1,0:T(8,128)(2,1)S(1)}, u32[]{:S(2)}, u32[]{:S(2)}) collective-permute-start(bf16[4,1,32,1024]{3,2,1,0:T(8,128)(2,1)S(1)} %both.1), channel_id=1, source_target_pairs={{0,4},{2,6},{4,0},{6,2},{8,12},{10,14},{12,8},{14,10},{1,5},{3,7},... | collective-permute-start | bytes 786440 | tf_op jit(solution)/shard_map/ppermute | solution.py:225
  17.1 11.6 %collective-permute-start.2 = (bf16[2,128,512]{2,1,0:T(8,128)(2,1)S(1)}, bf16[2,128,512]{2,1,0:T(8,128)(2,1)S(1)}, u32[]{:S(2)}, u32[]{:S(2)}) collective-permute-start(bf16[2,128,512]{2,1,0:T(8,128)(2,1)S(1)} %constant_dynamic-update-slice_fusion), channel_id=1, source_target_pairs={{0,2},{2,0},{4,6},{6,4},{8,10},{10,8},{12,14},{14,12},{1,3},{3,1},... | collective-permute-start | bytes 786440 | tf_op jit(solution)/shard_map/ppermute | solution.py:225
  17.9 30.3 %all-to-all-start = ((bf16[8,512,128]{2,1,0:T(8,128)(2,1)}), bf16[8,512,128]{2,1,0:T(8,128)(2,1)S(1)}, u32[]{:S(2)}, u32[]{:S(2)}) async-start(bf16[8,512,128]{2,1,0:T(8,128)(2,1)} %bitcast.6), calls=%async_computation | async-start | bytes 2097152 | tf_op jit(solution)/shard_map/all_to_all | solution.py:338
  28.8 9.2 %collective-permute-start.5 = (bf16[4,128,512]{2,1,0:T(8,128)(2,1)S(1)}, bf16[4,128,512]{2,1,0:T(8,128)(2,1)S(1)}, u32[]{:S(2)}, u32[]{:S(2)}) collective-permute-start(bf16[4,128,512]{2,1,0:T(8,128)(2,1)S(1)} %pad_maximum_fusion), channel_id=1, source_target_pairs={{0,16},{16,0},{1,17},{17,1},{2,18},{18,2},{3,19},{19,3},{4,20},{20... | collective-permute-start | bytes 1572872 | tf_op jit(solution)/shard_map/ppermute | solution.py:225
  38.1 10.2 %collective-permute-start.6 = (bf16[8,128,512]{2,1,0:T(8,128)(2,1)S(1)}, bf16[8,128,512]{2,1,0:T(8,128)(2,1)}, u32[]{:S(2)}, u32[]{:S(2)}) collective-permute-start(bf16[8,128,512]{2,1,0:T(8,128)(2,1)S(1)} %constant_dynamic-update-slice_fusion.2.mine), channel_id=1, source_target_pairs={{0,1},{1,0},{2,3},{3,2},{4,5},{5,4},{6,7},{7,6},{8,9},{9,8},{10,11... | collective-permute-start | bytes 3145736 | tf_op jit(solution)/shard_map/ppermute | solution.py:225
  38.9 12.8 %collective-permute-start.8 = (bf16[4,1,32,1024]{3,2,1,0:T(8,128)(2,1)}, bf16[4,1,32,1024]{3,2,1,0:T(8,128)(2,1)}, u32[]{:S(2)}, u32[]{:S(2)}) collective-permute-start(bf16[4,1,32,1024]{3,2,1,0:T(8,128)(2,1)} %pad_maximum_fusion.1), channel_id=1, source_target_pairs={{0,2},{2,0},{4,6},{6,4},{8,10},{10,8},{12,14},{14,12},{1,3},{3,1},... | collective-permute-start | bytes 786440 | tf_op jit(solution)/shard_map/ppermute | solution.py:225
  42.1 9.5 %collective-permute-start.7 = (bf16[1,1,32,1024]{3,2,1,0:T(8,128)(2,1)S(1)}, bf16[1,1,32,1024]{3,2,1,0:T(8,128)(2,1)S(1)}, u32[]{:S(2)}, u32[]{:S(2)}) collective-permute-start(bf16[1,1,32,1024]{3,2,1,0:T(8,128)(2,1)S(1)} %pick.1), channel_id=1, source_target_pairs={{0,8},{2,10},{4,12},{6,14},{8,0},{10,2},{12,4},{14,6},{1,9},{3,11}... | collective-permute-start | bytes 196616 | tf_op jit(solution)/shard_map/ppermute | solution.py:225
  51.6 5.1 %copy-start.3 = (bf16[128,1024]{1,0:T(8,128)(2,1)S(1)}, bf16[128,1024]{1,0:T(8,128)(2,1)}, u32[]{:S(2)}) copy-start(bf16[128,1024]{1,0:T(8,128)(2,1)} %get-tuple-element.44.weighted) | copy-start | bytes 786436
  51.6 18.5 %copy-start = (bf16[8192,64]{0,1:T(8,128)(2,1)S(1)}, bf16[8192,64]{0,1:T(8,128)(2,1)}, u32[]{:S(2)}) copy-start(bf16[8192,64]{0,1:T(8,128)(2,1)} %param.12) | copy-start | bytes 3145732
  51.6 18.5 %all-to-all-start.1 = ((bf16[8,128,512]{2,1,0:T(8,128)(2,1)}), bf16[8,128,512]{2,1,0:T(8,128)(2,1)S(1)}, u32[]{:S(2)}, u32[]{:S(2)}) async-start(bf16[8,128,512]{2,1,0:T(8,128)(2,1)} %frozen.1), calls=%async_computation.1 | async-start | bytes 2097152 | tf_op jit(solution)/shard_map/all_to_all | solution.py:357
  56.6 2.1 %collective-permute-start.10 = (bf16[2,32,1024]{2,1,0:T(8,128)(2,1)S(1)}, bf16[2,32,1024]{2,1,0:T(8,128)(2,1)S(1)}, u32[]{:S(2)}, u32[]{:S(2)}) collective-permute-start(bf16[2,32,1024]{2,1,0:T(8,128)(2,1)S(1)} %gradient.1), channel_id=1, source_target_pairs={{0,1},{1,0},{2,3},{3,2},{4,5},{5,4},{6,7},{7,6},{8,9},{9,8},{10,11... | collective-permute-start | bytes 393224 | tf_op jit(solution)/shard_map/ppermute | solution.py:225
  57.4 1.3 %collective-permute-start.9 = (bf16[32,128]{1,0:T(8,128)(2,1)S(1)}, bf16[32,128]{1,0:T(8,128)(2,1)S(1)}, u32[]{:S(2)}, u32[]{:S(2)}) collective-permute-start(bf16[32,128]{1,0:T(8,128)(2,1)S(1)} %back.1.mine), channel_id=1, source_target_pairs={{0,1},{1,0},{2,3},{3,2},{4,5},{5,4},{6,7},{7,6},{8,9},{9,8},{10,11... | collective-permute-start | bytes 24584 | tf_op jit(solution)/shard_map/ppermute | solution.py:225

commit v6 on v5

--- a/solution.py
+++ b/solution.py
@@ -26,7 +26,7 @@
 
 
 def prepare_kernel(
-    leaving, counts, upstream, tenants, up, down, hidden, weighted, my_cols, picked, block,
+    leaving, counts, upstream, tenants, up, down, hidden, weighted, my_cols, sooner, later, block,
     held_counts, held_upstream, held_tenants, held_up, held_down, held_hidden, sem,
 ):
     _, _, m = place()
@@ -55,9 +55,10 @@
     my_cols[...] = weighted[:, piece(m, part)]
     loads[2].wait()
     loads[3].wait()
-    for i, k in enumerate(leaving):
-        for n in range(own_blocks):
-            picked[i, n] = chosen(held_tenants, held_up, k, n, own_blocks, part_rank)
+    for ks, picked in zip(leaving, (sooner, later)):
+        for i, k in enumerate(ks):
+            for n in range(own_blocks):
+                picked[i, n] = chosen(held_tenants, held_up, k, n, own_blocks, part_rank)
     loads[4].wait()
     loads[5].wait()
     low = lax.dot_general(
@@ -104,7 +105,8 @@
         for n in range(out.shape[1]):
             value = chosen(tenants, up, k, n, out.shape[1], out.shape[2])
             for kept, got in zip(held, refs[:-1]):
-                value = value + got[kept.index(k), n]
+                if k in kept:
+                    value = value + got[kept.index(k), n]
             out[i, n] = value
 
 
@@ -125,7 +127,8 @@
     for n in range(own_blocks):
         value = chosen(tenants, up, 0, n, own_blocks, part_rank)
         for kept, got in zip(held, refs[:-1]):
-            value = value + got[kept.index(0), n]
+            if 0 in kept:
+                value = value + got[kept.index(0), n]
         at = slice(n * size, (n + 1) * size)
         out[:, at] = lax.dot_general(
             value, weighted[at], (((1,), (1,)), ((), ())), preferred_element_type=f32
@@ -238,18 +241,19 @@
     tie = lax.optimization_barrier
 
     repeats = dp_count // near
-    leaving = [k for k in range(dp_count) if k & 1]
+    leaving = [[k for k in range(dp_count) if k & 1 and bool(k & 2) == sooner] for sooner in (True, False)]
     remaining = [k for k in range(dp_count) if not k & 1]
-    weighted, my_cols, picked, block = call(
+    weighted, my_cols, *picked, block = call(
         functools.partial(prepare_kernel, leaving), "prepare",
         [
             shape(rows, out_width),
             shape(rows, part_cols),
-            shape(len(leaving), own_blocks, part_rank, out_width),
+            shape(len(leaving[0]), own_blocks, part_rank, out_width),
+            shape(len(leaving[1]), own_blocks, part_rank, out_width),
             shape(1, own_blocks, part_rank, out_width),
         ],
         [HBM] * 6, rollout_row_counts[None], upstream, tenant_of_block, adapter_up_factor, common_down_factor.T,
-        hidden_input, out_specs=[VMEM] * 4, params=pltpu.CompilerParams(),
+        hidden_input, out_specs=[VMEM] * 5, params=pltpu.CompilerParams(),
         scratch=[
             pltpu.VMEM((1, rows), jnp.int32),
             pltpu.VMEM((rows, out_width), bf16),
@@ -273,16 +277,21 @@
         ("groups", 1 << k, near << k) for k in range(group_count.bit_length() - 1)
     ]
     team_rows, distances = my_cols[None], [0]
-    held, got = [list(remaining)], [swap(picked, "dp", 1)]
+    held = [[k ^ 1 for k in ks] for ks in leaving]
+    got = [swap(value, "dp", 1) for value in picked]
+
+    def useful(keys):
+        return [i for i, kept in enumerate(held) if set(kept) & set(keys)]
     pieces, orders = [block], [[0]]
     last = []
 
     def up_step(bit):
         leaving = [k for k in remaining if k & bit]
+        some = useful(leaving)
         value = call(
-            functools.partial(pick_kernel, leaving, list(held)), "pick",
-            shape(len(leaving), own_blocks, part_rank, out_width), [SMEM, VMEM] + [VMEM] * len(got),
-            tenant_of_block, adapter_up_factor, *got,
+            functools.partial(pick_kernel, leaving, [held[i] for i in some]), "pick",
+            shape(len(leaving), own_blocks, part_rank, out_width), [SMEM, VMEM] + [VMEM] * len(some),
+            tenant_of_block, adapter_up_factor, *[got[i] for i in some],
         )
         last.append(value)
         remaining[:] = [k for k in remaining if not k & bit]
@@ -302,11 +311,12 @@
     def both_step(bit):
         leaving = [k for k in remaining if k & bit]
         blocks = gathered()
+        some = useful(leaving)
         value = call(
-            functools.partial(both_kernel, leaving, list(held)), "both",
+            functools.partial(both_kernel, leaving, [held[i] for i in some]), "both",
             shape(len(leaving) + len(blocks), own_blocks, part_rank, out_width),
-            [SMEM, VMEM] + [VMEM] * (len(got) + len(pieces)),
-            tenant_of_block, adapter_up_factor, *got, *pieces,
+            [SMEM, VMEM] + [VMEM] * (len(some) + len(pieces)),
+            tenant_of_block, adapter_up_factor, *[got[i] for i in some], *pieces,
         )
         last.append(value)
         remaining[:] = [k for k in remaining if not k & bit]
@@ -329,9 +339,11 @@
         if step == 1:
             to_send, *_ = tie((to_send, team_rows, *last))
         if step == 0:
-            team_rows, new_rows, got, to_send = tie((team_rows, new_rows, got, to_send))
+            team_rows, new_rows, got[:1], to_send = tie((team_rows, new_rows, got[:1], to_send))
         elif step < len(row_steps) - 1:
-            team_rows, new_rows, got, pieces = tie((team_rows, new_rows, got, pieces))
+            team_rows, new_rows, got[::2], pieces = tie((team_rows, new_rows, got[::2], pieces))
+        else:
+            new_rows, got[1] = tie((new_rows, got[1]))
         team_rows = jnp.concatenate([team_rows, new_rows])
         distances = distances + [k | distance for k in distances]
     other_rows = swap(team_rows, "mp", 1)
@@ -361,9 +373,10 @@
         up_step(bit)
     for bit in block_bits:
         block_step(bit)
+    some = useful([0])
     back_part = call(
-        functools.partial(back_kernel, held), "back", shape(part_rank, rows), [SMEM, VMEM, VMEM] + [VMEM] * len(got),
-        tenant_of_block, adapter_up_factor, weighted, *got,
+        functools.partial(back_kernel, [held[i] for i in some]), "back", shape(part_rank, rows),
+        [SMEM, VMEM, VMEM] + [VMEM] * len(some), tenant_of_block, adapter_up_factor, weighted, *[got[i] for i in some],
     )
 
     grad_part = call(

time: 71.8 us -> 71.3 us (level)
  local copies, waits for them, and re-layouts: 0.14 us -> 1.57 us
  waiting for transfers between devices: 30.9 us -> 29.9 us
    ppermute x11 -> x12, waiting for transfers between devices: 16.6 us -> 13.6 us  [swap(): return lax.ppermute(value, axis, [(k, k ^ bit) for k in range(size)])]
    all_to_all x1, waiting for transfers between devices: 3 us -> 5.55 us  [local(): lax.all_to_all(to_send.reshape(dp_count, features, cols), 'dp', split_axi...]
    unnamed x15 -> x21, local copies, waits for them, and re-layouts: 0.08 us -> 1.52 us
    ppermute x11 -> x12, starting transfers between devices: 17.8 us -> 17 us  [swap(): return lax.ppermute(value, axis, [(k, k ^ bit) for k in range(size)])]
  transfers between devices with their start and end apart: 13 -> 14, of which waited for: 8 -> 8; matrix products, arithmetic and copies ran while one was open for 1% -> 1% of each run, Pallas kernels for 11% -> 10%
where the time goes in v6:
time: 71.3 us; the launch traced here: 71 us
  waiting for transfers between devices  29.9 us (42%)
  starting transfers between devices  24.9 us (35%)
  Pallas kernels  12.9 us (18%)
  local copies, waits for them, and re-layouts  1.57 us (2%)
  between operations  0.87 us (1%)
  other arithmetic  0.77 us (1%)
    ppermute x12, starting transfers between devices, swap(): return lax.ppermute(value, axis, [(k, k ^ bit) for k in range(size)])  17 us
    ppermute x12, waiting for transfers between devices, swap(): return lax.ppermute(value, axis, [(k, k ^ bit) for k in range(size)])  13.6 us
    pallas_call x8, Pallas kernels, call(): pl.pallas_call(kernel, in_specs=in_specs, out_specs=out_specs, out_shape=...  12.9 us
    all_to_all x1, waiting for transfers between devices, local(): lax.all_to_all(frozen, ALL, split_axis=0, concat_axis=0, tiled=True, axis...  10.7 us
    all_to_all x1, waiting for transfers between devices, local(): lax.all_to_all(to_send.reshape(dp_count, features, cols), 'dp', split_axi...  5.55 us
    all_to_all x1, starting transfers between devices, local(): lax.all_to_all(to_send.reshape(dp_count, features, cols), 'dp', split_axi...  4.3 us
    all_to_all x1, starting transfers between devices, local(): lax.all_to_all(frozen, ALL, split_axis=0, concat_axis=0, tiled=True, axis...  3.62 us
    unnamed x21, local copies, waits for them, and re-layouts  1.52 us
  transfers between devices with their start and end apart: 14, of which 8 were waited for; matrix products, arithmetic and copies ran while one was open for 1% of the time, Pallas kernels for 10%

profile of v6, /device:TPU:0, one launch (start us, length us, event | category | flops | bytes accessed | tf_op | source)
XLA Modules:
  0.0 71.0 jit_solution(9679572509439955659)
XLA Ops:
  0.6 3.6 %prepare.1 = (bf16[128,1024]{1,0:T(8,128)(2,1)}, bf16[128,512]{1,0:T(8,128)(2,1)}, bf16[2,1,32,1024]{3,2,1,0:T(8,128)(2,1)}, bf16[2,1,32,1024]{3,2,1,0:T(8,128)(2,1)}, bf16[1,1,32,1024]{3,2,1,0:T(8,128)(2,1)}) custom-call(s32[1,128]{1,0:T(1,128)} %bitcast.9, bf16[128,1024]{1,0:T(8,128)(2,1)} %upstream.1, s32[8]{0:T(128)} %tenants.9, ...), custom_call_target="tpu_custom_call" | custom-call | tf_op jit(solution)/shard_map/prepare/pallas_call | solution.py:234
  4.3 3.1 %collective-permute-start = (bf16[1,128,512]{2,1,0:T(8,128)(2,1)}, bf16[1,128,512]{2,1,0:T(8,128)(2,1)S(1)}, u32[]{:S(2)}, u32[]{:S(2)}) collective-permute-start(bf16[1,128,512]{2,1,0:T(8,128)(2,1)} %bitcast.7), channel_id=1, source_target_pairs={{0,4},{2,6},{4,0},{6,2},{8,12},{10,14},{12,8},{14,10},{1,5},{3,7},... | collective-permute-start | bytes 393224 | tf_op jit(solution)/shard_map/ppermute | solution.py:228
  7.4 1.5 %collective-permute-start.1 = (bf16[2,1,32,1024]{3,2,1,0:T(8,128)(2,1)}, bf16[2,1,32,1024]{3,2,1,0:T(8,128)(2,1)S(1)}, u32[]{:S(2)}, u32[]{:S(2)}) collective-permute-start(bf16[2,1,32,1024]{3,2,1,0:T(8,128)(2,1)} %get-tuple-element.30), channel_id=1, source_target_pairs={{0,2},{2,0},{4,6},{6,4},{8,10},{10,8},{12,14},{14,12},{1,3},{3,1},... | collective-permute-start | bytes 393224 | tf_op jit(solution)/shard_map/ppermute | solution.py:228
  8.9 2.6 %collective-permute-start.3 = (bf16[1,1,32,1024]{3,2,1,0:T(8,128)(2,1)}, bf16[1,1,32,1024]{3,2,1,0:T(8,128)(2,1)S(1)}, u32[]{:S(2)}, u32[]{:S(2)}) collective-permute-start(bf16[1,1,32,1024]{3,2,1,0:T(8,128)(2,1)} %get-tuple-element.52._.refs_1_.refs_0_), channel_id=1, source_target_pairs={{0,8},{2,10},{4,12},{6,14},{8,0},{10,2},{12,4},{14,6},{1,9},{3,11}... | collective-permute-start | bytes 196616 | tf_op jit(solution)/shard_map/ppermute | solution.py:228
  11.5 2.0 %spread.1 = bf16[2,2048,128]{2,1,0:T(8,128)(2,1)} custom-call(bf16[4096,128]{1,0:T(8,128)(2,1)} %weight.1, bf16[1,1,32,1024]{3,2,1,0:T(8,128)(2,1)} %get-tuple-element.52._.refs_1_.refs_0_), custom_call_target="tpu_custom_call" | custom-call | tf_op jit(solution)/shard_map/spread/pallas_call | solution.py:234
  13.5 1.5 %collective-permute-done.3.refs_2_.refs_1_ = bf16[1,1,32,1024]{3,2,1,0:T(8,128)(2,1)S(1)} collective-permute-done((bf16[1,1,32,1024]{3,2,1,0:T(8,128)(2,1)}, bf16[1,1,32,1024]{3,2,1,0:T(8,128)(2,1)S(1)}, u32[]{:S(2)}, u32[]{:S(2)}) %collective-permute-start.3) | collective-permute-done | bytes 65568 | tf_op jit(solution)/shard_map/ppermute | solution.py:228
  15.0 0.6 both.1
  15.5 0.5 collective-permute-start.4
  16.0 1.5 %collective-permute-start.2 = (bf16[2,128,512]{2,1,0:T(8,128)(2,1)S(1)}, bf16[2,128,512]{2,1,0:T(8,128)(2,1)S(1)}, u32[]{:S(2)}, u32[]{:S(2)}) collective-permute-start(bf16[2,128,512]{2,1,0:T(8,128)(2,1)S(1)} %constant_dynamic-update-slice_fusion), channel_id=1, source_target_pairs={{0,2},{2,0},{4,6},{6,4},{8,10},{10,8},{12,14},{14,12},{1,3},{3,1},... | collective-permute-start | bytes 786440 | tf_op jit(solution)/shard_map/ppermute | solution.py:228
  17.5 4.3 %all-to-all-start = ((bf16[8,512,128]{2,1,0:T(8,128)(2,1)}), bf16[8,512,128]{2,1,0:T(8,128)(2,1)S(1)}, u32[]{:S(2)}, u32[]{:S(2)}) async-start(bf16[8,512,128]{2,1,0:T(8,128)(2,1)} %bitcast.6), calls=%async_computation | async-start | bytes 2097152 | tf_op jit(solution)/shard_map/all_to_all | solution.py:350
  21.8 0.3 collective-permute-done.4.refs_1_.refs_2_
  22.0 6.3 %collective-permute-done.2 = bf16[2,128,512]{2,1,0:T(8,128)(2,1)S(1)} collective-permute-done((bf16[2,128,512]{2,1,0:T(8,128)(2,1)S(1)}, bf16[2,128,512]{2,1,0:T(8,128)(2,1)S(1)}, u32[]{:S(2)}, u32[]{:S(2)}) %collective-permute-start.2) | collective-permute-done | bytes 262176 | tf_op jit(solution)/shard_map/ppermute | solution.py:228
  28.3 1.6 %collective-permute-start.5 = (bf16[4,128,512]{2,1,0:T(8,128)(2,1)S(1)}, bf16[4,128,512]{2,1,0:T(8,128)(2,1)S(1)}, u32[]{:S(2)}, u32[]{:S(2)}) collective-permute-start(bf16[4,128,512]{2,1,0:T(8,128)(2,1)S(1)} %pad_maximum_fusion), channel_id=1, source_target_pairs={{0,16},{16,0},{1,17},{17,1},{2,18},{18,2},{3,19},{19,3},{4,20},{20... | collective-permute-start | bytes 1572872 | tf_op jit(solution)/shard_map/ppermute | solution.py:228
  29.9 2.8 %collective-permute-start.6 = (bf16[2,1,32,1024]{3,2,1,0:T(8,128)(2,1)S(1)}, bf16[2,1,32,1024]{3,2,1,0:T(8,128)(2,1)S(1)}, u32[]{:S(2)}, u32[]{:S(2)}) collective-permute-start(bf16[2,1,32,1024]{3,2,1,0:T(8,128)(2,1)S(1)} %copy-done.8), channel_id=1, source_target_pairs={{0,2},{2,0},{4,6},{6,4},{8,10},{10,8},{12,14},{14,12},{1,3},{3,1},... | collective-permute-start | bytes 393224 | tf_op jit(solution)/shard_map/ppermute | solution.py:228
  32.8 3.3 %collective-permute-done.6.refs_0_ = bf16[2,1,32,1024]{3,2,1,0:T(8,128)(2,1)S(1)} collective-permute-done((bf16[2,1,32,1024]{3,2,1,0:T(8,128)(2,1)S(1)}, bf16[2,1,32,1024]{3,2,1,0:T(8,128)(2,1)S(1)}, u32[]{:S(2)}, u32[]{:S(2)}) %collective-permute-start.6) | collective-permute-done | bytes 131104 | tf_op jit(solution)/shard_map/ppermute | solution.py:228
  36.1 1.5 %collective-permute-done.5 = bf16[4,128,512]{2,1,0:T(8,128)(2,1)S(1)} collective-permute-done((bf16[4,128,512]{2,1,0:T(8,128)(2,1)S(1)}, bf16[4,128,512]{2,1,0:T(8,128)(2,1)S(1)}, u32[]{:S(2)}, u32[]{:S(2)}) %collective-permute-start.5) | collective-permute-done | bytes 524320 | tf_op jit(solution)/shard_map/ppermute | solution.py:228
  37.6 0.1 collective-permute-start.7
  37.7 0.7 %pad_maximum_fusion.1 = bf16[4,1,32,1024]{3,2,1,0:T(8,128)(2,1)} fusion(bf16[2,1,32,1024]{3,2,1,0:T(8,128)(2,1)S(1)} %slice.3, bf16[1,1,32,1024]{3,2,1,0:T(8,128)(2,1)S(1)} %collective-permute-done.3.refs_2_.refs_1_, bf16[1,1,32,1024]{3,2,1,0:T(8,128)(2,1)S(1)} %copy-done.2), kind=kLoop, calls=%fused_computation.1 | loop fusion | flops 262144 | bytes 524288 | tf_op jit(solution)/shard_map/concatenate | solution.py:306
  38.4 2.8 %collective-permute-start.9 = (bf16[4,1,32,1024]{3,2,1,0:T(8,128)(2,1)}, bf16[4,1,32,1024]{3,2,1,0:T(8,128)(2,1)S(1)}, u32[]{:S(2)}, u32[]{:S(2)}) collective-permute-start(bf16[4,1,32,1024]{3,2,1,0:T(8,128)(2,1)} %pad_maximum_fusion.1), channel_id=1, source_target_pairs={{0,2},{2,0},{4,6},{6,4},{8,10},{10,8},{12,14},{14,12},{1,3},{3,1},... | collective-permute-start | bytes 786440 | tf_op jit(solution)/shard_map/ppermute | solution.py:228
  41.2 0.6 pick.1
  41.9 5.6 %all-to-all-done.slices = bf16[8,512,128]{2,1,0:T(8,128)(2,1)S(1)} async-done(((bf16[8,512,128]{2,1,0:T(8,128)(2,1)}), bf16[8,512,128]{2,1,0:T(8,128)(2,1)S(1)}, u32[]{:S(2)}, u32[]{:S(2)}) %all-to-all-start) | async-done | bytes 1048608 | tf_op jit(solution)/shard_map/all_to_all | solution.py:350
  47.4 3.4 %frozen.1 = bf16[8,128,512]{2,1,0:T(8,128)(2,1)} custom-call(bf16[8,128,512]{2,1,0:T(8,128)(2,1)S(1)} %constant_dynamic-update-slice_fusion.2.mine, bf16[8,128,512]{2,1,0:T(8,128)(2,1)} %collective-permute-done.7.other, bf16[8,512,128]{2,1,0:T(8,128)(2,1)S(1)} %all-to-all-done.slices), custom_call_target="tpu_custom_call" | custom-call | tf_op jit(solution)/shard_map/frozen/pallas_call | solution.py:234
  50.9 0.6 copy-done.4
  51.5 3.6 %all-to-all-start.1 = ((bf16[8,128,512]{2,1,0:T(8,128)(2,1)}), bf16[8,128,512]{2,1,0:T(8,128)(2,1)S(1)}, u32[]{:S(2)}, u32[]{:S(2)}) async-start(bf16[8,128,512]{2,1,0:T(8,128)(2,1)} %frozen.1), calls=%async_computation.1 | async-start | bytes 2097152 | tf_op jit(solution)/shard_map/all_to_all | solution.py:369
  55.1 0.8 %gradient.1 = bf16[2,32,1024]{2,1,0:T(8,128)(2,1)S(1)} custom-call(s32[8]{0:T(128)S(1)} %copy-done.6, bf16[1,1,32,1024]{3,2,1,0:T(8,128)(2,1)S(1)} %copy-done.2, bf16[1,1,32,1024]{3,2,1,0:T(8,128)(2,1)S(1)} %collective-permute-done.3.refs_2_.refs_1_, bf16[4,1,32,1024]{3,2,1,0:T(8,128)(2,1)S(1)} %collective-permute-done.4.refs_1_.refs_2_, ...), custom_call_target="tpu_custom_call" | custom-call | tf_op jit(solution)/shard_map/gradient/pallas_call | solution.py:234
  55.9 0.1 collective-permute-start.11
  56.0 0.8 %copy-done.5 = bf16[1,1,32,1024]{3,2,1,0:T(8,128)(2,1)S(1)} copy-done((bf16[1,1,32,1024]{3,2,1,0:T(8,128)(2,1)S(1)}, bf16[1,1,32,1024]{3,2,1,0:T(8,128)(2,1)}, u32[]{:S(2)}) %copy-start.5) | copy-done | bytes 65560
  56.8 0.7 back.1.mine
  57.5 0.5 collective-permute-start.10
  58.0 0.8 %collective-permute-done.10.other = bf16[32,128]{1,0:T(8,128)(2,1)S(1)} collective-permute-done((bf16[32,128]{1,0:T(8,128)(2,1)S(1)}, bf16[32,128]{1,0:T(8,128)(2,1)S(1)}, u32[]{:S(2)}, u32[]{:S(2)}) %collective-permute-start.10) | collective-permute-done | bytes 8224 | tf_op jit(solution)/shard_map/ppermute | solution.py:228
  58.9 10.7 %all-to-all-done.1.frozen = bf16[8,128,512]{2,1,0:T(8,128)(2,1)S(1)} async-done(((bf16[8,128,512]{2,1,0:T(8,128)(2,1)}), bf16[8,128,512]{2,1,0:T(8,128)(2,1)S(1)}, u32[]{:S(2)}, u32[]{:S(2)}) %all-to-all-start.1) | async-done | bytes 1048608 | tf_op jit(solution)/shard_map/all_to_all | solution.py:369
  69.6 1.4 %last.1 = (bf16[128,4096]{1,0:T(8,128)(2,1)}, bf16[2,64,1024]{2,1,0:T(8,128)(2,1)}) custom-call(bf16[8,128,512]{2,1,0:T(8,128)(2,1)S(1)} %all-to-all-done.1.frozen, bf16[32,128]{1,0:T(8,128)(2,1)S(1)} %back.1.mine, bf16[32,128]{1,0:T(8,128)(2,1)S(1)} %collective-permute-done.10.other, bf16[64,8192]{1,0:T(8,128)(2,1)S(1)} %bitcast.5, ...), custom_call_target="tpu_custom_call" | custom-call | tf_op jit(solution)/shard_map/last/pallas_call | solution.py:234
  (30 shorter events, 0.3 us)
Async XLA Ops:
  4.2 9.2 %copy-start.7 = (bf16[128,512]{1,0:T(8,128)(2,1)S(1)}, bf16[128,512]{1,0:T(8,128)(2,1)}, u32[]{:S(2)}) copy-start(bf16[128,512]{1,0:T(8,128)(2,1)} %get-tuple-element.29) | copy-start | bytes 393220
  4.3 10.7 %copy-start.1 = (bf16[2,64,1024]{2,1,0:T(8,128)(2,1)S(1)}, bf16[2,64,1024]{2,1,0:T(8,128)(2,1)}, u32[]{:S(2)}) copy-start(bf16[2,64,1024]{2,1,0:T(8,128)(2,1)} %up.7) | copy-start | bytes 786436
  4.3 10.7 %copy-start.2 = (bf16[1,1,32,1024]{3,2,1,0:T(8,128)(2,1)S(1)}, bf16[1,1,32,1024]{3,2,1,0:T(8,128)(2,1)}, u32[]{:S(2)}) copy-start(bf16[1,1,32,1024]{3,2,1,0:T(8,128)(2,1)} %get-tuple-element.52._.refs_1_.refs_0_) | copy-start | bytes 196612
  4.3 10.7 %copy-start.6 = (s32[8]{0:T(128)S(1)}, s32[8]{0:T(128)}, u32[]{:S(2)}) copy-start(s32[8]{0:T(128)} %tenants.9) | copy-start | bytes 100
  4.3 9.1 %collective-permute-start = (bf16[1,128,512]{2,1,0:T(8,128)(2,1)}, bf16[1,128,512]{2,1,0:T(8,128)(2,1)S(1)}, u32[]{:S(2)}, u32[]{:S(2)}) collective-permute-start(bf16[1,128,512]{2,1,0:T(8,128)(2,1)} %bitcast.7), channel_id=1, source_target_pairs={{0,4},{2,6},{4,0},{6,2},{8,12},{10,14},{12,8},{14,10},{1,5},{3,7},... | collective-permute-start | bytes 393224 | tf_op jit(solution)/shard_map/ppermute | solution.py:228
  7.4 6.1 %collective-permute-start.1 = (bf16[2,1,32,1024]{3,2,1,0:T(8,128)(2,1)}, bf16[2,1,32,1024]{3,2,1,0:T(8,128)(2,1)S(1)}, u32[]{:S(2)}, u32[]{:S(2)}) collective-permute-start(bf16[2,1,32,1024]{3,2,1,0:T(8,128)(2,1)} %get-tuple-element.30), channel_id=1, source_target_pairs={{0,2},{2,0},{4,6},{6,4},{8,10},{10,8},{12,14},{14,12},{1,3},{3,1},... | collective-permute-start | bytes 393224 | tf_op jit(solution)/shard_map/ppermute | solution.py:228
  8.9 6.1 %collective-permute-start.3 = (bf16[1,1,32,1024]{3,2,1,0:T(8,128)(2,1)}, bf16[1,1,32,1024]{3,2,1,0:T(8,128)(2,1)S(1)}, u32[]{:S(2)}, u32[]{:S(2)}) collective-permute-start(bf16[1,1,32,1024]{3,2,1,0:T(8,128)(2,1)} %get-tuple-element.52._.refs_1_.refs_0_), channel_id=1, source_target_pairs={{0,8},{2,10},{4,12},{6,14},{8,0},{10,2},{12,4},{14,6},{1,9},{3,11}... | collective-permute-start | bytes 196616 | tf_op jit(solution)/shard_map/ppermute | solution.py:228
  13.5 16.4 %copy-start.8 = (bf16[2,1,32,1024]{3,2,1,0:T(8,128)(2,1)S(1)}, bf16[2,1,32,1024]{3,2,1,0:T(8,128)(2,1)}, u32[]{:S(2)}) copy-start(bf16[2,1,32,1024]{3,2,1,0:T(8,128)(2,1)} %get-tuple-element.37) | copy-start | bytes 393220
  15.5 6.5 %collective-permute-start.4 = (bf16[4,1,32,1024]{3,2,1,0:T(8,128)(2,1)S(1)}, bf16[4,1,32,1024]{3,2,1,0:T(8,128)(2,1)S(1)}, u32[]{:S(2)}, u32[]{:S(2)}) collective-permute-start(bf16[4,1,32,1024]{3,2,1,0:T(8,128)(2,1)S(1)} %both.1), channel_id=1, source_target_pairs={{0,4},{2,6},{4,0},{6,2},{8,12},{10,14},{12,8},{14,10},{1,5},{3,7},... | collective-permute-start | bytes 786440 | tf_op jit(solution)/shard_map/ppermute | solution.py:228
  16.0 12.3 %collective-permute-start.2 = (bf16[2,128,512]{2,1,0:T(8,128)(2,1)S(1)}, bf16[2,128,512]{2,1,0:T(8,128)(2,1)S(1)}, u32[]{:S(2)}, u32[]{:S(2)}) collective-permute-start(bf16[2,128,512]{2,1,0:T(8,128)(2,1)S(1)} %constant_dynamic-update-slice_fusion), channel_id=1, source_target_pairs={{0,2},{2,0},{4,6},{6,4},{8,10},{10,8},{12,14},{14,12},{1,3},{3,1},... | collective-permute-start | bytes 786440 | tf_op jit(solution)/shard_map/ppermute | solution.py:228
  17.5 30.0 %all-to-all-start = ((bf16[8,512,128]{2,1,0:T(8,128)(2,1)}), bf16[8,512,128]{2,1,0:T(8,128)(2,1)S(1)}, u32[]{:S(2)}, u32[]{:S(2)}) async-start(bf16[8,512,128]{2,1,0:T(8,128)(2,1)} %bitcast.6), calls=%async_computation | async-start | bytes 2097152 | tf_op jit(solution)/shard_map/all_to_all | solution.py:350
  28.3 9.2 %collective-permute-start.5 = (bf16[4,128,512]{2,1,0:T(8,128)(2,1)S(1)}, bf16[4,128,512]{2,1,0:T(8,128)(2,1)S(1)}, u32[]{:S(2)}, u32[]{:S(2)}) collective-permute-start(bf16[4,128,512]{2,1,0:T(8,128)(2,1)S(1)} %pad_maximum_fusion), channel_id=1, source_target_pairs={{0,16},{16,0},{1,17},{17,1},{2,18},{18,2},{3,19},{19,3},{4,20},{20... | collective-permute-start | bytes 1572872 | tf_op jit(solution)/shard_map/ppermute | solution.py:228
  29.9 6.2 %collective-permute-start.6 = (bf16[2,1,32,1024]{3,2,1,0:T(8,128)(2,1)S(1)}, bf16[2,1,32,1024]{3,2,1,0:T(8,128)(2,1)S(1)}, u32[]{:S(2)}, u32[]{:S(2)}) collective-permute-start(bf16[2,1,32,1024]{3,2,1,0:T(8,128)(2,1)S(1)} %copy-done.8), channel_id=1, source_target_pairs={{0,2},{2,0},{4,6},{6,4},{8,10},{10,8},{12,14},{14,12},{1,3},{3,1},... | collective-permute-start | bytes 393224 | tf_op jit(solution)/shard_map/ppermute | solution.py:228
  37.6 9.8 %collective-permute-start.7 = (bf16[8,128,512]{2,1,0:T(8,128)(2,1)S(1)}, bf16[8,128,512]{2,1,0:T(8,128)(2,1)}, u32[]{:S(2)}, u32[]{:S(2)}) collective-permute-start(bf16[8,128,512]{2,1,0:T(8,128)(2,1)S(1)} %constant_dynamic-update-slice_fusion.2.mine), channel_id=1, source_target_pairs={{0,1},{1,0},{2,3},{3,2},{4,5},{5,4},{6,7},{7,6},{8,9},{9,8},{10,11... | collective-permute-start | bytes 3145736 | tf_op jit(solution)/shard_map/ppermute | solution.py:228
  38.4 12.4 %collective-permute-start.9 = (bf16[4,1,32,1024]{3,2,1,0:T(8,128)(2,1)}, bf16[4,1,32,1024]{3,2,1,0:T(8,128)(2,1)S(1)}, u32[]{:S(2)}, u32[]{:S(2)}) collective-permute-start(bf16[4,1,32,1024]{3,2,1,0:T(8,128)(2,1)} %pad_maximum_fusion.1), channel_id=1, source_target_pairs={{0,2},{2,0},{4,6},{6,4},{8,10},{10,8},{12,14},{14,12},{1,3},{3,1},... | collective-permute-start | bytes 786440 | tf_op jit(solution)/shard_map/ppermute | solution.py:228
  41.8 9.0 %collective-permute-start.8 = (bf16[1,1,32,1024]{3,2,1,0:T(8,128)(2,1)S(1)}, bf16[1,1,32,1024]{3,2,1,0:T(8,128)(2,1)S(1)}, u32[]{:S(2)}, u32[]{:S(2)}) collective-permute-start(bf16[1,1,32,1024]{3,2,1,0:T(8,128)(2,1)S(1)} %pick.1), channel_id=1, source_target_pairs={{0,8},{2,10},{4,12},{6,14},{8,0},{10,2},{12,4},{14,6},{1,9},{3,11}... | collective-permute-start | bytes 196616 | tf_op jit(solution)/shard_map/ppermute | solution.py:228
  50.8 5.1 %copy-start.3 = (bf16[128,1024]{1,0:T(8,128)(2,1)S(1)}, bf16[128,1024]{1,0:T(8,128)(2,1)}, u32[]{:S(2)}) copy-start(bf16[128,1024]{1,0:T(8,128)(2,1)} %get-tuple-element.48.weighted) | copy-start | bytes 786436
  50.8 18.8 %copy-start = (bf16[8192,64]{0,1:T(8,128)(2,1)S(1)}, bf16[8192,64]{0,1:T(8,128)(2,1)}, u32[]{:S(2)}) copy-start(bf16[8192,64]{0,1:T(8,128)(2,1)} %param.12) | copy-start | bytes 3145732
  50.9 0.6 copy-start.4
  51.5 18.1 %all-to-all-start.1 = ((bf16[8,128,512]{2,1,0:T(8,128)(2,1)}), bf16[8,128,512]{2,1,0:T(8,128)(2,1)S(1)}, u32[]{:S(2)}, u32[]{:S(2)}) async-start(bf16[8,128,512]{2,1,0:T(8,128)(2,1)} %frozen.1), calls=%async_computation.1 | async-start | bytes 2097152 | tf_op jit(solution)/shard_map/all_to_all | solution.py:369
  55.9 3.0 %collective-permute-start.11 = (bf16[2,32,1024]{2,1,0:T(8,128)(2,1)S(1)}, bf16[2,32,1024]{2,1,0:T(8,128)(2,1)S(1)}, u32[]{:S(2)}, u32[]{:S(2)}) collective-permute-start(bf16[2,32,1024]{2,1,0:T(8,128)(2,1)S(1)} %gradient.1), channel_id=1, source_target_pairs={{0,1},{1,0},{2,3},{3,2},{4,5},{5,4},{6,7},{7,6},{8,9},{9,8},{10,11... | collective-permute-start | bytes 393224 | tf_op jit(solution)/shard_map/ppermute | solution.py:228
  56.0 0.8 %copy-start.5 = (bf16[1,1,32,1024]{3,2,1,0:T(8,128)(2,1)S(1)}, bf16[1,1,32,1024]{3,2,1,0:T(8,128)(2,1)}, u32[]{:S(2)}) copy-start(bf16[1,1,32,1024]{3,2,1,0:T(8,128)(2,1)} %copy-done.4) | copy-start | bytes 196612
  57.5 1.4 %collective-permute-start.10 = (bf16[32,128]{1,0:T(8,128)(2,1)S(1)}, bf16[32,128]{1,0:T(8,128)(2,1)S(1)}, u32[]{:S(2)}, u32[]{:S(2)}) collective-permute-start(bf16[32,128]{1,0:T(8,128)(2,1)S(1)} %back.1.mine), channel_id=1, source_target_pairs={{0,1},{1,0},{2,3},{3,2},{4,5},{5,4},{6,7},{7,6},{8,9},{9,8},{10,11... | collective-permute-start | bytes 24584 | tf_op jit(solution)/shard_map/ppermute | solution.py:228

commit v7 on v6

--- a/solution.py
+++ b/solution.py
@@ -365,7 +365,7 @@
             pltpu.SemaphoreType.DMA((team,)),
         ],
     )
-    frozen, got, pieces = tie((frozen, got, pieces))
+    frozen, *_ = tie((frozen, got, pieces))
     frozen_mine = lax.all_to_all(
         frozen, ALL, split_axis=0, concat_axis=0, tiled=True, axis_index_groups=teams
     )

time: 71.3 us -> 68.2 us (0.957)
  waiting for transfers between devices: 29.9 us -> 27.4 us
    ppermute x12, waiting for transfers between devices: 13.6 us -> 11.1 us  [swap(): return lax.ppermute(value, axis, [(k, k ^ bit) for k in range(size)])]
    all_to_all x1, waiting for transfers between devices: 10.7 us -> 8.68 us  [local(): lax.all_to_all(frozen, ALL, split_axis=0, concat_axis=0, tiled=True, axis...]
    all_to_all x1, waiting for transfers between devices: 5.55 us -> 7.6 us  [local(): lax.all_to_all(to_send.reshape(dp_count, features, cols), 'dp', split_axi...]
  transfers between devices with their start and end apart: 14 -> 14, of which waited for: 8 -> 7; matrix products, arithmetic and copies ran while one was open for 1% -> 1% of each run, Pallas kernels for 10% -> 12%
where the time goes in v7:
time: 68.2 us; the launch traced here: 67.9 us
  waiting for transfers between devices  27.4 us (40%)
  starting transfers between devices  24.3 us (36%)
  Pallas kernels  12.9 us (19%)
  local copies, waits for them, and re-layouts  1.57 us (2%)
  between operations  0.87 us (1%)
  other arithmetic  0.77 us (1%)
    ppermute x12, starting transfers between devices, swap(): return lax.ppermute(value, axis, [(k, k ^ bit) for k in range(size)])  16.4 us
    pallas_call x8, Pallas kernels, call(): pl.pallas_call(kernel, in_specs=in_specs, out_specs=out_specs, out_shape=...  12.9 us
    ppermute x12, waiting for transfers between devices, swap(): return lax.ppermute(value, axis, [(k, k ^ bit) for k in range(size)])  11.1 us
    all_to_all x1, waiting for transfers between devices, local(): lax.all_to_all(frozen, ALL, split_axis=0, concat_axis=0, tiled=True, axis...  8.68 us
    all_to_all x1, waiting for transfers between devices, local(): lax.all_to_all(to_send.reshape(dp_count, features, cols), 'dp', split_axi...  7.6 us
    all_to_all x1, starting transfers between devices, local(): lax.all_to_all(to_send.reshape(dp_count, features, cols), 'dp', split_axi...  4.37 us
    all_to_all x1, starting transfers between devices, local(): lax.all_to_all(frozen, ALL, split_axis=0, concat_axis=0, tiled=True, axis...  3.61 us
    unnamed x21, local copies, waits for them, and re-layouts  1.52 us
  transfers between devices with their start and end apart: 14, of which 7 were waited for; matrix products, arithmetic and copies ran while one was open for 1% of the time, Pallas kernels for 12%

profile of v7, /device:TPU:0, one launch (start us, length us, event | category | flops | bytes accessed | tf_op | source)
XLA Modules:
  0.0 67.9 jit_solution(8243248248798428447)
XLA Ops:
  0.6 3.6 %prepare.1 = (bf16[128,1024]{1,0:T(8,128)(2,1)}, bf16[128,512]{1,0:T(8,128)(2,1)}, bf16[2,1,32,1024]{3,2,1,0:T(8,128)(2,1)}, bf16[2,1,32,1024]{3,2,1,0:T(8,128)(2,1)}, bf16[1,1,32,1024]{3,2,1,0:T(8,128)(2,1)}) custom-call(s32[1,128]{1,0:T(1,128)} %bitcast.9, bf16[128,1024]{1,0:T(8,128)(2,1)} %upstream.1, s32[8]{0:T(128)} %tenants.9, ...), custom_call_target="tpu_custom_call" | custom-call | tf_op jit(solution)/shard_map/prepare/pallas_call | solution.py:234
  4.3 3.1 %collective-permute-start = (bf16[1,128,512]{2,1,0:T(8,128)(2,1)}, bf16[1,128,512]{2,1,0:T(8,128)(2,1)S(1)}, u32[]{:S(2)}, u32[]{:S(2)}) collective-permute-start(bf16[1,128,512]{2,1,0:T(8,128)(2,1)} %bitcast.7), channel_id=1, source_target_pairs={{0,4},{2,6},{4,0},{6,2},{8,12},{10,14},{12,8},{14,10},{1,5},{3,7},... | collective-permute-start | bytes 393224 | tf_op jit(solution)/shard_map/ppermute | solution.py:228
  7.4 1.5 %collective-permute-start.1 = (bf16[2,1,32,1024]{3,2,1,0:T(8,128)(2,1)}, bf16[2,1,32,1024]{3,2,1,0:T(8,128)(2,1)S(1)}, u32[]{:S(2)}, u32[]{:S(2)}) collective-permute-start(bf16[2,1,32,1024]{3,2,1,0:T(8,128)(2,1)} %get-tuple-element.23), channel_id=1, source_target_pairs={{0,2},{2,0},{4,6},{6,4},{8,10},{10,8},{12,14},{14,12},{1,3},{3,1},... | collective-permute-start | bytes 393224 | tf_op jit(solution)/shard_map/ppermute | solution.py:228
  8.9 2.6 %collective-permute-start.3 = (bf16[1,1,32,1024]{3,2,1,0:T(8,128)(2,1)}, bf16[1,1,32,1024]{3,2,1,0:T(8,128)(2,1)S(1)}, u32[]{:S(2)}, u32[]{:S(2)}) collective-permute-start(bf16[1,1,32,1024]{3,2,1,0:T(8,128)(2,1)} %get-tuple-element.35._.refs_1_.refs_0_), channel_id=1, source_target_pairs={{0,8},{2,10},{4,12},{6,14},{8,0},{10,2},{12,4},{14,6},{1,9},{3,11}... | collective-permute-start | bytes 196616 | tf_op jit(solution)/shard_map/ppermute | solution.py:228
  11.5 2.0 %spread.1 = bf16[2,2048,128]{2,1,0:T(8,128)(2,1)} custom-call(bf16[4096,128]{1,0:T(8,128)(2,1)} %weight.1, bf16[1,1,32,1024]{3,2,1,0:T(8,128)(2,1)} %get-tuple-element.35._.refs_1_.refs_0_), custom_call_target="tpu_custom_call" | custom-call | tf_op jit(solution)/shard_map/spread/pallas_call | solution.py:234
  13.5 0.7 collective-permute-start.2
  14.2 0.8 %collective-permute-done.3.refs_2_.refs_1_ = bf16[1,1,32,1024]{3,2,1,0:T(8,128)(2,1)S(1)} collective-permute-done((bf16[1,1,32,1024]{3,2,1,0:T(8,128)(2,1)}, bf16[1,1,32,1024]{3,2,1,0:T(8,128)(2,1)S(1)}, u32[]{:S(2)}, u32[]{:S(2)}) %collective-permute-start.3) | collective-permute-done | bytes 65568 | tf_op jit(solution)/shard_map/ppermute | solution.py:228
  15.0 0.6 both.1
  15.5 0.5 collective-permute-start.4
  16.0 4.4 %all-to-all-start = ((bf16[8,512,128]{2,1,0:T(8,128)(2,1)}), bf16[8,512,128]{2,1,0:T(8,128)(2,1)S(1)}, u32[]{:S(2)}, u32[]{:S(2)}) async-start(bf16[8,512,128]{2,1,0:T(8,128)(2,1)} %bitcast.6), calls=%async_computation | async-start | bytes 2097152 | tf_op jit(solution)/shard_map/all_to_all | solution.py:350
  20.4 0.4 collective-permute-done.2
  20.8 2.3 %collective-permute-done.4.refs_1_.refs_2_ = bf16[4,1,32,1024]{3,2,1,0:T(8,128)(2,1)S(1)} collective-permute-done((bf16[4,1,32,1024]{3,2,1,0:T(8,128)(2,1)S(1)}, bf16[4,1,32,1024]{3,2,1,0:T(8,128)(2,1)S(1)}, u32[]{:S(2)}, u32[]{:S(2)}) %collective-permute-start.4) | collective-permute-done | bytes 262176 | tf_op jit(solution)/shard_map/ppermute | solution.py:228
  23.1 1.6 %collective-permute-start.5 = (bf16[4,128,512]{2,1,0:T(8,128)(2,1)S(1)}, bf16[4,128,512]{2,1,0:T(8,128)(2,1)S(1)}, u32[]{:S(2)}, u32[]{:S(2)}) collective-permute-start(bf16[4,128,512]{2,1,0:T(8,128)(2,1)S(1)} %pad_maximum_fusion), channel_id=1, source_target_pairs={{0,16},{16,0},{1,17},{17,1},{2,18},{18,2},{3,19},{19,3},{4,20},{20... | collective-permute-start | bytes 1572872 | tf_op jit(solution)/shard_map/ppermute | solution.py:228
  24.7 2.0 %collective-permute-start.6 = (bf16[2,1,32,1024]{3,2,1,0:T(8,128)(2,1)S(1)}, bf16[2,1,32,1024]{3,2,1,0:T(8,128)(2,1)S(1)}, u32[]{:S(2)}, u32[]{:S(2)}) collective-permute-start(bf16[2,1,32,1024]{3,2,1,0:T(8,128)(2,1)S(1)} %copy-done.8), channel_id=1, source_target_pairs={{0,2},{2,0},{4,6},{6,4},{8,10},{10,8},{12,14},{14,12},{1,3},{3,1},... | collective-permute-start | bytes 393224 | tf_op jit(solution)/shard_map/ppermute | solution.py:228
  26.7 6.8 %collective-permute-done.6.refs_0_ = bf16[2,1,32,1024]{3,2,1,0:T(8,128)(2,1)S(1)} collective-permute-done((bf16[2,1,32,1024]{3,2,1,0:T(8,128)(2,1)S(1)}, bf16[2,1,32,1024]{3,2,1,0:T(8,128)(2,1)S(1)}, u32[]{:S(2)}, u32[]{:S(2)}) %collective-permute-start.6) | collective-permute-done | bytes 131104 | tf_op jit(solution)/shard_map/ppermute | solution.py:228
  33.5 0.1 collective-permute-start.7
  33.6 0.7 %pad_maximum_fusion.1 = bf16[4,1,32,1024]{3,2,1,0:T(8,128)(2,1)} fusion(bf16[2,1,32,1024]{3,2,1,0:T(8,128)(2,1)S(1)} %slice.3, bf16[1,1,32,1024]{3,2,1,0:T(8,128)(2,1)S(1)} %collective-permute-done.3.refs_2_.refs_1_, bf16[1,1,32,1024]{3,2,1,0:T(8,128)(2,1)S(1)} %copy-done.2), kind=kLoop, calls=%fused_computation.1 | loop fusion | flops 262144 | bytes 524288 | tf_op jit(solution)/shard_map/concatenate | solution.py:306
  34.4 1.4 %collective-permute-start.9 = (bf16[4,1,32,1024]{3,2,1,0:T(8,128)(2,1)}, bf16[4,1,32,1024]{3,2,1,0:T(8,128)(2,1)S(1)}, u32[]{:S(2)}, u32[]{:S(2)}) collective-permute-start(bf16[4,1,32,1024]{3,2,1,0:T(8,128)(2,1)} %pad_maximum_fusion.1), channel_id=1, source_target_pairs={{0,2},{2,0},{4,6},{6,4},{8,10},{10,8},{12,14},{14,12},{1,3},{3,1},... | collective-permute-start | bytes 786440 | tf_op jit(solution)/shard_map/ppermute | solution.py:228
  35.8 0.6 pick.1
  36.4 2.4 %collective-permute-start.8 = (bf16[1,1,32,1024]{3,2,1,0:T(8,128)(2,1)S(1)}, bf16[1,1,32,1024]{3,2,1,0:T(8,128)(2,1)S(1)}, u32[]{:S(2)}, u32[]{:S(2)}) collective-permute-start(bf16[1,1,32,1024]{3,2,1,0:T(8,128)(2,1)S(1)} %pick.1), channel_id=1, source_target_pairs={{0,8},{2,10},{4,12},{6,14},{8,0},{10,2},{12,4},{14,6},{1,9},{3,11}... | collective-permute-start | bytes 196616 | tf_op jit(solution)/shard_map/ppermute | solution.py:228
  38.8 7.6 %all-to-all-done.slices = bf16[8,512,128]{2,1,0:T(8,128)(2,1)S(1)} async-done(((bf16[8,512,128]{2,1,0:T(8,128)(2,1)}), bf16[8,512,128]{2,1,0:T(8,128)(2,1)S(1)}, u32[]{:S(2)}, u32[]{:S(2)}) %all-to-all-start) | async-done | bytes 1048608 | tf_op jit(solution)/shard_map/all_to_all | solution.py:350
  46.4 3.4 %frozen.1 = bf16[8,128,512]{2,1,0:T(8,128)(2,1)} custom-call(bf16[8,128,512]{2,1,0:T(8,128)(2,1)S(1)} %constant_dynamic-update-slice_fusion.2.mine, bf16[8,128,512]{2,1,0:T(8,128)(2,1)} %collective-permute-done.7.other, bf16[8,512,128]{2,1,0:T(8,128)(2,1)S(1)} %all-to-all-done.slices), custom_call_target="tpu_custom_call" | custom-call | tf_op jit(solution)/shard_map/frozen/pallas_call | solution.py:234
  49.8 0.6 copy-done.4
  50.4 3.6 %all-to-all-start.1 = ((bf16[8,128,512]{2,1,0:T(8,128)(2,1)}), bf16[8,128,512]{2,1,0:T(8,128)(2,1)S(1)}, u32[]{:S(2)}, u32[]{:S(2)}) async-start(bf16[8,128,512]{2,1,0:T(8,128)(2,1)} %frozen.1), calls=%async_computation.1 | async-start | bytes 2097152 | tf_op jit(solution)/shard_map/all_to_all | solution.py:369
  54.1 0.8 %gradient.1 = bf16[2,32,1024]{2,1,0:T(8,128)(2,1)S(1)} custom-call(s32[8]{0:T(128)S(1)} %copy-done.6, bf16[1,1,32,1024]{3,2,1,0:T(8,128)(2,1)S(1)} %copy-done.2, bf16[1,1,32,1024]{3,2,1,0:T(8,128)(2,1)S(1)} %collective-permute-done.3.refs_2_.refs_1_, bf16[4,1,32,1024]{3,2,1,0:T(8,128)(2,1)S(1)} %collective-permute-done.4.refs_1_.refs_2_, ...), custom_call_target="tpu_custom_call" | custom-call | tf_op jit(solution)/shard_map/gradient/pallas_call | solution.py:234
  54.8 0.1 collective-permute-start.11
  54.9 0.8 %copy-done.5 = bf16[1,1,32,1024]{3,2,1,0:T(8,128)(2,1)S(1)} copy-done((bf16[1,1,32,1024]{3,2,1,0:T(8,128)(2,1)S(1)}, bf16[1,1,32,1024]{3,2,1,0:T(8,128)(2,1)}, u32[]{:S(2)}) %copy-start.5) | copy-done | bytes 65560
  55.8 0.7 %back.1.mine = bf16[32,128]{1,0:T(8,128)(2,1)S(1)} custom-call(s32[8]{0:T(128)S(1)} %copy-done.6, bf16[2,64,1024]{2,1,0:T(8,128)(2,1)S(1)} %copy-done.1, bf16[128,1024]{1,0:T(8,128)(2,1)S(1)} %copy-done.3, bf16[2,1,32,1024]{3,2,1,0:T(8,128)(2,1)S(1)} %collective-permute-done.6.refs_0_, bf16[4,1,32,1024]{3,2,1,0:T(8,128)(2,1)S(1)} %collective-permute-done.4.refs_1_.refs_2_, ...), custom_call_target="tpu_custom_call" | custom-call | tf_op jit(solution)/shard_map/back/pallas_call | solution.py:234
  56.5 0.5 collective-permute-start.10
  57.0 0.8 %collective-permute-done.10.other = bf16[32,128]{1,0:T(8,128)(2,1)S(1)} collective-permute-done((bf16[32,128]{1,0:T(8,128)(2,1)S(1)}, bf16[32,128]{1,0:T(8,128)(2,1)S(1)}, u32[]{:S(2)}, u32[]{:S(2)}) %collective-permute-start.10) | collective-permute-done | bytes 8224 | tf_op jit(solution)/shard_map/ppermute | solution.py:228
  57.8 8.7 %all-to-all-done.1.frozen = bf16[8,128,512]{2,1,0:T(8,128)(2,1)S(1)} async-done(((bf16[8,128,512]{2,1,0:T(8,128)(2,1)}), bf16[8,128,512]{2,1,0:T(8,128)(2,1)S(1)}, u32[]{:S(2)}, u32[]{:S(2)}) %all-to-all-start.1) | async-done | bytes 1048608 | tf_op jit(solution)/shard_map/all_to_all | solution.py:369
  66.5 1.4 %last.1 = (bf16[128,4096]{1,0:T(8,128)(2,1)}, bf16[2,64,1024]{2,1,0:T(8,128)(2,1)}) custom-call(bf16[8,128,512]{2,1,0:T(8,128)(2,1)S(1)} %all-to-all-done.1.frozen, bf16[32,128]{1,0:T(8,128)(2,1)S(1)} %back.1.mine, bf16[32,128]{1,0:T(8,128)(2,1)S(1)} %collective-permute-done.10.other, bf16[64,8192]{1,0:T(8,128)(2,1)S(1)} %bitcast.5, ...), custom_call_target="tpu_custom_call" | custom-call | tf_op jit(solution)/shard_map/last/pallas_call | solution.py:234
  (30 shorter events, 0.2 us)
Async XLA Ops:
  4.2 9.2 %copy-start.7 = (bf16[128,512]{1,0:T(8,128)(2,1)S(1)}, bf16[128,512]{1,0:T(8,128)(2,1)}, u32[]{:S(2)}) copy-start(bf16[128,512]{1,0:T(8,128)(2,1)} %get-tuple-element.22) | copy-start | bytes 393220
  4.3 10.7 %copy-start.1 = (bf16[2,64,1024]{2,1,0:T(8,128)(2,1)S(1)}, bf16[2,64,1024]{2,1,0:T(8,128)(2,1)}, u32[]{:S(2)}) copy-start(bf16[2,64,1024]{2,1,0:T(8,128)(2,1)} %up.7) | copy-start | bytes 786436
  4.3 10.7 %copy-start.2 = (bf16[1,1,32,1024]{3,2,1,0:T(8,128)(2,1)S(1)}, bf16[1,1,32,1024]{3,2,1,0:T(8,128)(2,1)}, u32[]{:S(2)}) copy-start(bf16[1,1,32,1024]{3,2,1,0:T(8,128)(2,1)} %get-tuple-element.35._.refs_1_.refs_0_) | copy-start | bytes 196612
  4.3 10.7 %copy-start.6 = (s32[8]{0:T(128)S(1)}, s32[8]{0:T(128)}, u32[]{:S(2)}) copy-start(s32[8]{0:T(128)} %tenants.9) | copy-start | bytes 100
  4.3 9.1 %collective-permute-start = (bf16[1,128,512]{2,1,0:T(8,128)(2,1)}, bf16[1,128,512]{2,1,0:T(8,128)(2,1)S(1)}, u32[]{:S(2)}, u32[]{:S(2)}) collective-permute-start(bf16[1,128,512]{2,1,0:T(8,128)(2,1)} %bitcast.7), channel_id=1, source_target_pairs={{0,4},{2,6},{4,0},{6,2},{8,12},{10,14},{12,8},{14,10},{1,5},{3,7},... | collective-permute-start | bytes 393224 | tf_op jit(solution)/shard_map/ppermute | solution.py:228
  7.4 6.1 %collective-permute-start.1 = (bf16[2,1,32,1024]{3,2,1,0:T(8,128)(2,1)}, bf16[2,1,32,1024]{3,2,1,0:T(8,128)(2,1)S(1)}, u32[]{:S(2)}, u32[]{:S(2)}) collective-permute-start(bf16[2,1,32,1024]{3,2,1,0:T(8,128)(2,1)} %get-tuple-element.23), channel_id=1, source_target_pairs={{0,2},{2,0},{4,6},{6,4},{8,10},{10,8},{12,14},{14,12},{1,3},{3,1},... | collective-permute-start | bytes 393224 | tf_op jit(solution)/shard_map/ppermute | solution.py:228
  8.9 6.1 %collective-permute-start.3 = (bf16[1,1,32,1024]{3,2,1,0:T(8,128)(2,1)}, bf16[1,1,32,1024]{3,2,1,0:T(8,128)(2,1)S(1)}, u32[]{:S(2)}, u32[]{:S(2)}) collective-permute-start(bf16[1,1,32,1024]{3,2,1,0:T(8,128)(2,1)} %get-tuple-element.35._.refs_1_.refs_0_), channel_id=1, source_target_pairs={{0,8},{2,10},{4,12},{6,14},{8,0},{10,2},{12,4},{14,6},{1,9},{3,11}... | collective-permute-start | bytes 196616 | tf_op jit(solution)/shard_map/ppermute | solution.py:228
  13.5 11.2 %copy-start.8 = (bf16[2,1,32,1024]{3,2,1,0:T(8,128)(2,1)S(1)}, bf16[2,1,32,1024]{3,2,1,0:T(8,128)(2,1)}, u32[]{:S(2)}) copy-start(bf16[2,1,32,1024]{3,2,1,0:T(8,128)(2,1)} %get-tuple-element.30) | copy-start | bytes 393220
  13.5 7.3 %collective-permute-start.2 = (bf16[2,128,512]{2,1,0:T(8,128)(2,1)S(1)}, bf16[2,128,512]{2,1,0:T(8,128)(2,1)S(1)}, u32[]{:S(2)}, u32[]{:S(2)}) collective-permute-start(bf16[2,128,512]{2,1,0:T(8,128)(2,1)S(1)} %constant_dynamic-update-slice_fusion), channel_id=1, source_target_pairs={{0,2},{2,0},{4,6},{6,4},{8,10},{10,8},{12,14},{14,12},{1,3},{3,1},... | collective-permute-start | bytes 786440 | tf_op jit(solution)/shard_map/ppermute | solution.py:228
  15.5 7.5 %collective-permute-start.4 = (bf16[4,1,32,1024]{3,2,1,0:T(8,128)(2,1)S(1)}, bf16[4,1,32,1024]{3,2,1,0:T(8,128)(2,1)S(1)}, u32[]{:S(2)}, u32[]{:S(2)}) collective-permute-start(bf16[4,1,32,1024]{3,2,1,0:T(8,128)(2,1)S(1)} %both.1), channel_id=1, source_target_pairs={{0,4},{2,6},{4,0},{6,2},{8,12},{10,14},{12,8},{14,10},{1,5},{3,7},... | collective-permute-start | bytes 786440 | tf_op jit(solution)/shard_map/ppermute | solution.py:228
  16.0 30.4 %all-to-all-start = ((bf16[8,512,128]{2,1,0:T(8,128)(2,1)}), bf16[8,512,128]{2,1,0:T(8,128)(2,1)S(1)}, u32[]{:S(2)}, u32[]{:S(2)}) async-start(bf16[8,512,128]{2,1,0:T(8,128)(2,1)} %bitcast.6), calls=%async_computation | async-start | bytes 2097152 | tf_op jit(solution)/shard_map/all_to_all | solution.py:350
  23.1 10.4 %collective-permute-start.5 = (bf16[4,128,512]{2,1,0:T(8,128)(2,1)S(1)}, bf16[4,128,512]{2,1,0:T(8,128)(2,1)S(1)}, u32[]{:S(2)}, u32[]{:S(2)}) collective-permute-start(bf16[4,128,512]{2,1,0:T(8,128)(2,1)S(1)} %pad_maximum_fusion), channel_id=1, source_target_pairs={{0,16},{16,0},{1,17},{17,1},{2,18},{18,2},{3,19},{19,3},{4,20},{20... | collective-permute-start | bytes 1572872 | tf_op jit(solution)/shard_map/ppermute | solution.py:228
  24.7 8.8 %collective-permute-start.6 = (bf16[2,1,32,1024]{3,2,1,0:T(8,128)(2,1)S(1)}, bf16[2,1,32,1024]{3,2,1,0:T(8,128)(2,1)S(1)}, u32[]{:S(2)}, u32[]{:S(2)}) collective-permute-start(bf16[2,1,32,1024]{3,2,1,0:T(8,128)(2,1)S(1)} %copy-done.8), channel_id=1, source_target_pairs={{0,2},{2,0},{4,6},{6,4},{8,10},{10,8},{12,14},{14,12},{1,3},{3,1},... | collective-permute-start | bytes 393224 | tf_op jit(solution)/shard_map/ppermute | solution.py:228
  33.5 12.9 %collective-permute-start.7 = (bf16[8,128,512]{2,1,0:T(8,128)(2,1)S(1)}, bf16[8,128,512]{2,1,0:T(8,128)(2,1)}, u32[]{:S(2)}, u32[]{:S(2)}) collective-permute-start(bf16[8,128,512]{2,1,0:T(8,128)(2,1)S(1)} %constant_dynamic-update-slice_fusion.2.mine), channel_id=1, source_target_pairs={{0,1},{1,0},{2,3},{3,2},{4,5},{5,4},{6,7},{7,6},{8,9},{9,8},{10,11... | collective-permute-start | bytes 3145736 | tf_op jit(solution)/shard_map/ppermute | solution.py:228
  34.4 15.5 %collective-permute-start.9 = (bf16[4,1,32,1024]{3,2,1,0:T(8,128)(2,1)}, bf16[4,1,32,1024]{3,2,1,0:T(8,128)(2,1)S(1)}, u32[]{:S(2)}, u32[]{:S(2)}) collective-permute-start(bf16[4,1,32,1024]{3,2,1,0:T(8,128)(2,1)} %pad_maximum_fusion.1), channel_id=1, source_target_pairs={{0,2},{2,0},{4,6},{6,4},{8,10},{10,8},{12,14},{14,12},{1,3},{3,1},... | collective-permute-start | bytes 786440 | tf_op jit(solution)/shard_map/ppermute | solution.py:228
  36.4 13.5 %collective-permute-start.8 = (bf16[1,1,32,1024]{3,2,1,0:T(8,128)(2,1)S(1)}, bf16[1,1,32,1024]{3,2,1,0:T(8,128)(2,1)S(1)}, u32[]{:S(2)}, u32[]{:S(2)}) collective-permute-start(bf16[1,1,32,1024]{3,2,1,0:T(8,128)(2,1)S(1)} %pick.1), channel_id=1, source_target_pairs={{0,8},{2,10},{4,12},{6,14},{8,0},{10,2},{12,4},{14,6},{1,9},{3,11}... | collective-permute-start | bytes 196616 | tf_op jit(solution)/shard_map/ppermute | solution.py:228
  49.8 5.1 %copy-start.3 = (bf16[128,1024]{1,0:T(8,128)(2,1)S(1)}, bf16[128,1024]{1,0:T(8,128)(2,1)}, u32[]{:S(2)}) copy-start(bf16[128,1024]{1,0:T(8,128)(2,1)} %get-tuple-element.41.weighted) | copy-start | bytes 786436
  49.8 16.7 %copy-start = (bf16[8192,64]{0,1:T(8,128)(2,1)S(1)}, bf16[8192,64]{0,1:T(8,128)(2,1)}, u32[]{:S(2)}) copy-start(bf16[8192,64]{0,1:T(8,128)(2,1)} %param.12) | copy-start | bytes 3145732
  49.8 0.6 copy-start.4
  50.4 16.1 %all-to-all-start.1 = ((bf16[8,128,512]{2,1,0:T(8,128)(2,1)}), bf16[8,128,512]{2,1,0:T(8,128)(2,1)S(1)}, u32[]{:S(2)}, u32[]{:S(2)}) async-start(bf16[8,128,512]{2,1,0:T(8,128)(2,1)} %frozen.1), calls=%async_computation.1 | async-start | bytes 2097152 | tf_op jit(solution)/shard_map/all_to_all | solution.py:369
  54.8 2.2 %collective-permute-start.11 = (bf16[2,32,1024]{2,1,0:T(8,128)(2,1)S(1)}, bf16[2,32,1024]{2,1,0:T(8,128)(2,1)S(1)}, u32[]{:S(2)}, u32[]{:S(2)}) collective-permute-start(bf16[2,32,1024]{2,1,0:T(8,128)(2,1)S(1)} %gradient.1), channel_id=1, source_target_pairs={{0,1},{1,0},{2,3},{3,2},{4,5},{5,4},{6,7},{7,6},{8,9},{9,8},{10,11... | collective-permute-start | bytes 393224 | tf_op jit(solution)/shard_map/ppermute | solution.py:228
  54.9 0.8 %copy-start.5 = (bf16[1,1,32,1024]{3,2,1,0:T(8,128)(2,1)S(1)}, bf16[1,1,32,1024]{3,2,1,0:T(8,128)(2,1)}, u32[]{:S(2)}) copy-start(bf16[1,1,32,1024]{3,2,1,0:T(8,128)(2,1)} %copy-done.4) | copy-start | bytes 196612
  56.5 1.4 %collective-permute-start.10 = (bf16[32,128]{1,0:T(8,128)(2,1)S(1)}, bf16[32,128]{1,0:T(8,128)(2,1)S(1)}, u32[]{:S(2)}, u32[]{:S(2)}) collective-permute-start(bf16[32,128]{1,0:T(8,128)(2,1)S(1)} %back.1.mine), channel_id=1, source_target_pairs={{0,1},{1,0},{2,3},{3,2},{4,5},{5,4},{6,7},{7,6},{8,9},{9,8},{10,11... | collective-permute-start | bytes 24584 | tf_op jit(solution)/shard_map/ppermute | solution.py:228

commit v8 on v7

--- a/solution.py
+++ b/solution.py
@@ -44,7 +44,7 @@
             ]
         )
     ]
-    for load in loads:
+    for load in loads[:2] + loads[5:] + loads[2:5]:
         load.start()
     rows, part = my_cols.shape
     diagonal = lax.broadcasted_iota(jnp.int32, (rows, rows), 0) == lax.broadcasted_iota(jnp.int32, (rows, rows), 1)
@@ -341,9 +341,9 @@
         if step == 0:
             team_rows, new_rows, got[:1], to_send = tie((team_rows, new_rows, got[:1], to_send))
         elif step < len(row_steps) - 1:
-            team_rows, new_rows, got[::2], pieces = tie((team_rows, new_rows, got[::2], pieces))
+            team_rows, new_rows, *_ = tie((team_rows, new_rows, got[::2], pieces))
         else:
-            new_rows, got[1] = tie((new_rows, got[1]))
+            new_rows, _ = tie((new_rows, got[1]))
         team_rows = jnp.concatenate([team_rows, new_rows])
         distances = distances + [k | distance for k in distances]
     other_rows = swap(team_rows, "mp", 1)

time: 68.2 us -> 68.1 us (level)
  no operation moved by 1% of the time
where the time goes in v8:
time: 68.1 us; the launch traced here: 67.8 us
  waiting for transfers between devices  27.4 us (40%)
  starting transfers between devices  24.3 us (36%)
  Pallas kernels  12.8 us (19%)
  local copies, waits for them, and re-layouts  1.57 us (2%)
  between operations  0.87 us (1%)
  other arithmetic  0.77 us (1%)
    ppermute x12, starting transfers between devices, swap(): return lax.ppermute(value, axis, [(k, k ^ bit) for k in range(size)])  16.4 us
    pallas_call x8, Pallas kernels, call(): pl.pallas_call(kernel, in_specs=in_specs, out_specs=out_specs, out_shape=...  12.8 us
    ppermute x12, waiting for transfers between devices, swap(): return lax.ppermute(value, axis, [(k, k ^ bit) for k in range(size)])  11.1 us
    all_to_all x1, waiting for transfers between devices, local(): lax.all_to_all(frozen, ALL, split_axis=0, concat_axis=0, tiled=True, axis...  8.67 us
    all_to_all x1, waiting for transfers between devices, local(): lax.all_to_all(to_send.reshape(dp_count, features, cols), 'dp', split_axi...  7.61 us
    all_to_all x1, starting transfers between devices, local(): lax.all_to_all(to_send.reshape(dp_count, features, cols), 'dp', split_axi...  4.37 us
    all_to_all x1, starting transfers between devices, local(): lax.all_to_all(frozen, ALL, split_axis=0, concat_axis=0, tiled=True, axis...  3.6 us
    unnamed x21, local copies, waits for them, and re-layouts  1.52 us
  transfers between devices with their start and end apart: 14, of which 7 were waited for; matrix products, arithmetic and copies ran while one was open for 1% of the time, Pallas kernels for 12%

profile of v8, /device:TPU:0, one launch (start us, length us, event | category | flops | bytes accessed | tf_op | source)
XLA Modules:
  0.0 67.8 jit_solution(7253192760195280907)
XLA Ops:
  0.6 3.5 %prepare.1 = (bf16[128,1024]{1,0:T(8,128)(2,1)}, bf16[128,512]{1,0:T(8,128)(2,1)}, bf16[2,1,32,1024]{3,2,1,0:T(8,128)(2,1)}, bf16[2,1,32,1024]{3,2,1,0:T(8,128)(2,1)}, bf16[1,1,32,1024]{3,2,1,0:T(8,128)(2,1)}) custom-call(s32[1,128]{1,0:T(1,128)} %bitcast.9, bf16[128,1024]{1,0:T(8,128)(2,1)} %upstream.1, s32[8]{0:T(128)} %tenants.9, ...), custom_call_target="tpu_custom_call" | custom-call | tf_op jit(solution)/shard_map/prepare/pallas_call | solution.py:234
  4.2 3.1 %collective-permute-start = (bf16[1,128,512]{2,1,0:T(8,128)(2,1)}, bf16[1,128,512]{2,1,0:T(8,128)(2,1)S(1)}, u32[]{:S(2)}, u32[]{:S(2)}) collective-permute-start(bf16[1,128,512]{2,1,0:T(8,128)(2,1)} %bitcast.7), channel_id=1, source_target_pairs={{0,4},{2,6},{4,0},{6,2},{8,12},{10,14},{12,8},{14,10},{1,5},{3,7},... | collective-permute-start | bytes 393224 | tf_op jit(solution)/shard_map/ppermute | solution.py:228
  7.3 1.5 %collective-permute-start.1 = (bf16[2,1,32,1024]{3,2,1,0:T(8,128)(2,1)}, bf16[2,1,32,1024]{3,2,1,0:T(8,128)(2,1)S(1)}, u32[]{:S(2)}, u32[]{:S(2)}) collective-permute-start(bf16[2,1,32,1024]{3,2,1,0:T(8,128)(2,1)} %get-tuple-element.18), channel_id=1, source_target_pairs={{0,2},{2,0},{4,6},{6,4},{8,10},{10,8},{12,14},{14,12},{1,3},{3,1},... | collective-permute-start | bytes 393224 | tf_op jit(solution)/shard_map/ppermute | solution.py:228
  8.8 2.6 %collective-permute-start.3 = (bf16[1,1,32,1024]{3,2,1,0:T(8,128)(2,1)}, bf16[1,1,32,1024]{3,2,1,0:T(8,128)(2,1)S(1)}, u32[]{:S(2)}, u32[]{:S(2)}) collective-permute-start(bf16[1,1,32,1024]{3,2,1,0:T(8,128)(2,1)} %get-tuple-element.19._.refs_1_.refs_0_), channel_id=1, source_target_pairs={{0,8},{2,10},{4,12},{6,14},{8,0},{10,2},{12,4},{14,6},{1,9},{3,11}... | collective-permute-start | bytes 196616 | tf_op jit(solution)/shard_map/ppermute | solution.py:228
  11.4 2.0 %spread.1 = bf16[2,2048,128]{2,1,0:T(8,128)(2,1)} custom-call(bf16[4096,128]{1,0:T(8,128)(2,1)} %weight.1, bf16[1,1,32,1024]{3,2,1,0:T(8,128)(2,1)} %get-tuple-element.19._.refs_1_.refs_0_), custom_call_target="tpu_custom_call" | custom-call | tf_op jit(solution)/shard_map/spread/pallas_call | solution.py:234
  13.4 0.7 collective-permute-start.2
  14.1 0.8 %collective-permute-done.3.refs_2_.refs_1_ = bf16[1,1,32,1024]{3,2,1,0:T(8,128)(2,1)S(1)} collective-permute-done((bf16[1,1,32,1024]{3,2,1,0:T(8,128)(2,1)}, bf16[1,1,32,1024]{3,2,1,0:T(8,128)(2,1)S(1)}, u32[]{:S(2)}, u32[]{:S(2)}) %collective-permute-start.3) | collective-permute-done | bytes 65568 | tf_op jit(solution)/shard_map/ppermute | solution.py:228
  14.9 0.6 both.1
  15.4 0.5 collective-permute-start.4
  15.9 4.4 %all-to-all-start = ((bf16[8,512,128]{2,1,0:T(8,128)(2,1)}), bf16[8,512,128]{2,1,0:T(8,128)(2,1)S(1)}, u32[]{:S(2)}, u32[]{:S(2)}) async-start(bf16[8,512,128]{2,1,0:T(8,128)(2,1)} %bitcast.6), calls=%async_computation | async-start | bytes 2097152 | tf_op jit(solution)/shard_map/all_to_all | solution.py:350
  20.3 0.4 collective-permute-done.2
  20.7 2.3 %collective-permute-done.4.refs_1_.refs_2_ = bf16[4,1,32,1024]{3,2,1,0:T(8,128)(2,1)S(1)} collective-permute-done((bf16[4,1,32,1024]{3,2,1,0:T(8,128)(2,1)S(1)}, bf16[4,1,32,1024]{3,2,1,0:T(8,128)(2,1)S(1)}, u32[]{:S(2)}, u32[]{:S(2)}) %collective-permute-start.4) | collective-permute-done | bytes 262176 | tf_op jit(solution)/shard_map/ppermute | solution.py:228
  23.0 1.6 %collective-permute-start.5 = (bf16[4,128,512]{2,1,0:T(8,128)(2,1)S(1)}, bf16[4,128,512]{2,1,0:T(8,128)(2,1)S(1)}, u32[]{:S(2)}, u32[]{:S(2)}) collective-permute-start(bf16[4,128,512]{2,1,0:T(8,128)(2,1)S(1)} %pad_maximum_fusion), channel_id=1, source_target_pairs={{0,16},{16,0},{1,17},{17,1},{2,18},{18,2},{3,19},{19,3},{4,20},{20... | collective-permute-start | bytes 1572872 | tf_op jit(solution)/shard_map/ppermute | solution.py:228
  24.6 2.0 %collective-permute-start.6 = (bf16[2,1,32,1024]{3,2,1,0:T(8,128)(2,1)S(1)}, bf16[2,1,32,1024]{3,2,1,0:T(8,128)(2,1)S(1)}, u32[]{:S(2)}, u32[]{:S(2)}) collective-permute-start(bf16[2,1,32,1024]{3,2,1,0:T(8,128)(2,1)S(1)} %copy-done.8), channel_id=1, source_target_pairs={{0,2},{2,0},{4,6},{6,4},{8,10},{10,8},{12,14},{14,12},{1,3},{3,1},... | collective-permute-start | bytes 393224 | tf_op jit(solution)/shard_map/ppermute | solution.py:228
  26.6 6.8 %collective-permute-done.6.refs_0_ = bf16[2,1,32,1024]{3,2,1,0:T(8,128)(2,1)S(1)} collective-permute-done((bf16[2,1,32,1024]{3,2,1,0:T(8,128)(2,1)S(1)}, bf16[2,1,32,1024]{3,2,1,0:T(8,128)(2,1)S(1)}, u32[]{:S(2)}, u32[]{:S(2)}) %collective-permute-start.6) | collective-permute-done | bytes 131104 | tf_op jit(solution)/shard_map/ppermute | solution.py:228
  33.4 0.1 collective-permute-start.7
  33.5 0.7 %pad_maximum_fusion.1 = bf16[4,1,32,1024]{3,2,1,0:T(8,128)(2,1)} fusion(bf16[2,1,32,1024]{3,2,1,0:T(8,128)(2,1)S(1)} %slice.4, bf16[1,1,32,1024]{3,2,1,0:T(8,128)(2,1)S(1)} %collective-permute-done.3.refs_2_.refs_1_, bf16[1,1,32,1024]{3,2,1,0:T(8,128)(2,1)S(1)} %copy-done.2), kind=kLoop, calls=%fused_computation.1 | loop fusion | flops 262144 | bytes 524288 | tf_op jit(solution)/shard_map/concatenate | solution.py:306
  34.3 1.4 %collective-permute-start.9 = (bf16[4,1,32,1024]{3,2,1,0:T(8,128)(2,1)}, bf16[4,1,32,1024]{3,2,1,0:T(8,128)(2,1)S(1)}, u32[]{:S(2)}, u32[]{:S(2)}) collective-permute-start(bf16[4,1,32,1024]{3,2,1,0:T(8,128)(2,1)} %pad_maximum_fusion.1), channel_id=1, source_target_pairs={{0,2},{2,0},{4,6},{6,4},{8,10},{10,8},{12,14},{14,12},{1,3},{3,1},... | collective-permute-start | bytes 786440 | tf_op jit(solution)/shard_map/ppermute | solution.py:228
  35.7 0.6 pick.1
  36.3 2.4 %collective-permute-start.8 = (bf16[1,1,32,1024]{3,2,1,0:T(8,128)(2,1)S(1)}, bf16[1,1,32,1024]{3,2,1,0:T(8,128)(2,1)S(1)}, u32[]{:S(2)}, u32[]{:S(2)}) collective-permute-start(bf16[1,1,32,1024]{3,2,1,0:T(8,128)(2,1)S(1)} %pick.1), channel_id=1, source_target_pairs={{0,8},{2,10},{4,12},{6,14},{8,0},{10,2},{12,4},{14,6},{1,9},{3,11}... | collective-permute-start | bytes 196616 | tf_op jit(solution)/shard_map/ppermute | solution.py:228
  38.7 7.6 %all-to-all-done.slices = bf16[8,512,128]{2,1,0:T(8,128)(2,1)S(1)} async-done(((bf16[8,512,128]{2,1,0:T(8,128)(2,1)}), bf16[8,512,128]{2,1,0:T(8,128)(2,1)S(1)}, u32[]{:S(2)}, u32[]{:S(2)}) %all-to-all-start) | async-done | bytes 1048608 | tf_op jit(solution)/shard_map/all_to_all | solution.py:350
  46.3 3.4 %frozen.1 = bf16[8,128,512]{2,1,0:T(8,128)(2,1)} custom-call(bf16[8,128,512]{2,1,0:T(8,128)(2,1)S(1)} %constant_dynamic-update-slice_fusion.2.mine, bf16[8,128,512]{2,1,0:T(8,128)(2,1)} %collective-permute-done.7.other, bf16[8,512,128]{2,1,0:T(8,128)(2,1)S(1)} %all-to-all-done.slices), custom_call_target="tpu_custom_call" | custom-call | tf_op jit(solution)/shard_map/frozen/pallas_call | solution.py:234
  49.8 0.6 copy-done.4
  50.4 3.6 %all-to-all-start.1 = ((bf16[8,128,512]{2,1,0:T(8,128)(2,1)}), bf16[8,128,512]{2,1,0:T(8,128)(2,1)S(1)}, u32[]{:S(2)}, u32[]{:S(2)}) async-start(bf16[8,128,512]{2,1,0:T(8,128)(2,1)} %frozen.1), calls=%async_computation.1 | async-start | bytes 2097152 | tf_op jit(solution)/shard_map/all_to_all | solution.py:369
  54.0 0.8 %gradient.1 = bf16[2,32,1024]{2,1,0:T(8,128)(2,1)S(1)} custom-call(s32[8]{0:T(128)S(1)} %copy-done.6, bf16[1,1,32,1024]{3,2,1,0:T(8,128)(2,1)S(1)} %copy-done.2, bf16[1,1,32,1024]{3,2,1,0:T(8,128)(2,1)S(1)} %collective-permute-done.3.refs_2_.refs_1_, bf16[4,1,32,1024]{3,2,1,0:T(8,128)(2,1)S(1)} %collective-permute-done.4.refs_1_.refs_2_, ...), custom_call_target="tpu_custom_call" | custom-call | tf_op jit(solution)/shard_map/gradient/pallas_call | solution.py:234
  54.7 0.1 collective-permute-start.11
  54.8 0.8 %copy-done.5 = bf16[1,1,32,1024]{3,2,1,0:T(8,128)(2,1)S(1)} copy-done((bf16[1,1,32,1024]{3,2,1,0:T(8,128)(2,1)S(1)}, bf16[1,1,32,1024]{3,2,1,0:T(8,128)(2,1)}, u32[]{:S(2)}) %copy-start.5) | copy-done | bytes 65560
  55.7 0.7 %back.1.mine = bf16[32,128]{1,0:T(8,128)(2,1)S(1)} custom-call(s32[8]{0:T(128)S(1)} %copy-done.6, bf16[2,64,1024]{2,1,0:T(8,128)(2,1)S(1)} %copy-done.1, bf16[128,1024]{1,0:T(8,128)(2,1)S(1)} %copy-done.3, bf16[2,1,32,1024]{3,2,1,0:T(8,128)(2,1)S(1)} %collective-permute-done.6.refs_0_, bf16[4,1,32,1024]{3,2,1,0:T(8,128)(2,1)S(1)} %collective-permute-done.4.refs_1_.refs_2_, ...), custom_call_target="tpu_custom_call" | custom-call | tf_op jit(solution)/shard_map/back/pallas_call | solution.py:234
  56.4 0.5 collective-permute-start.10
  56.9 0.8 %collective-permute-done.10.other = bf16[32,128]{1,0:T(8,128)(2,1)S(1)} collective-permute-done((bf16[32,128]{1,0:T(8,128)(2,1)S(1)}, bf16[32,128]{1,0:T(8,128)(2,1)S(1)}, u32[]{:S(2)}, u32[]{:S(2)}) %collective-permute-start.10) | collective-permute-done | bytes 8224 | tf_op jit(solution)/shard_map/ppermute | solution.py:228
  57.7 8.7 %all-to-all-done.1.frozen = bf16[8,128,512]{2,1,0:T(8,128)(2,1)S(1)} async-done(((bf16[8,128,512]{2,1,0:T(8,128)(2,1)}), bf16[8,128,512]{2,1,0:T(8,128)(2,1)S(1)}, u32[]{:S(2)}, u32[]{:S(2)}) %all-to-all-start.1) | async-done | bytes 1048608 | tf_op jit(solution)/shard_map/all_to_all | solution.py:369
  66.4 1.4 %last.1 = (bf16[128,4096]{1,0:T(8,128)(2,1)}, bf16[2,64,1024]{2,1,0:T(8,128)(2,1)}) custom-call(bf16[8,128,512]{2,1,0:T(8,128)(2,1)S(1)} %all-to-all-done.1.frozen, bf16[32,128]{1,0:T(8,128)(2,1)S(1)} %back.1.mine, bf16[32,128]{1,0:T(8,128)(2,1)S(1)} %collective-permute-done.10.other, bf16[64,8192]{1,0:T(8,128)(2,1)S(1)} %bitcast.5, ...), custom_call_target="tpu_custom_call" | custom-call | tf_op jit(solution)/shard_map/last/pallas_call | solution.py:234
  (30 shorter events, 0.2 us)
Async XLA Ops:
  4.1 9.2 %copy-start.7 = (bf16[128,512]{1,0:T(8,128)(2,1)S(1)}, bf16[128,512]{1,0:T(8,128)(2,1)}, u32[]{:S(2)}) copy-start(bf16[128,512]{1,0:T(8,128)(2,1)} %get-tuple-element.17) | copy-start | bytes 393220
  4.2 10.7 %copy-start.1 = (bf16[2,64,1024]{2,1,0:T(8,128)(2,1)S(1)}, bf16[2,64,1024]{2,1,0:T(8,128)(2,1)}, u32[]{:S(2)}) copy-start(bf16[2,64,1024]{2,1,0:T(8,128)(2,1)} %up.7) | copy-start | bytes 786436
  4.2 10.7 %copy-start.2 = (bf16[1,1,32,1024]{3,2,1,0:T(8,128)(2,1)S(1)}, bf16[1,1,32,1024]{3,2,1,0:T(8,128)(2,1)}, u32[]{:S(2)}) copy-start(bf16[1,1,32,1024]{3,2,1,0:T(8,128)(2,1)} %get-tuple-element.19._.refs_1_.refs_0_) | copy-start | bytes 196612
  4.2 10.7 %copy-start.6 = (s32[8]{0:T(128)S(1)}, s32[8]{0:T(128)}, u32[]{:S(2)}) copy-start(s32[8]{0:T(128)} %tenants.9) | copy-start | bytes 100
  4.2 9.1 %collective-permute-start = (bf16[1,128,512]{2,1,0:T(8,128)(2,1)}, bf16[1,128,512]{2,1,0:T(8,128)(2,1)S(1)}, u32[]{:S(2)}, u32[]{:S(2)}) collective-permute-start(bf16[1,128,512]{2,1,0:T(8,128)(2,1)} %bitcast.7), channel_id=1, source_target_pairs={{0,4},{2,6},{4,0},{6,2},{8,12},{10,14},{12,8},{14,10},{1,5},{3,7},... | collective-permute-start | bytes 393224 | tf_op jit(solution)/shard_map/ppermute | solution.py:228
  7.3 6.1 %collective-permute-start.1 = (bf16[2,1,32,1024]{3,2,1,0:T(8,128)(2,1)}, bf16[2,1,32,1024]{3,2,1,0:T(8,128)(2,1)S(1)}, u32[]{:S(2)}, u32[]{:S(2)}) collective-permute-start(bf16[2,1,32,1024]{3,2,1,0:T(8,128)(2,1)} %get-tuple-element.18), channel_id=1, source_target_pairs={{0,2},{2,0},{4,6},{6,4},{8,10},{10,8},{12,14},{14,12},{1,3},{3,1},... | collective-permute-start | bytes 393224 | tf_op jit(solution)/shard_map/ppermute | solution.py:228
  8.8 6.1 %collective-permute-start.3 = (bf16[1,1,32,1024]{3,2,1,0:T(8,128)(2,1)}, bf16[1,1,32,1024]{3,2,1,0:T(8,128)(2,1)S(1)}, u32[]{:S(2)}, u32[]{:S(2)}) collective-permute-start(bf16[1,1,32,1024]{3,2,1,0:T(8,128)(2,1)} %get-tuple-element.19._.refs_1_.refs_0_), channel_id=1, source_target_pairs={{0,8},{2,10},{4,12},{6,14},{8,0},{10,2},{12,4},{14,6},{1,9},{3,11}... | collective-permute-start | bytes 196616 | tf_op jit(solution)/shard_map/ppermute | solution.py:228
  13.4 11.2 %copy-start.8 = (bf16[2,1,32,1024]{3,2,1,0:T(8,128)(2,1)S(1)}, bf16[2,1,32,1024]{3,2,1,0:T(8,128)(2,1)}, u32[]{:S(2)}) copy-start(bf16[2,1,32,1024]{3,2,1,0:T(8,128)(2,1)} %get-tuple-element.25) | copy-start | bytes 393220
  13.4 7.3 %collective-permute-start.2 = (bf16[2,128,512]{2,1,0:T(8,128)(2,1)S(1)}, bf16[2,128,512]{2,1,0:T(8,128)(2,1)S(1)}, u32[]{:S(2)}, u32[]{:S(2)}) collective-permute-start(bf16[2,128,512]{2,1,0:T(8,128)(2,1)S(1)} %constant_dynamic-update-slice_fusion), channel_id=1, source_target_pairs={{0,2},{2,0},{4,6},{6,4},{8,10},{10,8},{12,14},{14,12},{1,3},{3,1},... | collective-permute-start | bytes 786440 | tf_op jit(solution)/shard_map/ppermute | solution.py:228
  15.4 7.5 %collective-permute-start.4 = (bf16[4,1,32,1024]{3,2,1,0:T(8,128)(2,1)S(1)}, bf16[4,1,32,1024]{3,2,1,0:T(8,128)(2,1)S(1)}, u32[]{:S(2)}, u32[]{:S(2)}) collective-permute-start(bf16[4,1,32,1024]{3,2,1,0:T(8,128)(2,1)S(1)} %both.1), channel_id=1, source_target_pairs={{0,4},{2,6},{4,0},{6,2},{8,12},{10,14},{12,8},{14,10},{1,5},{3,7},... | collective-permute-start | bytes 786440 | tf_op jit(solution)/shard_map/ppermute | solution.py:228
  15.9 30.4 %all-to-all-start = ((bf16[8,512,128]{2,1,0:T(8,128)(2,1)}), bf16[8,512,128]{2,1,0:T(8,128)(2,1)S(1)}, u32[]{:S(2)}, u32[]{:S(2)}) async-start(bf16[8,512,128]{2,1,0:T(8,128)(2,1)} %bitcast.6), calls=%async_computation | async-start | bytes 2097152 | tf_op jit(solution)/shard_map/all_to_all | solution.py:350
  23.0 10.4 %collective-permute-start.5 = (bf16[4,128,512]{2,1,0:T(8,128)(2,1)S(1)}, bf16[4,128,512]{2,1,0:T(8,128)(2,1)S(1)}, u32[]{:S(2)}, u32[]{:S(2)}) collective-permute-start(bf16[4,128,512]{2,1,0:T(8,128)(2,1)S(1)} %pad_maximum_fusion), channel_id=1, source_target_pairs={{0,16},{16,0},{1,17},{17,1},{2,18},{18,2},{3,19},{19,3},{4,20},{20... | collective-permute-start | bytes 1572872 | tf_op jit(solution)/shard_map/ppermute | solution.py:228
  24.6 8.8 %collective-permute-start.6 = (bf16[2,1,32,1024]{3,2,1,0:T(8,128)(2,1)S(1)}, bf16[2,1,32,1024]{3,2,1,0:T(8,128)(2,1)S(1)}, u32[]{:S(2)}, u32[]{:S(2)}) collective-permute-start(bf16[2,1,32,1024]{3,2,1,0:T(8,128)(2,1)S(1)} %copy-done.8), channel_id=1, source_target_pairs={{0,2},{2,0},{4,6},{6,4},{8,10},{10,8},{12,14},{14,12},{1,3},{3,1},... | collective-permute-start | bytes 393224 | tf_op jit(solution)/shard_map/ppermute | solution.py:228
  33.4 12.9 %collective-permute-start.7 = (bf16[8,128,512]{2,1,0:T(8,128)(2,1)S(1)}, bf16[8,128,512]{2,1,0:T(8,128)(2,1)}, u32[]{:S(2)}, u32[]{:S(2)}) collective-permute-start(bf16[8,128,512]{2,1,0:T(8,128)(2,1)S(1)} %constant_dynamic-update-slice_fusion.2.mine), channel_id=1, source_target_pairs={{0,1},{1,0},{2,3},{3,2},{4,5},{5,4},{6,7},{7,6},{8,9},{9,8},{10,11... | collective-permute-start | bytes 3145736 | tf_op jit(solution)/shard_map/ppermute | solution.py:228
  34.3 15.5 %collective-permute-start.9 = (bf16[4,1,32,1024]{3,2,1,0:T(8,128)(2,1)}, bf16[4,1,32,1024]{3,2,1,0:T(8,128)(2,1)S(1)}, u32[]{:S(2)}, u32[]{:S(2)}) collective-permute-start(bf16[4,1,32,1024]{3,2,1,0:T(8,128)(2,1)} %pad_maximum_fusion.1), channel_id=1, source_target_pairs={{0,2},{2,0},{4,6},{6,4},{8,10},{10,8},{12,14},{14,12},{1,3},{3,1},... | collective-permute-start | bytes 786440 | tf_op jit(solution)/shard_map/ppermute | solution.py:228
  36.3 13.5 %collective-permute-start.8 = (bf16[1,1,32,1024]{3,2,1,0:T(8,128)(2,1)S(1)}, bf16[1,1,32,1024]{3,2,1,0:T(8,128)(2,1)S(1)}, u32[]{:S(2)}, u32[]{:S(2)}) collective-permute-start(bf16[1,1,32,1024]{3,2,1,0:T(8,128)(2,1)S(1)} %pick.1), channel_id=1, source_target_pairs={{0,8},{2,10},{4,12},{6,14},{8,0},{10,2},{12,4},{14,6},{1,9},{3,11}... | collective-permute-start | bytes 196616 | tf_op jit(solution)/shard_map/ppermute | solution.py:228
  49.7 5.1 %copy-start.3 = (bf16[128,1024]{1,0:T(8,128)(2,1)S(1)}, bf16[128,1024]{1,0:T(8,128)(2,1)}, u32[]{:S(2)}) copy-start(bf16[128,1024]{1,0:T(8,128)(2,1)} %get-tuple-element.31.weighted) | copy-start | bytes 786436
  49.7 16.7 %copy-start = (bf16[8192,64]{0,1:T(8,128)(2,1)S(1)}, bf16[8192,64]{0,1:T(8,128)(2,1)}, u32[]{:S(2)}) copy-start(bf16[8192,64]{0,1:T(8,128)(2,1)} %param.12) | copy-start | bytes 3145732
  49.7 0.6 copy-start.4
  50.4 16.0 %all-to-all-start.1 = ((bf16[8,128,512]{2,1,0:T(8,128)(2,1)}), bf16[8,128,512]{2,1,0:T(8,128)(2,1)S(1)}, u32[]{:S(2)}, u32[]{:S(2)}) async-start(bf16[8,128,512]{2,1,0:T(8,128)(2,1)} %frozen.1), calls=%async_computation.1 | async-start | bytes 2097152 | tf_op jit(solution)/shard_map/all_to_all | solution.py:369
  54.7 3.0 %collective-permute-start.11 = (bf16[2,32,1024]{2,1,0:T(8,128)(2,1)S(1)}, bf16[2,32,1024]{2,1,0:T(8,128)(2,1)S(1)}, u32[]{:S(2)}, u32[]{:S(2)}) collective-permute-start(bf16[2,32,1024]{2,1,0:T(8,128)(2,1)S(1)} %gradient.1), channel_id=1, source_target_pairs={{0,1},{1,0},{2,3},{3,2},{4,5},{5,4},{6,7},{7,6},{8,9},{9,8},{10,11... | collective-permute-start | bytes 393224 | tf_op jit(solution)/shard_map/ppermute | solution.py:228
  54.8 0.8 %copy-start.5 = (bf16[1,1,32,1024]{3,2,1,0:T(8,128)(2,1)S(1)}, bf16[1,1,32,1024]{3,2,1,0:T(8,128)(2,1)}, u32[]{:S(2)}) copy-start(bf16[1,1,32,1024]{3,2,1,0:T(8,128)(2,1)} %copy-done.4) | copy-start | bytes 196612
  56.4 1.4 %collective-permute-start.10 = (bf16[32,128]{1,0:T(8,128)(2,1)S(1)}, bf16[32,128]{1,0:T(8,128)(2,1)S(1)}, u32[]{:S(2)}, u32[]{:S(2)}) collective-permute-start(bf16[32,128]{1,0:T(8,128)(2,1)S(1)} %back.1.mine), channel_id=1, source_target_pairs={{0,1},{1,0},{2,3},{3,2},{4,5},{5,4},{6,7},{7,6},{8,9},{9,8},{10,11... | collective-permute-start | bytes 24584 | tf_op jit(solution)/shard_map/ppermute | solution.py:228

commit v9 on v8

--- a/solution.py
+++ b/solution.py
@@ -161,11 +161,11 @@
             held[half, :, j * width : (j + 1) * width] = slices[at + j]
     dims = (((1,), (1,)), ((), ()))
     stores = []
-    for c in range(0, team, 2):
-        total = lax.dot_general(mine[c : c + 2].reshape(2 * rows, part), held[0], dims, preferred_element_type=f32)
-        total += lax.dot_general(other[c : c + 2].reshape(2 * rows, part), held[1], dims, preferred_element_type=f32)
-        ready[c : c + 2] = total.astype(bf16).reshape(2, rows, features)
-        for k in range(c, c + 2):
+    for c in range(0, team, 4):
+        total = lax.dot_general(mine[c : c + 4].reshape(4 * rows, part), held[0], dims, preferred_element_type=f32)
+        total += lax.dot_general(other[c : c + 4].reshape(4 * rows, part), held[1], dims, preferred_element_type=f32)
+        ready[c : c + 4] = total.astype(bf16).reshape(4, rows, features)
+        for k in range(c, c + 4):
             stores.append(pltpu.make_async_copy(ready.at[k], out.at[own ^ distances[k]], sem.at[k]))
             stores[-1].start()
     for store in stores:

time: 68.1 us -> 68.2 us (level)
  no operation moved by 1% of the time
where the time goes in v9:
time: 68.2 us; the launch traced here: 67.8 us
  waiting for transfers between devices  27.4 us (40%)
  starting transfers between devices  24.3 us (36%)
  Pallas kernels  12.9 us (19%)
  local copies, waits for them, and re-layouts  1.57 us (2%)
  between operations  0.87 us (1%)
  other arithmetic  0.77 us (1%)
    ppermute x12, starting transfers between devices, swap(): return lax.ppermute(value, axis, [(k, k ^ bit) for k in range(size)])  16.4 us
    pallas_call x8, Pallas kernels, call(): pl.pallas_call(kernel, in_specs=in_specs, out_specs=out_specs, out_shape=...  12.9 us
    ppermute x12, waiting for transfers between devices, swap(): return lax.ppermute(value, axis, [(k, k ^ bit) for k in range(size)])  11.1 us
    all_to_all x1, waiting for transfers between devices, local(): lax.all_to_all(frozen, ALL, split_axis=0, concat_axis=0, tiled=True, axis...  8.67 us
    all_to_all x1, waiting for transfers between devices, local(): lax.all_to_all(to_send.reshape(dp_count, features, cols), 'dp', split_axi...  7.61 us
    all_to_all x1, starting transfers between devices, local(): lax.all_to_all(to_send.reshape(dp_count, features, cols), 'dp', split_axi...  4.37 us
    all_to_all x1, starting transfers between devices, local(): lax.all_to_all(frozen, ALL, split_axis=0, concat_axis=0, tiled=True, axis...  3.6 us
    unnamed x21, local copies, waits for them, and re-layouts  1.52 us
  transfers between devices with their start and end apart: 14, of which 7 were waited for; matrix products, arithmetic and copies ran while one was open for 1% of the time, Pallas kernels for 12%

profile of v9, /device:TPU:0, one launch (start us, length us, event | category | flops | bytes accessed | tf_op | source)
XLA Modules:
  0.0 67.8 jit_solution(2837341572255241028)
XLA Ops:
  0.6 3.5 %prepare.1 = (bf16[128,1024]{1,0:T(8,128)(2,1)}, bf16[128,512]{1,0:T(8,128)(2,1)}, bf16[2,1,32,1024]{3,2,1,0:T(8,128)(2,1)}, bf16[2,1,32,1024]{3,2,1,0:T(8,128)(2,1)}, bf16[1,1,32,1024]{3,2,1,0:T(8,128)(2,1)}) custom-call(s32[1,128]{1,0:T(1,128)} %bitcast.9, bf16[128,1024]{1,0:T(8,128)(2,1)} %upstream.1, s32[8]{0:T(128)} %tenants.9, ...), custom_call_target="tpu_custom_call" | custom-call | tf_op jit(solution)/shard_map/prepare/pallas_call | solution.py:234
  4.2 3.1 %collective-permute-start = (bf16[1,128,512]{2,1,0:T(8,128)(2,1)}, bf16[1,128,512]{2,1,0:T(8,128)(2,1)S(1)}, u32[]{:S(2)}, u32[]{:S(2)}) collective-permute-start(bf16[1,128,512]{2,1,0:T(8,128)(2,1)} %bitcast.7), channel_id=1, source_target_pairs={{0,4},{2,6},{4,0},{6,2},{8,12},{10,14},{12,8},{14,10},{1,5},{3,7},... | collective-permute-start | bytes 393224 | tf_op jit(solution)/shard_map/ppermute | solution.py:228
  7.3 1.5 %collective-permute-start.1 = (bf16[2,1,32,1024]{3,2,1,0:T(8,128)(2,1)}, bf16[2,1,32,1024]{3,2,1,0:T(8,128)(2,1)S(1)}, u32[]{:S(2)}, u32[]{:S(2)}) collective-permute-start(bf16[2,1,32,1024]{3,2,1,0:T(8,128)(2,1)} %get-tuple-element.18), channel_id=1, source_target_pairs={{0,2},{2,0},{4,6},{6,4},{8,10},{10,8},{12,14},{14,12},{1,3},{3,1},... | collective-permute-start | bytes 393224 | tf_op jit(solution)/shard_map/ppermute | solution.py:228
  8.8 2.6 %collective-permute-start.3 = (bf16[1,1,32,1024]{3,2,1,0:T(8,128)(2,1)}, bf16[1,1,32,1024]{3,2,1,0:T(8,128)(2,1)S(1)}, u32[]{:S(2)}, u32[]{:S(2)}) collective-permute-start(bf16[1,1,32,1024]{3,2,1,0:T(8,128)(2,1)} %get-tuple-element.19._.refs_1_.refs_0_), channel_id=1, source_target_pairs={{0,8},{2,10},{4,12},{6,14},{8,0},{10,2},{12,4},{14,6},{1,9},{3,11}... | collective-permute-start | bytes 196616 | tf_op jit(solution)/shard_map/ppermute | solution.py:228
  11.4 2.0 %spread.1 = bf16[2,2048,128]{2,1,0:T(8,128)(2,1)} custom-call(bf16[4096,128]{1,0:T(8,128)(2,1)} %weight.1, bf16[1,1,32,1024]{3,2,1,0:T(8,128)(2,1)} %get-tuple-element.19._.refs_1_.refs_0_), custom_call_target="tpu_custom_call" | custom-call | tf_op jit(solution)/shard_map/spread/pallas_call | solution.py:234
  13.4 0.7 collective-permute-start.2
  14.1 0.8 %collective-permute-done.3.refs_2_.refs_1_ = bf16[1,1,32,1024]{3,2,1,0:T(8,128)(2,1)S(1)} collective-permute-done((bf16[1,1,32,1024]{3,2,1,0:T(8,128)(2,1)}, bf16[1,1,32,1024]{3,2,1,0:T(8,128)(2,1)S(1)}, u32[]{:S(2)}, u32[]{:S(2)}) %collective-permute-start.3) | collective-permute-done | bytes 65568 | tf_op jit(solution)/shard_map/ppermute | solution.py:228
  14.9 0.6 both.1
  15.4 0.5 collective-permute-start.4
  15.9 4.4 %all-to-all-start = ((bf16[8,512,128]{2,1,0:T(8,128)(2,1)}), bf16[8,512,128]{2,1,0:T(8,128)(2,1)S(1)}, u32[]{:S(2)}, u32[]{:S(2)}) async-start(bf16[8,512,128]{2,1,0:T(8,128)(2,1)} %bitcast.6), calls=%async_computation | async-start | bytes 2097152 | tf_op jit(solution)/shard_map/all_to_all | solution.py:350
  20.3 0.4 collective-permute-done.2
  20.7 2.3 %collective-permute-done.4.refs_1_.refs_2_ = bf16[4,1,32,1024]{3,2,1,0:T(8,128)(2,1)S(1)} collective-permute-done((bf16[4,1,32,1024]{3,2,1,0:T(8,128)(2,1)S(1)}, bf16[4,1,32,1024]{3,2,1,0:T(8,128)(2,1)S(1)}, u32[]{:S(2)}, u32[]{:S(2)}) %collective-permute-start.4) | collective-permute-done | bytes 262176 | tf_op jit(solution)/shard_map/ppermute | solution.py:228
  23.0 1.6 %collective-permute-start.5 = (bf16[4,128,512]{2,1,0:T(8,128)(2,1)S(1)}, bf16[4,128,512]{2,1,0:T(8,128)(2,1)S(1)}, u32[]{:S(2)}, u32[]{:S(2)}) collective-permute-start(bf16[4,128,512]{2,1,0:T(8,128)(2,1)S(1)} %pad_maximum_fusion), channel_id=1, source_target_pairs={{0,16},{16,0},{1,17},{17,1},{2,18},{18,2},{3,19},{19,3},{4,20},{20... | collective-permute-start | bytes 1572872 | tf_op jit(solution)/shard_map/ppermute | solution.py:228
  24.6 2.0 %collective-permute-start.6 = (bf16[2,1,32,1024]{3,2,1,0:T(8,128)(2,1)S(1)}, bf16[2,1,32,1024]{3,2,1,0:T(8,128)(2,1)S(1)}, u32[]{:S(2)}, u32[]{:S(2)}) collective-permute-start(bf16[2,1,32,1024]{3,2,1,0:T(8,128)(2,1)S(1)} %copy-done.8), channel_id=1, source_target_pairs={{0,2},{2,0},{4,6},{6,4},{8,10},{10,8},{12,14},{14,12},{1,3},{3,1},... | collective-permute-start | bytes 393224 | tf_op jit(solution)/shard_map/ppermute | solution.py:228
  26.6 6.8 %collective-permute-done.6.refs_0_ = bf16[2,1,32,1024]{3,2,1,0:T(8,128)(2,1)S(1)} collective-permute-done((bf16[2,1,32,1024]{3,2,1,0:T(8,128)(2,1)S(1)}, bf16[2,1,32,1024]{3,2,1,0:T(8,128)(2,1)S(1)}, u32[]{:S(2)}, u32[]{:S(2)}) %collective-permute-start.6) | collective-permute-done | bytes 131104 | tf_op jit(solution)/shard_map/ppermute | solution.py:228
  33.4 0.1 collective-permute-start.7
  33.5 0.7 %pad_maximum_fusion.1 = bf16[4,1,32,1024]{3,2,1,0:T(8,128)(2,1)} fusion(bf16[2,1,32,1024]{3,2,1,0:T(8,128)(2,1)S(1)} %slice.4, bf16[1,1,32,1024]{3,2,1,0:T(8,128)(2,1)S(1)} %collective-permute-done.3.refs_2_.refs_1_, bf16[1,1,32,1024]{3,2,1,0:T(8,128)(2,1)S(1)} %copy-done.2), kind=kLoop, calls=%fused_computation.1 | loop fusion | flops 262144 | bytes 524288 | tf_op jit(solution)/shard_map/concatenate | solution.py:306
  34.3 1.4 %collective-permute-start.9 = (bf16[4,1,32,1024]{3,2,1,0:T(8,128)(2,1)}, bf16[4,1,32,1024]{3,2,1,0:T(8,128)(2,1)S(1)}, u32[]{:S(2)}, u32[]{:S(2)}) collective-permute-start(bf16[4,1,32,1024]{3,2,1,0:T(8,128)(2,1)} %pad_maximum_fusion.1), channel_id=1, source_target_pairs={{0,2},{2,0},{4,6},{6,4},{8,10},{10,8},{12,14},{14,12},{1,3},{3,1},... | collective-permute-start | bytes 786440 | tf_op jit(solution)/shard_map/ppermute | solution.py:228
  35.7 0.6 pick.1
  36.3 2.4 %collective-permute-start.8 = (bf16[1,1,32,1024]{3,2,1,0:T(8,128)(2,1)S(1)}, bf16[1,1,32,1024]{3,2,1,0:T(8,128)(2,1)S(1)}, u32[]{:S(2)}, u32[]{:S(2)}) collective-permute-start(bf16[1,1,32,1024]{3,2,1,0:T(8,128)(2,1)S(1)} %pick.1), channel_id=1, source_target_pairs={{0,8},{2,10},{4,12},{6,14},{8,0},{10,2},{12,4},{14,6},{1,9},{3,11}... | collective-permute-start | bytes 196616 | tf_op jit(solution)/shard_map/ppermute | solution.py:228
  38.7 7.6 %all-to-all-done.slices = bf16[8,512,128]{2,1,0:T(8,128)(2,1)S(1)} async-done(((bf16[8,512,128]{2,1,0:T(8,128)(2,1)}), bf16[8,512,128]{2,1,0:T(8,128)(2,1)S(1)}, u32[]{:S(2)}, u32[]{:S(2)}) %all-to-all-start) | async-done | bytes 1048608 | tf_op jit(solution)/shard_map/all_to_all | solution.py:350
  46.3 3.4 %frozen.1 = bf16[8,128,512]{2,1,0:T(8,128)(2,1)} custom-call(bf16[8,128,512]{2,1,0:T(8,128)(2,1)S(1)} %constant_dynamic-update-slice_fusion.2.mine, bf16[8,128,512]{2,1,0:T(8,128)(2,1)} %collective-permute-done.7.other, bf16[8,512,128]{2,1,0:T(8,128)(2,1)S(1)} %all-to-all-done.slices), custom_call_target="tpu_custom_call" | custom-call | tf_op jit(solution)/shard_map/frozen/pallas_call | solution.py:234
  49.8 0.6 copy-done.4
  50.4 3.6 %all-to-all-start.1 = ((bf16[8,128,512]{2,1,0:T(8,128)(2,1)}), bf16[8,128,512]{2,1,0:T(8,128)(2,1)S(1)}, u32[]{:S(2)}, u32[]{:S(2)}) async-start(bf16[8,128,512]{2,1,0:T(8,128)(2,1)} %frozen.1), calls=%async_computation.1 | async-start | bytes 2097152 | tf_op jit(solution)/shard_map/all_to_all | solution.py:369
  54.0 0.8 %gradient.1 = bf16[2,32,1024]{2,1,0:T(8,128)(2,1)S(1)} custom-call(s32[8]{0:T(128)S(1)} %copy-done.6, bf16[1,1,32,1024]{3,2,1,0:T(8,128)(2,1)S(1)} %copy-done.2, bf16[1,1,32,1024]{3,2,1,0:T(8,128)(2,1)S(1)} %collective-permute-done.3.refs_2_.refs_1_, bf16[4,1,32,1024]{3,2,1,0:T(8,128)(2,1)S(1)} %collective-permute-done.4.refs_1_.refs_2_, ...), custom_call_target="tpu_custom_call" | custom-call | tf_op jit(solution)/shard_map/gradient/pallas_call | solution.py:234
  54.8 0.1 collective-permute-start.11
  54.9 0.8 %copy-done.5 = bf16[1,1,32,1024]{3,2,1,0:T(8,128)(2,1)S(1)} copy-done((bf16[1,1,32,1024]{3,2,1,0:T(8,128)(2,1)S(1)}, bf16[1,1,32,1024]{3,2,1,0:T(8,128)(2,1)}, u32[]{:S(2)}) %copy-start.5) | copy-done | bytes 65560
  55.7 0.7 %back.1.mine = bf16[32,128]{1,0:T(8,128)(2,1)S(1)} custom-call(s32[8]{0:T(128)S(1)} %copy-done.6, bf16[2,64,1024]{2,1,0:T(8,128)(2,1)S(1)} %copy-done.1, bf16[128,1024]{1,0:T(8,128)(2,1)S(1)} %copy-done.3, bf16[2,1,32,1024]{3,2,1,0:T(8,128)(2,1)S(1)} %collective-permute-done.6.refs_0_, bf16[4,1,32,1024]{3,2,1,0:T(8,128)(2,1)S(1)} %collective-permute-done.4.refs_1_.refs_2_, ...), custom_call_target="tpu_custom_call" | custom-call | tf_op jit(solution)/shard_map/back/pallas_call | solution.py:234
  56.4 0.5 collective-permute-start.10
  56.9 0.8 %collective-permute-done.10.other = bf16[32,128]{1,0:T(8,128)(2,1)S(1)} collective-permute-done((bf16[32,128]{1,0:T(8,128)(2,1)S(1)}, bf16[32,128]{1,0:T(8,128)(2,1)S(1)}, u32[]{:S(2)}, u32[]{:S(2)}) %collective-permute-start.10) | collective-permute-done | bytes 8224 | tf_op jit(solution)/shard_map/ppermute | solution.py:228
  57.8 8.7 %all-to-all-done.1.frozen = bf16[8,128,512]{2,1,0:T(8,128)(2,1)S(1)} async-done(((bf16[8,128,512]{2,1,0:T(8,128)(2,1)}), bf16[8,128,512]{2,1,0:T(8,128)(2,1)S(1)}, u32[]{:S(2)}, u32[]{:S(2)}) %all-to-all-start.1) | async-done | bytes 1048608 | tf_op jit(solution)/shard_map/all_to_all | solution.py:369
  66.4 1.4 %last.1 = (bf16[128,4096]{1,0:T(8,128)(2,1)}, bf16[2,64,1024]{2,1,0:T(8,128)(2,1)}) custom-call(bf16[8,128,512]{2,1,0:T(8,128)(2,1)S(1)} %all-to-all-done.1.frozen, bf16[32,128]{1,0:T(8,128)(2,1)S(1)} %back.1.mine, bf16[32,128]{1,0:T(8,128)(2,1)S(1)} %collective-permute-done.10.other, bf16[64,8192]{1,0:T(8,128)(2,1)S(1)} %bitcast.5, ...), custom_call_target="tpu_custom_call" | custom-call | tf_op jit(solution)/shard_map/last/pallas_call | solution.py:234
  (30 shorter events, 0.2 us)
Async XLA Ops:
  4.1 9.2 %copy-start.7 = (bf16[128,512]{1,0:T(8,128)(2,1)S(1)}, bf16[128,512]{1,0:T(8,128)(2,1)}, u32[]{:S(2)}) copy-start(bf16[128,512]{1,0:T(8,128)(2,1)} %get-tuple-element.17) | copy-start | bytes 393220
  4.2 10.7 %copy-start.1 = (bf16[2,64,1024]{2,1,0:T(8,128)(2,1)S(1)}, bf16[2,64,1024]{2,1,0:T(8,128)(2,1)}, u32[]{:S(2)}) copy-start(bf16[2,64,1024]{2,1,0:T(8,128)(2,1)} %up.7) | copy-start | bytes 786436
  4.2 10.7 %copy-start.2 = (bf16[1,1,32,1024]{3,2,1,0:T(8,128)(2,1)S(1)}, bf16[1,1,32,1024]{3,2,1,0:T(8,128)(2,1)}, u32[]{:S(2)}) copy-start(bf16[1,1,32,1024]{3,2,1,0:T(8,128)(2,1)} %get-tuple-element.19._.refs_1_.refs_0_) | copy-start | bytes 196612
  4.2 10.7 %copy-start.6 = (s32[8]{0:T(128)S(1)}, s32[8]{0:T(128)}, u32[]{:S(2)}) copy-start(s32[8]{0:T(128)} %tenants.9) | copy-start | bytes 100
  4.2 9.1 %collective-permute-start = (bf16[1,128,512]{2,1,0:T(8,128)(2,1)}, bf16[1,128,512]{2,1,0:T(8,128)(2,1)S(1)}, u32[]{:S(2)}, u32[]{:S(2)}) collective-permute-start(bf16[1,128,512]{2,1,0:T(8,128)(2,1)} %bitcast.7), channel_id=1, source_target_pairs={{0,4},{2,6},{4,0},{6,2},{8,12},{10,14},{12,8},{14,10},{1,5},{3,7},... | collective-permute-start | bytes 393224 | tf_op jit(solution)/shard_map/ppermute | solution.py:228
  7.3 6.1 %collective-permute-start.1 = (bf16[2,1,32,1024]{3,2,1,0:T(8,128)(2,1)}, bf16[2,1,32,1024]{3,2,1,0:T(8,128)(2,1)S(1)}, u32[]{:S(2)}, u32[]{:S(2)}) collective-permute-start(bf16[2,1,32,1024]{3,2,1,0:T(8,128)(2,1)} %get-tuple-element.18), channel_id=1, source_target_pairs={{0,2},{2,0},{4,6},{6,4},{8,10},{10,8},{12,14},{14,12},{1,3},{3,1},... | collective-permute-start | bytes 393224 | tf_op jit(solution)/shard_map/ppermute | solution.py:228
  8.8 6.1 %collective-permute-start.3 = (bf16[1,1,32,1024]{3,2,1,0:T(8,128)(2,1)}, bf16[1,1,32,1024]{3,2,1,0:T(8,128)(2,1)S(1)}, u32[]{:S(2)}, u32[]{:S(2)}) collective-permute-start(bf16[1,1,32,1024]{3,2,1,0:T(8,128)(2,1)} %get-tuple-element.19._.refs_1_.refs_0_), channel_id=1, source_target_pairs={{0,8},{2,10},{4,12},{6,14},{8,0},{10,2},{12,4},{14,6},{1,9},{3,11}... | collective-permute-start | bytes 196616 | tf_op jit(solution)/shard_map/ppermute | solution.py:228
  13.4 11.2 %copy-start.8 = (bf16[2,1,32,1024]{3,2,1,0:T(8,128)(2,1)S(1)}, bf16[2,1,32,1024]{3,2,1,0:T(8,128)(2,1)}, u32[]{:S(2)}) copy-start(bf16[2,1,32,1024]{3,2,1,0:T(8,128)(2,1)} %get-tuple-element.25) | copy-start | bytes 393220
  13.4 7.3 %collective-permute-start.2 = (bf16[2,128,512]{2,1,0:T(8,128)(2,1)S(1)}, bf16[2,128,512]{2,1,0:T(8,128)(2,1)S(1)}, u32[]{:S(2)}, u32[]{:S(2)}) collective-permute-start(bf16[2,128,512]{2,1,0:T(8,128)(2,1)S(1)} %constant_dynamic-update-slice_fusion), channel_id=1, source_target_pairs={{0,2},{2,0},{4,6},{6,4},{8,10},{10,8},{12,14},{14,12},{1,3},{3,1},... | collective-permute-start | bytes 786440 | tf_op jit(solution)/shard_map/ppermute | solution.py:228
  15.4 7.5 %collective-permute-start.4 = (bf16[4,1,32,1024]{3,2,1,0:T(8,128)(2,1)S(1)}, bf16[4,1,32,1024]{3,2,1,0:T(8,128)(2,1)S(1)}, u32[]{:S(2)}, u32[]{:S(2)}) collective-permute-start(bf16[4,1,32,1024]{3,2,1,0:T(8,128)(2,1)S(1)} %both.1), channel_id=1, source_target_pairs={{0,4},{2,6},{4,0},{6,2},{8,12},{10,14},{12,8},{14,10},{1,5},{3,7},... | collective-permute-start | bytes 786440 | tf_op jit(solution)/shard_map/ppermute | solution.py:228
  15.9 30.4 %all-to-all-start = ((bf16[8,512,128]{2,1,0:T(8,128)(2,1)}), bf16[8,512,128]{2,1,0:T(8,128)(2,1)S(1)}, u32[]{:S(2)}, u32[]{:S(2)}) async-start(bf16[8,512,128]{2,1,0:T(8,128)(2,1)} %bitcast.6), calls=%async_computation | async-start | bytes 2097152 | tf_op jit(solution)/shard_map/all_to_all | solution.py:350
  23.0 10.4 %collective-permute-start.5 = (bf16[4,128,512]{2,1,0:T(8,128)(2,1)S(1)}, bf16[4,128,512]{2,1,0:T(8,128)(2,1)S(1)}, u32[]{:S(2)}, u32[]{:S(2)}) collective-permute-start(bf16[4,128,512]{2,1,0:T(8,128)(2,1)S(1)} %pad_maximum_fusion), channel_id=1, source_target_pairs={{0,16},{16,0},{1,17},{17,1},{2,18},{18,2},{3,19},{19,3},{4,20},{20... | collective-permute-start | bytes 1572872 | tf_op jit(solution)/shard_map/ppermute | solution.py:228
  24.6 8.8 %collective-permute-start.6 = (bf16[2,1,32,1024]{3,2,1,0:T(8,128)(2,1)S(1)}, bf16[2,1,32,1024]{3,2,1,0:T(8,128)(2,1)S(1)}, u32[]{:S(2)}, u32[]{:S(2)}) collective-permute-start(bf16[2,1,32,1024]{3,2,1,0:T(8,128)(2,1)S(1)} %copy-done.8), channel_id=1, source_target_pairs={{0,2},{2,0},{4,6},{6,4},{8,10},{10,8},{12,14},{14,12},{1,3},{3,1},... | collective-permute-start | bytes 393224 | tf_op jit(solution)/shard_map/ppermute | solution.py:228
  33.4 12.9 %collective-permute-start.7 = (bf16[8,128,512]{2,1,0:T(8,128)(2,1)S(1)}, bf16[8,128,512]{2,1,0:T(8,128)(2,1)}, u32[]{:S(2)}, u32[]{:S(2)}) collective-permute-start(bf16[8,128,512]{2,1,0:T(8,128)(2,1)S(1)} %constant_dynamic-update-slice_fusion.2.mine), channel_id=1, source_target_pairs={{0,1},{1,0},{2,3},{3,2},{4,5},{5,4},{6,7},{7,6},{8,9},{9,8},{10,11... | collective-permute-start | bytes 3145736 | tf_op jit(solution)/shard_map/ppermute | solution.py:228
  34.3 15.5 %collective-permute-start.9 = (bf16[4,1,32,1024]{3,2,1,0:T(8,128)(2,1)}, bf16[4,1,32,1024]{3,2,1,0:T(8,128)(2,1)S(1)}, u32[]{:S(2)}, u32[]{:S(2)}) collective-permute-start(bf16[4,1,32,1024]{3,2,1,0:T(8,128)(2,1)} %pad_maximum_fusion.1), channel_id=1, source_target_pairs={{0,2},{2,0},{4,6},{6,4},{8,10},{10,8},{12,14},{14,12},{1,3},{3,1},... | collective-permute-start | bytes 786440 | tf_op jit(solution)/shard_map/ppermute | solution.py:228
  36.3 13.5 %collective-permute-start.8 = (bf16[1,1,32,1024]{3,2,1,0:T(8,128)(2,1)S(1)}, bf16[1,1,32,1024]{3,2,1,0:T(8,128)(2,1)S(1)}, u32[]{:S(2)}, u32[]{:S(2)}) collective-permute-start(bf16[1,1,32,1024]{3,2,1,0:T(8,128)(2,1)S(1)} %pick.1), channel_id=1, source_target_pairs={{0,8},{2,10},{4,12},{6,14},{8,0},{10,2},{12,4},{14,6},{1,9},{3,11}... | collective-permute-start | bytes 196616 | tf_op jit(solution)/shard_map/ppermute | solution.py:228
  49.7 5.1 %copy-start.3 = (bf16[128,1024]{1,0:T(8,128)(2,1)S(1)}, bf16[128,1024]{1,0:T(8,128)(2,1)}, u32[]{:S(2)}) copy-start(bf16[128,1024]{1,0:T(8,128)(2,1)} %get-tuple-element.31.weighted) | copy-start | bytes 786436
  49.8 16.7 %copy-start = (bf16[8192,64]{0,1:T(8,128)(2,1)S(1)}, bf16[8192,64]{0,1:T(8,128)(2,1)}, u32[]{:S(2)}) copy-start(bf16[8192,64]{0,1:T(8,128)(2,1)} %param.12) | copy-start | bytes 3145732
  49.8 0.6 copy-start.4
  50.4 16.0 %all-to-all-start.1 = ((bf16[8,128,512]{2,1,0:T(8,128)(2,1)}), bf16[8,128,512]{2,1,0:T(8,128)(2,1)S(1)}, u32[]{:S(2)}, u32[]{:S(2)}) async-start(bf16[8,128,512]{2,1,0:T(8,128)(2,1)} %frozen.1), calls=%async_computation.1 | async-start | bytes 2097152 | tf_op jit(solution)/shard_map/all_to_all | solution.py:369
  54.8 3.0 %collective-permute-start.11 = (bf16[2,32,1024]{2,1,0:T(8,128)(2,1)S(1)}, bf16[2,32,1024]{2,1,0:T(8,128)(2,1)S(1)}, u32[]{:S(2)}, u32[]{:S(2)}) collective-permute-start(bf16[2,32,1024]{2,1,0:T(8,128)(2,1)S(1)} %gradient.1), channel_id=1, source_target_pairs={{0,1},{1,0},{2,3},{3,2},{4,5},{5,4},{6,7},{7,6},{8,9},{9,8},{10,11... | collective-permute-start | bytes 393224 | tf_op jit(solution)/shard_map/ppermute | solution.py:228
  54.9 0.8 %copy-start.5 = (bf16[1,1,32,1024]{3,2,1,0:T(8,128)(2,1)S(1)}, bf16[1,1,32,1024]{3,2,1,0:T(8,128)(2,1)}, u32[]{:S(2)}) copy-start(bf16[1,1,32,1024]{3,2,1,0:T(8,128)(2,1)} %copy-done.4) | copy-start | bytes 196612
  56.4 1.4 %collective-permute-start.10 = (bf16[32,128]{1,0:T(8,128)(2,1)S(1)}, bf16[32,128]{1,0:T(8,128)(2,1)S(1)}, u32[]{:S(2)}, u32[]{:S(2)}) collective-permute-start(bf16[32,128]{1,0:T(8,128)(2,1)S(1)} %back.1.mine), channel_id=1, source_target_pairs={{0,1},{1,0},{2,3},{3,2},{4,5},{5,4},{6,7},{7,6},{8,9},{9,8},{10,11... | collective-permute-start | bytes 24584 | tf_op jit(solution)/shard_map/ppermute | solution.py:228
